TPU v7x, 32 devices: a whole 2x2x4 slice. The times are simulated.
32 devices in a mesh: tm: 2 (over y), space: 16 (over z, x, core).
Axes of the slice: x: 2, y: 2, z: 4, core: 2. Of those that a mesh axis runs over, the one named last changes fastest.
Arguments:
- image: float32 [2, 2, 2560, 128], P(None, 'tm', 'space'), may hold values from -6 to 6
- extrap: float32 [2, 2, 2560, 128], P(None, 'tm', 'space'), may hold values from -6 to 6
- tv_dual: float32 [2, 2, 2560, 128], P(None, 'tm', 'space'), may hold values from -1 to 1
- data_dual: float32 [2, 2, 16, 16, 160, 128], P(None, 'tm', 'space'), may hold values from -4 to 4
- kspace: float32 [2, 2, 16, 16, 160, 128], P(None, 'tm', 'space'), may hold values from -6 to 6
- coil_maps: float32 [2, 16, 2560, 128], P(None, 'space'), may hold values from -1 to 1
- sampling: int32 [2, 160, 128], P('tm'), may hold values 0 or 1
Outputs:
- image_new: float32 [2, 2, 2560, 128], P(None, 'tm', 'space')
- tv_new: float32 [2, 2, 2560, 128], P(None, 'tm', 'space')
- data_new: float32 [2, 2, 16, 16, 160, 128], P(None, 'tm', 'space')
All inputs are finite; a program needn't handle non-finite values. No bound on the sum of `sampling` on one device may be relied on, other than what follows from the above.
Results may differ from a plain program's by a relative error of at most 0.000061.
Values sent between devices are 32-bit elements; how exact they have to be, the bound alone decides.
No kernel may reach another device: no remote copies, remote signals or barrier semaphores. Data moves between devices by JAX's collectives and lax.ppermute only.
A program may use at most 64 MiB of HBM per device.

v0:
```python
import math

import jax
import jax.numpy as jnp
from jax import lax
from jax.sharding import PartitionSpec as P

dual_step = 0.4
primal_step = 0.4
clip_level = 0.5
highest = lax.Precision.HIGHEST


def passed_along(value, axis, steps):
    count = lax.axis_size(axis)
    initial, last = (max(0, -steps), min(count, count - steps))
    return lax.ppermute(value, axis, [(source, source + steps) for source in range(initial, last)])


def tables(length):
    places = lax.iota(jnp.int32, length)
    product = places[:, None] * places[None, :] % length
    angles = product.astype(jnp.float32) * (2.0 * math.pi / length)
    factor = 1.0 / math.sqrt(length)
    return (jnp.cos(angles) * factor, jnp.sin(angles) * factor)


def project(real_part, imag_part):
    magnitude = jnp.sqrt(real_part * real_part + imag_part * imag_part)
    factor = clip_level / jnp.maximum(magnitude, clip_level)
    return (real_part * factor, imag_part * factor)


def right_mult(values, table):
    return jnp.dot(values, table, precision=highest, preferred_element_type=jnp.float32)


def left_mult(table, values):
    return jnp.einsum(
        "ky,cxyz->cxkz", table, values, precision=highest, preferred_element_type=jnp.float32
    )


def on_device(image, extrap, tv_dual, data_dual, kspace, coil_maps, sampling):
    readout = kspace.shape[3]
    height = kspace.shape[4]
    depth = kspace.shape[5]
    coil_count = kspace.shape[2]
    own_rows = image.shape[2]
    cos_cols, sin_cols = tables(depth)
    cos_rows, sin_rows = tables(height)
    frame_here = lax.axis_index("tm")
    frame_total = lax.axis_size("tm")
    not_last = (frame_here < frame_total - 1).astype(jnp.float32)
    current = extrap[:, 0]
    later = passed_along(current, "tm", -1)
    moved = tv_dual[:, 0] + dual_step * not_last * (later - current)
    tv_real, tv_imag = project(moved[0], moved[1])
    tv_here = jnp.stack([tv_real, tv_imag])
    piece = lax.all_gather(current, "space", axis=1, tiled=True)
    piece_real = piece[0][None]
    piece_imag = piece[1][None]
    coil_real = coil_maps[0] * piece_real - coil_maps[1] * piece_imag
    coil_imag = coil_maps[0] * piece_imag + coil_maps[1] * piece_real
    out_real = right_mult(coil_real, cos_cols) + right_mult(coil_imag, sin_cols)
    out_imag = right_mult(coil_imag, cos_cols) - right_mult(coil_real, sin_cols)
    half_spectrum = jnp.stack([out_real, out_imag])
    half_spectrum = half_spectrum.reshape(2, coil_count, readout, height, depth)
    spec_real = left_mult(cos_rows, half_spectrum[0]) + left_mult(sin_rows, half_spectrum[1])
    spec_imag = left_mult(cos_rows, half_spectrum[1]) - left_mult(sin_rows, half_spectrum[0])
    weight = sampling[0].astype(jnp.float32)
    scaled = weight / (1.0 + dual_step)
    dual_real = scaled * (data_dual[0, 0] + dual_step * (spec_real - kspace[0, 0]))
    dual_imag = scaled * (data_dual[1, 0] + dual_step * (spec_imag - kspace[1, 0]))
    back_real = left_mult(cos_rows, dual_real) - left_mult(sin_rows, dual_imag)
    back_imag = left_mult(cos_rows, dual_imag) + left_mult(sin_rows, dual_real)
    back_real = back_real.reshape(coil_count, readout * height, depth)
    back_imag = back_imag.reshape(coil_count, readout * height, depth)
    plane_real = right_mult(back_real, cos_cols) - right_mult(back_imag, sin_cols)
    plane_imag = right_mult(back_imag, cos_cols) + right_mult(back_real, sin_cols)
    term_real = jnp.sum(coil_maps[0] * plane_real + coil_maps[1] * plane_imag, axis=0)
    term_imag = jnp.sum(coil_maps[0] * plane_imag - coil_maps[1] * plane_real, axis=0)
    coil_term = jnp.stack([term_real, term_imag])
    combined = lax.psum(coil_term, "space")
    adjoint = lax.dynamic_slice_in_dim(combined, lax.axis_index("space") * own_rows, own_rows, 1)
    earlier = passed_along(tv_here, "tm", 1)
    temporal = earlier - not_last * tv_here
    image_new = image[:, 0] - primal_step * (adjoint + temporal)
    data_new = jnp.stack([dual_real, dual_imag])[:, None]
    return (image_new[:, None], tv_here[:, None], data_new)


def solution(mesh):
    in_specs = (
        P(None, "tm", "space", None),
        P(None, "tm", "space", None),
        P(None, "tm", "space", None),
        P(None, "tm", "space", None, None, None),
        P(None, "tm", "space", None, None, None),
        P(None, "space", None, None),
        P("tm", None, None),
    )
    out_specs = (
        P(None, "tm", "space", None),
        P(None, "tm", "space", None),
        P(None, "tm", "space", None, None, None),
    )
    return jax.shard_map(
        on_device, mesh=mesh, in_specs=in_specs, out_specs=out_specs, check_vma=False
    )
```

profile of v0, /device:TPU:0, one launch (start us, length us, event | category | flops | bytes accessed | tf_op | source)
XLA Modules:
  0.0 197.6 jit_solution(1482569988004621814)
XLA Ops:
  7.2 0.7 all-gather.3.cloned.1.call-update
  7.9 0.0 all-reduce.2.cloned.1.call-start
  7.9 0.9 multiply_bitcast_fusion
  8.8 47.4 %all-gather.3.cloned.1.call-done = f32[2,1,2560,128]{3,2,1,0:T(8,128)} async-done(((f32[2,1,160,128]{3,2,1,0:T(8,128)}), f32[2,1,2560,128]{3,2,1,0:T(8,128)}) %all-gather.3.cloned.1.call-update) | async-done | bytes 2621456 | tf_op jit(solution)/shard_map/all_gather | solution.py:60
  56.3 2.8 %multiply_add_fusion = (f32[1,1,2560,128]{3,2,1,0:T(8,128)S(1)}, f32[1,1,2560,128]{3,2,1,0:T(8,128)S(1)}) fusion(f32[2,1,2560,128]{3,2,1,0:T(8,128)} %all-gather.3.cloned.1.call-done, f32[2,1,2560,128]{3,2,1,0:T(8,128)} %param.12), kind=kLoop, calls=%fused_computation.40 | loop fusion | flops 1966080 | bytes 7864320 | tf_op jit(solution)/shard_map/add | solution.py:64
  59.0 1.4 fusion.24
  60.5 1.4 fusion.20
  61.9 1.5 convolution_add_fusion.1
  63.4 1.9 fusion.36
  65.3 1.5 convolution_subtract_fusion.1
  66.9 1.9 fusion.33
  68.8 2.4 %fusion.9 = f32[1,16,160,128]{3,2,1,0:T(8,128)S(1)} fusion(f32[16,128,160]{1,2,0:T(8,128)S(1)} %fusion.36, f32[16,160,128]{2,1,0:T(8,128)S(1)} %bitcast.141, f32[2,1,1,16,160,128]{5,4,3,2,1,0:T(8,128)S(1)} %copy-done.1, f32[2,1,1,16,160,128]{5,4,3,2,1,0:T(8,128)S(1)} %copy-done.2, f32[160,128]{1,0:T(8,128)S(1)} %multiply_bitcast_fusion), kind=kOutput, calls=%fused_computation.19 | convolution fusion | flops 631040000 | bytes 6635520 | tf_op jit(solution)/shard_map/ky,cxyz->cxkz/dot_general | solution.py:39
  71.2 1.9 fusion.18
  73.2 2.3 %fusion.5 = f32[1,16,160,128]{3,2,1,0:T(8,128)S(1)} fusion(f32[16,128,160]{1,2,0:T(8,128)S(1)} %fusion.33, f32[16,160,128]{2,1,0:T(8,128)S(1)} %bitcast.139, f32[2,1,1,16,160,128]{5,4,3,2,1,0:T(8,128)S(1)} %copy-done.1, f32[2,1,1,16,160,128]{5,4,3,2,1,0:T(8,128)S(1)} %copy-done.2, f32[160,128]{1,0:T(8,128)S(1)} %multiply_bitcast_fusion), kind=kOutput, calls=%fused_computation.15 | convolution fusion | flops 631040000 | bytes 6635520 | tf_op jit(solution)/shard_map/ky,cxyz->cxkz/dot_general | solution.py:39
  75.4 1.9 fusion.14
  77.4 1.9 convolution_subtract_fusion.2
  79.3 2.0 %convolution_add_fusion.2 = f32[16,128,160]{1,2,0:T(8,128)S(1)} fusion(f32[16,128,160]{1,2,0:T(8,128)S(1)} %fusion.14, f32[1,16,160,128]{3,2,1,0:T(8,128)S(1)} %fusion.9), kind=kOutput, calls=%fused_computation.6 | convolution fusion | flops 629729280 | bytes 3932160 | tf_op jit(solution)/shard_map/ky,cxyz->cxkz/dot_general | solution.py:39
  81.3 1.4 fusion.82
  82.8 1.7 fusion.83
  84.5 1.5 convolution_add_fusion
  85.9 0.3 copy-done
  86.2 1.8 fusion.11
  88.0 1.7 pad_maximum_fusion
  89.7 0.9 copy-done.3
  90.6 1.3 collective-permute-start
  91.9 6.9 %collective-permute-done = f32[2,160,128]{2,1,0:T(8,128)S(1)} collective-permute-done((f32[2,160,128]{2,1,0:T(8,128)S(1)}, f32[2,160,128]{2,1,0:T(8,128)S(1)}, u32[]{:S(2)}, u32[]{:S(2)}) %collective-permute-start) | collective-permute-done | bytes 163872 | tf_op jit(solution)/shard_map/ppermute | solution.py:17
  98.8 0.1 fusion.43
  98.9 1.5 collective-permute-start.1
  100.4 1.7 maximum_bitcast_fusion
  102.1 1.6 collective-permute-done.1
  103.6 85.5 %all-reduce.2.cloned.1.call-done = f32[2,2560,128]{2,1,0:T(8,128)} async-done(((f32[2,2560,128]{2,1,0:T(8,128)}), f32[2,2560,128]{2,1,0:T(8,128)}) %all-reduce.2.cloned.1.call-update) | async-done | bytes 2621456 | tf_op jit(solution)/shard_map/psum | solution.py:84
  189.1 1.7 fusion.172
  (14 shorter events, 0.1 us)
Async XLA Ops:
  7.2 49.1 %all-gather.3.cloned.1.call-start = ((), (), s32[]{:S(2)}) async-start(), calls=%async_computation.1 | async-start | bytes 2785280 | tf_op jit(solution)/shard_map/all_gather | solution.py:60
  7.9 181.2 %all-reduce.2.cloned.1.call-start = ((), (), s32[]{:S(2)}) async-start(), calls=%async_computation | async-start | bytes 5242880 | tf_op jit(solution)/shard_map/psum | solution.py:84
  65.3 3.5 %copy-start.2 = (f32[2,1,1,16,160,128]{5,4,3,2,1,0:T(8,128)S(1)}, f32[2,1,1,16,160,128]{5,4,3,2,1,0:T(8,128)}, u32[]{:S(2)}) copy-start(f32[2,1,1,16,160,128]{5,4,3,2,1,0:T(8,128)} %param.10) | copy-start | bytes 7864324
  66.8 2.0 copy-start.1
  84.5 1.7 copy-start
  89.7 0.9 copy-start.3
  89.7 9.2 %copy-start.4 = (f32[2,1,160,128]{3,2,1,0:T(8,128)S(1)}, f32[2,1,160,128]{3,2,1,0:T(8,128)}, u32[]{:S(2)}) copy-start(f32[2,1,160,128]{3,2,1,0:T(8,128)} %param.9) | copy-start | bytes 491524
  90.6 8.2 %collective-permute-start = (f32[2,160,128]{2,1,0:T(8,128)S(1)}, f32[2,160,128]{2,1,0:T(8,128)S(1)}, u32[]{:S(2)}, u32[]{:S(2)}) collective-permute-start(f32[2,160,128]{2,1,0:T(8,128)S(1)} %bitcast.146), channel_id=1, source_target_pairs={{16,0},{17,1},{18,2},{19,3},{20,4},{21,5},{22,6},{23,7},{24,8},{25... | collective-permute-start | bytes 491528 | tf_op jit(solution)/shard_map/ppermute | solution.py:17
  98.9 4.7 %collective-permute-start.1 = (f32[2,160,128]{2,1,0:T(8,128)S(1)}, f32[2,160,128]{2,1,0:T(8,128)S(1)}, u32[]{:S(2)}, u32[]{:S(2)}) collective-permute-start(f32[2,160,128]{2,1,0:T(8,128)S(1)} %pad_maximum_fusion.1), channel_id=1, source_target_pairs={{0,16},{1,17},{2,18},{3,19},{4,20},{5,21},{6,22},{7,23},{8,24},{9,... | collective-permute-start | bytes 491528 | tf_op jit(solution)/shard_map/ppermute | solution.py:17
  100.4 88.7 %copy-start.5 = (f32[2,1,160,128]{3,2,1,0:T(8,128)S(1)}, f32[2,1,160,128]{3,2,1,0:T(8,128)}, u32[]{:S(2)}) copy-start(f32[2,1,160,128]{3,2,1,0:T(8,128)} %param.7) | copy-start | bytes 491524
Sparse Core Ops, SparseCore 0:
  10.3 45.9 all-gather.2
  89.8 99.2 all-reduce.1
where the time goes:
time: 198 us
  waiting for transfers between devices  142 us (72%)
  matrix products  28.5 us (14%)
  between operations  14.3 us (7%)
  other arithmetic  8.8 us (4%)
  starting transfers between devices  2.81 us (1%)
    psum x1, waiting for transfers between devices, on_device(): combined = lax.psum(coil_term, 'space')  85.5 us
    all_gather x1, waiting for transfers between devices, on_device(): piece = lax.all_gather(current, 'space', axis=1, tiled=True)  47.4 us
    dot_general x8, matrix products, left_mult(): jnp.einsum('ky,cxyz->cxkz', table, values, precision=highest, preferred_e...  16.3 us
    dot_general x8, matrix products, right_mult(): jnp.dot(values, table, precision=highest, preferred_element_type=jnp.floa...  12.2 us
    ppermute x2, waiting for transfers between devices, passed_along(): lax.ppermute(value, axis, [(source, source + steps) for source in range(i...  8.51 us
  transfers between devices with their start and end apart: 4, of which 4 were waited for; matrix products, arithmetic and copies ran while one was open for 1% of the time, Pallas kernels for 0%

commit v1 on v0

v1 whole, which is shorter than its diff:
```python
import functools
import math

import jax
import jax.numpy as jnp
import ml_dtypes
import numpy as np
from jax import lax
from jax.experimental import pallas as pl
from jax.experimental.pallas import tpu as pltpu
from jax.sharding import PartitionSpec as P

dual_step = 0.4
primal_step = 0.4
clip_level = 0.5


def split_host(table):
    high = table.astype(ml_dtypes.bfloat16)
    low = (table - high.astype(np.float64)).astype(ml_dtypes.bfloat16)
    return high, low


def column_table(length, sign):
    places = np.arange(length)
    angles = 2.0 * math.pi * (np.outer(places, places) % length) / length
    real = np.cos(angles) / math.sqrt(length)
    imag = sign * np.sin(angles) / math.sqrt(length)
    whole = np.block([[real, imag], [-imag, real]])
    high, low = split_host(whole)
    return np.concatenate([high, high, low], axis=0)


def row_tables(length, sign):
    half = length // 2
    found = []
    for odd in (0, 1):
        lines = np.arange(half)
        cells = 2 * np.arange(half) + odd
        product = np.outer(lines, cells)
        angles = 2.0 * math.pi * (product % length) / length
        real = np.cos(angles) / math.sqrt(length)
        imag = sign * np.sin(angles) / math.sqrt(length)
        if sign > 0:
            real, imag = real.T, imag.T
        whole = np.block([[real, -imag], [imag, real]])
        high, low = split_host(whole)
        found.append(np.concatenate([high, high, low], axis=1))
    return found


def split(values):
    high = values.astype(jnp.bfloat16)
    low = (values - high.astype(jnp.float32)).astype(jnp.bfloat16)
    return high, low


def columns_dft(real, imag, table):
    real_high, real_low = split(real)
    imag_high, imag_low = split(imag)
    left = jnp.concatenate([real_high, imag_high, real_low, imag_low, real_high, imag_high], axis=1)
    return jnp.dot(left, table, preferred_element_type=jnp.float32)


def rows_dft(table, values):
    high, low = split(values)
    return jnp.dot(table, jnp.concatenate([high, low, high], axis=0), preferred_element_type=jnp.float32)


def coil_kernel(offsets, chained, *refs):
    count = len(offsets)
    place, refs = refs[0], refs[1:]
    mine, theirs, refs = refs[:count], refs[count:2 * count], refs[2 * count:]
    coil, dual, kspace, mask = refs[:4]
    col_fwd, even_fwd, odd_fwd, col_bwd, even_bwd, odd_bwd = refs[4:10]
    refs = refs[10 + chained:]
    keep, give, data_new = refs[:3]
    coil_buf, dual_buf, ksp_buf, new_buf, u_buf, v_buf, weight, in_sem, out_sem = refs[3:]
    own = mine[0].shape[1]
    rows = 2 * own
    height = mask.shape[1]
    half = height // 2
    planes = rows // height
    core = place[1]
    at = [pl.multiple_of(core * own, own), pl.multiple_of((1 - core) * own, own)]

    loads = []
    for n, offset in enumerate(offsets):
        chip = jnp.bitwise_xor(place[0], offset)
        row0 = pl.multiple_of(chip * rows, rows)
        plane0 = chip * planes
        loads.append([
            pltpu.make_async_copy(coil.at[:, 0, pl.ds(row0, rows), :], coil_buf.at[n], in_sem.at[n, 0]),
            pltpu.make_async_copy(dual.at[:, 0, 0, pl.ds(plane0, planes)], dual_buf.at[n], in_sem.at[n, 1]),
            pltpu.make_async_copy(kspace.at[:, 0, 0, pl.ds(plane0, planes)], ksp_buf.at[n], in_sem.at[n, 2]),
        ])
        for load in loads[-1]:
            load.start()
    weight[...] = mask[0].astype(jnp.float32) / (1.0 + dual_step)

    stores = []
    for n, offset in enumerate(offsets):
        loads[n][0].wait()
        parts = []
        for block, start in zip((mine[n], theirs[n]), at):
            map_re = coil_buf[n, 0, pl.ds(start, own), :]
            map_im = coil_buf[n, 1, pl.ds(start, own), :]
            parts.append((map_re * block[0] - map_im * block[1], map_re * block[1] + map_im * block[0]))
        lines = columns_dft(
            jnp.concatenate([parts[0][0], parts[1][0]], axis=0),
            jnp.concatenate([parts[0][1], parts[1][1]], axis=0),
            col_fwd[...],
        )
        depth = lines.shape[1] // 2
        for part, start in enumerate(at):
            u_buf[0, pl.ds(start, own), :] = lines[part * own:(part + 1) * own, :depth]
            u_buf[1, pl.ds(start, own), :] = lines[part * own:(part + 1) * own, depth:]
        halves = []
        for odd, table in ((0, even_fwd), (1, odd_fwd)):
            cells = jnp.concatenate([
                jnp.concatenate([u_buf[part, pl.ds(p * height + odd, half, stride=2), :] for part in (0, 1)], axis=0)
                for p in range(planes)
            ], axis=1)
            halves.append(rows_dft(table[...], cells))
        loads[n][1].wait()
        loads[n][2].wait()
        spectrum = (halves[0] + halves[1], halves[0] - halves[1])
        updated = []
        for q in (0, 1):
            span = pl.ds(q * half, half)
            columns = []
            for p in range(planes):
                pieces = []
                for part in (0, 1):
                    value = spectrum[q][part * half:(part + 1) * half, p * depth:(p + 1) * depth]
                    new = weight[span, :] * (
                        dual_buf[n, part, p, span, :] + dual_step * (value - ksp_buf[n, part, p, span, :])
                    )
                    new_buf[n, part, p, span, :] = new
                    pieces.append(new)
                columns.append(jnp.concatenate(pieces, axis=0))
            updated.append(jnp.concatenate(columns, axis=1))
        chip = jnp.bitwise_xor(place[0], offset)
        store = pltpu.make_async_copy(
            new_buf.at[n], data_new.at[:, 0, 0, pl.ds(chip * planes, planes)], out_sem.at[n]
        )
        store.start()
        stores.append(store)
        for odd, table in ((0, even_bwd), (1, odd_bwd)):
            back = rows_dft(table[...], updated[0] - updated[1] if odd else updated[0] + updated[1])
            for p in range(planes):
                for part in (0, 1):
                    v_buf[part, pl.ds(p * height + odd, half, stride=2), :] = back[
                        part * half:(part + 1) * half, p * depth:(p + 1) * depth
                    ]
        plane = columns_dft(
            jnp.concatenate([v_buf[0, pl.ds(start, own), :] for start in at], axis=0),
            jnp.concatenate([v_buf[1, pl.ds(start, own), :] for start in at], axis=0),
            col_bwd[...],
        )
        for part, (target, start) in enumerate(zip((keep, give), at)):
            map_re = coil_buf[n, 0, pl.ds(start, own), :]
            map_im = coil_buf[n, 1, pl.ds(start, own), :]
            back_re = plane[part * own:(part + 1) * own, :depth]
            back_im = plane[part * own:(part + 1) * own, depth:]
            target[n, 0] = map_re * back_re + map_im * back_im
            target[n, 1] = map_re * back_im - map_im * back_re
    for store in stores:
        store.wait()


def coil_terms(offsets, place, mine, theirs, coil, dual, kspace, mask, constants, previous):
    count = len(offsets)
    own, depth = mine[0].shape[1:]
    height = mask.shape[1]
    planes = 2 * own // height
    vmem = pl.BlockSpec(memory_space=pltpu.VMEM)
    anywhere = pl.BlockSpec(memory_space=pl.ANY)
    operands = [place, *mine, *theirs, coil, dual, kspace, mask, *constants]
    in_specs = (
        [pl.BlockSpec(memory_space=pltpu.SMEM)] + [vmem] * (2 * count) + [anywhere] * 3 + [vmem] * 7
    )
    aliases = {}
    if previous is not None:
        aliases = {len(operands): 2}
        operands.append(previous)
        in_specs.append(anywhere)
    block = (count, 2, own, depth)
    planes_shape = (count, 2, planes, height, depth)
    return pl.pallas_call(
        functools.partial(coil_kernel, offsets, previous is not None),
        out_shape=[
            jax.ShapeDtypeStruct(block, jnp.float32),
            jax.ShapeDtypeStruct(block, jnp.float32),
            jax.ShapeDtypeStruct(dual.shape, jnp.float32),
        ],
        in_specs=in_specs,
        out_specs=[vmem, vmem, anywhere],
        scratch_shapes=[
            pltpu.VMEM((count, 2, 2 * own, depth), jnp.float32),
            pltpu.VMEM(planes_shape, jnp.float32),
            pltpu.VMEM(planes_shape, jnp.float32),
            pltpu.VMEM(planes_shape, jnp.float32),
            pltpu.VMEM((2, 2 * own, depth), jnp.float32),
            pltpu.VMEM((2, 2 * own, depth), jnp.float32),
            pltpu.VMEM((height, depth), jnp.float32),
            pltpu.SemaphoreType.DMA((count, 3)),
            pltpu.SemaphoreType.DMA((count,)),
        ],
        input_output_aliases=aliases,
        compiler_params=pltpu.CompilerParams(vmem_limit_bytes=24 * 1024 * 1024),
        cost_estimate=pl.CostEstimate(
            flops=count * 200_000_000, bytes_accessed=count * 1_400_000, transcendentals=0
        ),
    )(*operands)


def passed_along(value, axis, steps):
    count = lax.axis_size(axis)
    initial, last = (max(0, -steps), min(count, count - steps))
    return lax.ppermute(value, axis, [(source, source + steps) for source in range(initial, last)])


def project(real_part, imag_part):
    magnitude = jnp.sqrt(real_part * real_part + imag_part * imag_part)
    factor = clip_level / jnp.maximum(magnitude, clip_level)
    return (real_part * factor, imag_part * factor)


def swapped(value, mask):
    count = lax.axis_size("space")
    return lax.ppermute(value, "space", [(source, source ^ mask) for source in range(count)])


def on_device(image, extrap, tv_dual, data_dual, kspace, coil_maps, sampling):
    height, depth = kspace.shape[4:]
    chips = lax.axis_size("space") // 2
    inner = chips // 4
    here = lax.axis_index("space")
    place = jnp.stack([here // 2, here % 2]).astype(jnp.int32)
    constants = [
        jnp.asarray(table)
        for table in (
            column_table(depth, -1), *row_tables(height, -1), column_table(depth, 1), *row_tables(height, 1)
        )
    ]
    frame_here = lax.axis_index("tm")
    frame_total = lax.axis_size("tm")
    not_last = (frame_here < frame_total - 1).astype(jnp.float32)
    current = extrap[:, 0]

    mine = {0: current}
    for z in (2, 3):
        mine[z * inner] = swapped(current, 2 * z * inner)
    for i in range(1, inner):
        mine[i] = swapped(current, 2 * i)
    for i in range(inner):
        mine[inner + i] = swapped(mine[i], 2 * inner)
    for z in (2, 3):
        for i in range(1, inner):
            mine[z * inner + i] = swapped(mine[z * inner], 2 * i)
    theirs = {offset: swapped(block, 1) for offset, block in mine.items()}

    near = tuple(range(2 * inner))
    far = tuple(range(2 * inner, 4 * inner))
    sums = {}
    data_new = None
    for offsets in (near, far):
        keep, give, data_new = coil_terms(
            offsets, place, [mine[o] for o in offsets], [theirs[o] for o in offsets],
            coil_maps, data_dual, kspace, sampling, constants, data_new,
        )
        both = keep + swapped(give, 1)
        for n, offset in enumerate(offsets):
            sums[offset] = both[n]

    adjoint = sums[0]
    for z in (2, 3):
        term = sums[z * inner]
        for i in range(1, inner):
            term = term + swapped(sums[z * inner + i], 2 * i)
        adjoint = adjoint + swapped(term, 2 * z * inner)
    for i in range(inner):
        term = swapped(sums[inner + i], 2 * inner)
        if i:
            term = swapped(term + sums[i], 2 * i)
        adjoint = adjoint + term

    later = passed_along(current, "tm", -1)
    moved = tv_dual[:, 0] + dual_step * not_last * (later - current)
    tv_real, tv_imag = project(moved[0], moved[1])
    tv_here = jnp.stack([tv_real, tv_imag])
    earlier = passed_along(tv_here, "tm", 1)
    temporal = earlier - not_last * tv_here
    image_new = image[:, 0] - primal_step * (adjoint + temporal)
    return (image_new[:, None], tv_here[:, None], data_new)


def solution(mesh):
    in_specs = (
        P(None, "tm", "space", None),
        P(None, "tm", "space", None),
        P(None, "tm", "space", None),
        P(None, "tm", "space", None, None, None),
        P(None, "tm", "space", None, None, None),
        P(None, "space", None, None),
        P("tm", None, None),
    )
    out_specs = (
        P(None, "tm", "space", None),
        P(None, "tm", "space", None),
        P(None, "tm", "space", None, None, None),
    )
    return jax.shard_map(
        on_device, mesh=mesh, in_specs=in_specs, out_specs=out_specs, check_vma=False
    )
```

time: 198 us -> 84.8 us (0.43)
  waiting for transfers between devices: 142 us -> 29.7 us
  matrix products: 28.5 us -> 0 us
  starting transfers between devices: 2.81 us -> 25.9 us
  Pallas kernels: 0 us -> 14 us
  between operations: 14.3 us -> 0.9 us
  local copies, waits for them, and re-layouts: 1.17 us -> 12.8 us
  other arithmetic: 8.8 us -> 1.16 us
    psum x1 -> x0, waiting for transfers between devices: 85.5 us -> none  [on_device(): combined = lax.psum(coil_term, 'space')]
    all_gather x1 -> x0, waiting for transfers between devices: 47.4 us -> none  [on_device(): piece = lax.all_gather(current, 'space', axis=1, tiled=True)]
    ppermute x0 -> x24, waiting for transfers between devices: none -> 29.7 us  [swapped(): lax.ppermute(value, 'space', [(source, source ^ mask) for source in range...]
    dot_general x16 -> x0, matrix products: 28.5 us -> none  [the longest x8 16.3 us: left_mult(): jnp.einsum('ky,cxyz->cxkz', table, values, precision=highest, preferred_e...]
    ppermute x0 -> x24, starting transfers between devices: none -> 21.1 us  [swapped(): lax.ppermute(value, 'space', [(source, source ^ mask) for source in range...]
    pallas_call x0 -> x2, Pallas kernels: none -> 14 us  [coil_terms(): pl.pallas_call(functools.partial(coil_kernel, offsets, previous is not No...]
    unnamed x12 -> x44, local copies, waits for them, and re-layouts: 1.17 us -> 12.7 us
    ppermute x2, waiting for transfers between devices: 8.51 us -> 0.01 us  [passed_along(): lax.ppermute(value, axis, [(source, source + steps) for source in range(i...]
  transfers between devices with their start and end apart: 4 -> 26, of which waited for: 4 -> 6; matrix products, arithmetic and copies ran while one was open for 1% -> 1% of each run, Pallas kernels for 0% -> 17%
where the time goes in v1:
time: 84.8 us; the launch traced here: 84.3 us
  waiting for transfers between devices  29.7 us (35%)
  starting transfers between devices  25.9 us (31%)
  Pallas kernels  14 us (17%)
  local copies, waits for them, and re-layouts  12.8 us (15%)
  other arithmetic  1.16 us (1%)
  between operations  0.9 us (1%)
    ppermute x24, waiting for transfers between devices, swapped(): lax.ppermute(value, 'space', [(source, source ^ mask) for source in range...  29.7 us
    ppermute x24, starting transfers between devices, swapped(): lax.ppermute(value, 'space', [(source, source ^ mask) for source in range...  21.1 us
    pallas_call x2, Pallas kernels, coil_terms(): pl.pallas_call(functools.partial(coil_kernel, offsets, previous is not No...  14 us
    unnamed x44, local copies, waits for them, and re-layouts  12.7 us
    ppermute x2, starting transfers between devices, passed_along(): lax.ppermute(value, axis, [(source, source + steps) for source in range(i...  4.72 us
  transfers between devices with their start and end apart: 26, of which 6 were waited for; matrix products, arithmetic and copies ran while one was open for 1% of the time, Pallas kernels for 17%

profile of v1, /device:TPU:0, one launch (start us, length us, event | category | flops | bytes accessed | tf_op | source)
XLA Modules:
  0.0 84.3 jit_solution(6629527107369896092)
XLA Ops:
  0.6 3.0 %collective-permute-start = (f32[2,160,128]{2,1,0:T(8,128)}, f32[2,160,128]{2,1,0:T(8,128)S(1)}, u32[]{:S(2)}, u32[]{:S(2)}) collective-permute-start(f32[2,160,128]{2,1,0:T(8,128)} %bitcast.54), channel_id=1, source_target_pairs={{0,2},{1,3},{2,0},{3,1},{4,6},{5,7},{6,4},{7,5},{8,10},{9,11},{10,... | collective-permute-start | bytes 491528 | tf_op jit(solution)/shard_map/ppermute | solution.py:232
  3.6 3.6 %collective-permute-start.10 = (f32[2,160,128]{2,1,0:T(8,128)}, f32[2,160,128]{2,1,0:T(8,128)S(1)}, u32[]{:S(2)}, u32[]{:S(2)}) collective-permute-start(f32[2,160,128]{2,1,0:T(8,128)} %bitcast.55), channel_id=1, source_target_pairs={{0,12},{1,13},{2,14},{3,15},{4,8},{5,9},{6,10},{7,11},{8,4},{9,5},... | collective-permute-start | bytes 491528 | tf_op jit(solution)/shard_map/ppermute | solution.py:232
  7.2 0.8 collective-permute-start.1
  8.0 1.8 %collective-permute-start.2 = (f32[2,160,128]{2,1,0:T(8,128)S(1)}, f32[2,160,128]{2,1,0:T(8,128)S(1)}, u32[]{:S(2)}, u32[]{:S(2)}) collective-permute-start(f32[2,160,128]{2,1,0:T(8,128)S(1)} %collective-permute-done.refs_2_), channel_id=1, source_target_pairs={{0,4},{1,5},{2,6},{3,7},{4,0},{5,1},{6,2},{7,3},{8,12},{9,13},{10,... | collective-permute-start | bytes 491528 | tf_op jit(solution)/shard_map/ppermute | solution.py:232
  9.9 2.9 %collective-permute-done.10.refs_3_ = f32[2,160,128]{2,1,0:T(8,128)S(1)} collective-permute-done((f32[2,160,128]{2,1,0:T(8,128)}, f32[2,160,128]{2,1,0:T(8,128)S(1)}, u32[]{:S(2)}, u32[]{:S(2)}) %collective-permute-start.10) | collective-permute-done | bytes 163872 | tf_op jit(solution)/shard_map/ppermute | solution.py:232
  13.1 8.0 %collective-permute-done.8.refs_1_ = f32[2,160,128]{2,1,0:T(8,128)S(1)} collective-permute-done((f32[2,160,128]{2,1,0:T(8,128)}, f32[2,160,128]{2,1,0:T(8,128)S(1)}, u32[]{:S(2)}, u32[]{:S(2)}) %collective-permute-start.8) | collective-permute-done | bytes 163872 | tf_op jit(solution)/shard_map/ppermute | solution.py:232
  22.3 1.3 %collective-permute-start.24 = (f32[2,160,128]{2,1,0:T(8,128)}, f32[2,160,128]{2,1,0:T(8,128)S(1)}, u32[]{:S(2)}, u32[]{:S(2)}) collective-permute-start(f32[2,160,128]{2,1,0:T(8,128)} %bitcast.59), channel_id=1, source_target_pairs={{16,0},{17,1},{18,2},{19,3},{20,4},{21,5},{22,6},{23,7},{24,8},{25... | collective-permute-start | bytes 491528 | tf_op jit(solution)/shard_map/ppermute | solution.py:221
  23.6 2.9 %collective-permute-done.9.refs_2_ = f32[2,160,128]{2,1,0:T(8,128)S(1)} collective-permute-done((f32[2,160,128]{2,1,0:T(8,128)S(1)}, f32[2,160,128]{2,1,0:T(8,128)S(1)}, u32[]{:S(2)}, u32[]{:S(2)}) %collective-permute-start.9) | collective-permute-done | bytes 163872 | tf_op jit(solution)/shard_map/ppermute | solution.py:232
  27.6 1.7 %copy-done = f32[2,1,2560,128]{3,2,1,0:T(8,128)S(1)} copy-done((f32[2,1,2560,128]{3,2,1,0:T(8,128)S(1)}, f32[2,1,2560,128]{3,2,1,0:T(8,128)}, u32[]{:S(2)}) %copy-start) | copy-done | bytes 2621464
  29.3 1.7 %copy-done.2 = f32[2,1,1,16,160,128]{5,4,3,2,1,0:T(8,128)S(1)} copy-done((f32[2,1,1,16,160,128]{5,4,3,2,1,0:T(8,128)S(1)}, f32[2,1,1,16,160,128]{5,4,3,2,1,0:T(8,128)}, u32[]{:S(2)}) %copy-start.2) | copy-done | bytes 2621464
  31.1 1.7 %copy-done.4 = f32[2,1,1,16,160,128]{5,4,3,2,1,0:T(8,128)S(1)} copy-done((f32[2,1,1,16,160,128]{5,4,3,2,1,0:T(8,128)S(1)}, f32[2,1,1,16,160,128]{5,4,3,2,1,0:T(8,128)}, u32[]{:S(2)}) %copy-start.4) | copy-done | bytes 2621464
  32.8 1.0 %copy-done.6 = bf16[768,256]{1,0:T(8,128)(2,1)S(1)} copy-done((bf16[768,256]{1,0:T(8,128)(2,1)S(1)}, bf16[768,256]{1,0:T(8,128)(2,1)}, u32[]{:S(2)}) %copy-start.6) | copy-done | bytes 393240
  33.8 1.0 %copy-done.8 = bf16[768,256]{1,0:T(8,128)(2,1)S(1)} copy-done((bf16[768,256]{1,0:T(8,128)(2,1)S(1)}, bf16[768,256]{1,0:T(8,128)(2,1)}, u32[]{:S(2)}) %copy-start.8) | copy-done | bytes 393240
  34.8 0.9 %copy-done.10 = f32[2,1,160,128]{3,2,1,0:T(8,128)S(1)} copy-done((f32[2,1,160,128]{3,2,1,0:T(8,128)S(1)}, f32[2,1,160,128]{3,2,1,0:T(8,128)}, u32[]{:S(2)}) %copy-start.10) | copy-done | bytes 163864
  35.7 0.9 %copy-done.11 = bf16[160,480]{1,0:T(8,128)(2,1)S(1)} copy-done((bf16[160,480]{1,0:T(8,128)(2,1)S(1)}, bf16[160,480]{1,0:T(8,128)(2,1)}, u32[]{:S(2)}) %copy-start.11) | copy-done | bytes 153624
  36.6 0.9 %copy-done.13 = bf16[160,480]{1,0:T(8,128)(2,1)S(1)} copy-done((bf16[160,480]{1,0:T(8,128)(2,1)S(1)}, bf16[160,480]{1,0:T(8,128)(2,1)}, u32[]{:S(2)}) %copy-start.13) | copy-done | bytes 153624
  37.5 0.9 %copy-done.15 = bf16[160,480]{1,0:T(8,128)(2,1)S(1)} copy-done((bf16[160,480]{1,0:T(8,128)(2,1)S(1)}, bf16[160,480]{1,0:T(8,128)(2,1)}, u32[]{:S(2)}) %copy-start.15) | copy-done | bytes 153624
  38.5 0.9 %copy-done.17 = bf16[160,480]{1,0:T(8,128)(2,1)S(1)} copy-done((bf16[160,480]{1,0:T(8,128)(2,1)S(1)}, bf16[160,480]{1,0:T(8,128)(2,1)}, u32[]{:S(2)}) %copy-start.17) | copy-done | bytes 153624
  39.4 0.9 %copy-done.19 = s32[1,160,128]{2,1,0:T(8,128)S(1)} copy-done((s32[1,160,128]{2,1,0:T(8,128)S(1)}, s32[1,160,128]{2,1,0:T(8,128)}, u32[]{:S(2)}) %copy-start.19) | copy-done | bytes 81944
  40.3 7.0 %shard_map.148 = (f32[4,2,160,128]{3,2,1,0:T(8,128)S(1)}, f32[4,2,160,128]{3,2,1,0:T(8,128)S(1)}, f32[2,1,1,16,160,128]{5,4,3,2,1,0:T(8,128)}) custom-call(s32[2]{0:T(128)S(1)} %pad_add_fusion.refs_0_, f32[2,160,128]{2,1,0:T(8,128)S(1)} %bitcast.60, f32[2,160,128]{2,1,0:T(8,128)S(1)} %collective-permute-done.refs_2_, ...), custom_call_target="tpu_custom_call" | custom-call | flops 800000000 | bytes 5600000 | tf_op jit(solution)/shard_map/pallas_call | solution.py:190
  47.6 7.0 %shard_map.149 = (f32[4,2,160,128]{3,2,1,0:T(8,128)S(1)}, f32[4,2,160,128]{3,2,1,0:T(8,128)S(1)}, f32[2,1,1,16,160,128]{5,4,3,2,1,0:T(8,128)}) custom-call(s32[2]{0:T(128)S(1)} %pad_add_fusion.refs_0_, f32[2,160,128]{2,1,0:T(8,128)S(1)} %collective-permute-done.8.refs_1_, ...), custom_call_target="tpu_custom_call", output_to_operand_aliasing={{2}: (19, {})} | custom-call | flops 800000000 | bytes 5600000 | tf_op jit(solution)/shard_map/pallas_call | solution.py:190
  55.2 3.4 %collective-permute-start.25 = (f32[2,160,128]{2,1,0:T(8,128)S(1)}, f32[2,160,128]{2,1,0:T(8,128)S(1)}, u32[]{:S(2)}, u32[]{:S(2)}) collective-permute-start(f32[2,160,128]{2,1,0:T(8,128)S(1)} %pad_maximum_fusion), channel_id=1, source_target_pairs={{0,16},{1,17},{2,18},{3,19},{4,20},{5,21},{6,22},{7,23},{8,24},{9,... | collective-permute-start | bytes 491528 | tf_op jit(solution)/shard_map/ppermute | solution.py:221
  58.8 1.7 %collective-permute-start.21 = (f32[2,160,128]{2,1,0:T(8,128)S(1)}, f32[2,160,128]{2,1,0:T(8,128)S(1)}, u32[]{:S(2)}, u32[]{:S(2)}) collective-permute-start(f32[2,160,128]{2,1,0:T(8,128)S(1)} %get-tuple-element.22), channel_id=1, source_target_pairs={{0,4},{1,5},{2,6},{3,7},{4,0},{5,1},{6,2},{7,3},{8,12},{9,13},{10,... | collective-permute-start | bytes 491528 | tf_op jit(solution)/shard_map/ppermute | solution.py:232
  61.0 0.6 collective-permute-start.17
  61.6 1.5 %collective-permute-start.19 = (f32[2,160,128]{2,1,0:T(8,128)S(1)}, f32[2,160,128]{2,1,0:T(8,128)S(1)}, u32[]{:S(2)}, u32[]{:S(2)}) collective-permute-start(f32[2,160,128]{2,1,0:T(8,128)S(1)} %get-tuple-element.21), channel_id=1, source_target_pairs={{0,2},{1,3},{2,0},{3,1},{4,6},{5,7},{6,4},{7,5},{8,10},{9,11},{10,... | collective-permute-start | bytes 491528 | tf_op jit(solution)/shard_map/ppermute | solution.py:232
  63.1 5.2 %collective-permute-done.22 = f32[2,160,128]{2,1,0:T(8,128)S(1)} collective-permute-done((f32[2,160,128]{2,1,0:T(8,128)S(1)}, f32[2,160,128]{2,1,0:T(8,128)S(1)}, u32[]{:S(2)}, u32[]{:S(2)}) %collective-permute-start.22) | collective-permute-done | bytes 163872 | tf_op jit(solution)/shard_map/ppermute | solution.py:232
  68.3 0.6 collective-permute-start.23
  68.9 1.0 %collective-permute-done.19 = f32[2,160,128]{2,1,0:T(8,128)S(1)} collective-permute-done((f32[2,160,128]{2,1,0:T(8,128)S(1)}, f32[2,160,128]{2,1,0:T(8,128)S(1)}, u32[]{:S(2)}, u32[]{:S(2)}) %collective-permute-start.19) | collective-permute-done | bytes 163872 | tf_op jit(solution)/shard_map/ppermute | solution.py:232
  69.9 2.0 %collective-permute-start.18 = (f32[2,160,128]{2,1,0:T(8,128)S(1)}, f32[2,160,128]{2,1,0:T(8,128)S(1)}, u32[]{:S(2)}, u32[]{:S(2)}) collective-permute-start(f32[2,160,128]{2,1,0:T(8,128)S(1)} %get-tuple-element.18), channel_id=1, source_target_pairs={{0,8},{1,9},{2,10},{3,11},{4,12},{5,13},{6,14},{7,15},{8,0},{9,1},... | collective-permute-start | bytes 491528 | tf_op jit(solution)/shard_map/ppermute | solution.py:232
  72.0 2.0 %collective-permute-start.20 = (f32[2,160,128]{2,1,0:T(8,128)S(1)}, f32[2,160,128]{2,1,0:T(8,128)S(1)}, u32[]{:S(2)}, u32[]{:S(2)}) collective-permute-start(f32[2,160,128]{2,1,0:T(8,128)S(1)} %get-tuple-element.19), channel_id=1, source_target_pairs={{0,12},{1,13},{2,14},{3,15},{4,8},{5,9},{6,10},{7,11},{8,4},{9,5},... | collective-permute-start | bytes 491528 | tf_op jit(solution)/shard_map/ppermute | solution.py:232
  74.0 9.6 %collective-permute-done.18 = f32[2,160,128]{2,1,0:T(8,128)S(1)} collective-permute-done((f32[2,160,128]{2,1,0:T(8,128)S(1)}, f32[2,160,128]{2,1,0:T(8,128)S(1)}, u32[]{:S(2)}, u32[]{:S(2)}) %collective-permute-start.18) | collective-permute-done | bytes 163872 | tf_op jit(solution)/shard_map/ppermute | solution.py:232
  83.6 0.8 fusion.13
  (77 shorter events, 4.1 us)
Async XLA Ops:
  0.6 7.4 %collective-permute-start = (f32[2,160,128]{2,1,0:T(8,128)}, f32[2,160,128]{2,1,0:T(8,128)S(1)}, u32[]{:S(2)}, u32[]{:S(2)}) collective-permute-start(f32[2,160,128]{2,1,0:T(8,128)} %bitcast.54), channel_id=1, source_target_pairs={{0,2},{1,3},{2,0},{3,1},{4,6},{5,7},{6,4},{7,5},{8,10},{9,11},{10,... | collective-permute-start | bytes 491528 | tf_op jit(solution)/shard_map/ppermute | solution.py:232
  3.6 9.2 %collective-permute-start.10 = (f32[2,160,128]{2,1,0:T(8,128)}, f32[2,160,128]{2,1,0:T(8,128)S(1)}, u32[]{:S(2)}, u32[]{:S(2)}) collective-permute-start(f32[2,160,128]{2,1,0:T(8,128)} %bitcast.55), channel_id=1, source_target_pairs={{0,12},{1,13},{2,14},{3,15},{4,8},{5,9},{6,10},{7,11},{8,4},{9,5},... | collective-permute-start | bytes 491528 | tf_op jit(solution)/shard_map/ppermute | solution.py:232
  7.2 13.9 %collective-permute-start.8 = (f32[2,160,128]{2,1,0:T(8,128)}, f32[2,160,128]{2,1,0:T(8,128)S(1)}, u32[]{:S(2)}, u32[]{:S(2)}) collective-permute-start(f32[2,160,128]{2,1,0:T(8,128)} %bitcast.56), channel_id=1, source_target_pairs={{0,8},{1,9},{2,10},{3,11},{4,12},{5,13},{6,14},{7,15},{8,0},{9,1},... | collective-permute-start | bytes 491528 | tf_op jit(solution)/shard_map/ppermute | solution.py:232
  7.2 14.5 %collective-permute-start.1 = (f32[2,160,128]{2,1,0:T(8,128)}, f32[2,160,128]{2,1,0:T(8,128)S(1)}, u32[]{:S(2)}, u32[]{:S(2)}) collective-permute-start(f32[2,160,128]{2,1,0:T(8,128)} %bitcast.57), channel_id=1, source_target_pairs={{0,4},{1,5},{2,6},{3,7},{4,0},{5,1},{6,2},{7,3},{8,12},{9,13},{10,... | collective-permute-start | bytes 491528 | tf_op jit(solution)/shard_map/ppermute | solution.py:232
  8.0 13.7 %collective-permute-start.3 = (f32[2,160,128]{2,1,0:T(8,128)}, f32[2,160,128]{2,1,0:T(8,128)S(1)}, u32[]{:S(2)}, u32[]{:S(2)}) collective-permute-start(f32[2,160,128]{2,1,0:T(8,128)} %bitcast.58), channel_id=1, source_target_pairs={{0,1},{1,0},{2,3},{3,2},{4,5},{5,4},{6,7},{7,6},{8,9},{9,8},{10,11... | collective-permute-start | bytes 491528 | tf_op jit(solution)/shard_map/ppermute | solution.py:232
  8.0 14.2 %collective-permute-start.2 = (f32[2,160,128]{2,1,0:T(8,128)S(1)}, f32[2,160,128]{2,1,0:T(8,128)S(1)}, u32[]{:S(2)}, u32[]{:S(2)}) collective-permute-start(f32[2,160,128]{2,1,0:T(8,128)S(1)} %collective-permute-done.refs_2_), channel_id=1, source_target_pairs={{0,4},{1,5},{2,6},{3,7},{4,0},{5,1},{6,2},{7,3},{8,12},{9,13},{10,... | collective-permute-start | bytes 491528 | tf_op jit(solution)/shard_map/ppermute | solution.py:232
  12.8 9.5 %collective-permute-start.11 = (f32[2,160,128]{2,1,0:T(8,128)S(1)}, f32[2,160,128]{2,1,0:T(8,128)S(1)}, u32[]{:S(2)}, u32[]{:S(2)}) collective-permute-start(f32[2,160,128]{2,1,0:T(8,128)S(1)} %collective-permute-done.10.refs_3_), channel_id=1, source_target_pairs={{0,2},{1,3},{2,0},{3,1},{4,6},{5,7},{6,4},{7,5},{8,10},{9,11},{10,... | collective-permute-start | bytes 491528 | tf_op jit(solution)/shard_map/ppermute | solution.py:232
  21.2 5.3 %collective-permute-start.9 = (f32[2,160,128]{2,1,0:T(8,128)S(1)}, f32[2,160,128]{2,1,0:T(8,128)S(1)}, u32[]{:S(2)}, u32[]{:S(2)}) collective-permute-start(f32[2,160,128]{2,1,0:T(8,128)S(1)} %collective-permute-done.8.refs_1_), channel_id=1, source_target_pairs={{0,2},{1,3},{2,0},{3,1},{4,6},{5,7},{6,4},{7,5},{8,10},{9,11},{10,... | collective-permute-start | bytes 491528 | tf_op jit(solution)/shard_map/ppermute | solution.py:232
  21.7 4.8 %collective-permute-start.5 = (f32[2,160,128]{2,1,0:T(8,128)S(1)}, f32[2,160,128]{2,1,0:T(8,128)S(1)}, u32[]{:S(2)}, u32[]{:S(2)}) collective-permute-start(f32[2,160,128]{2,1,0:T(8,128)S(1)} %collective-permute-done.1.refs_3_), channel_id=1, source_target_pairs={{0,1},{1,0},{2,3},{3,2},{4,5},{5,4},{6,7},{7,6},{8,9},{9,8},{10,11... | collective-permute-start | bytes 491528 | tf_op jit(solution)/shard_map/ppermute | solution.py:232
  21.7 5.3 %collective-permute-start.4 = (f32[2,160,128]{2,1,0:T(8,128)S(1)}, f32[2,160,128]{2,1,0:T(8,128)S(1)}, u32[]{:S(2)}, u32[]{:S(2)}) collective-permute-start(f32[2,160,128]{2,1,0:T(8,128)S(1)} %collective-permute-done.refs_2_), channel_id=1, source_target_pairs={{0,1},{1,0},{2,3},{3,2},{4,5},{5,4},{6,7},{7,6},{8,9},{9,8},{10,11... | collective-permute-start | bytes 491528 | tf_op jit(solution)/shard_map/ppermute | solution.py:232
  22.2 4.9 %collective-permute-start.6 = (f32[2,160,128]{2,1,0:T(8,128)S(1)}, f32[2,160,128]{2,1,0:T(8,128)S(1)}, u32[]{:S(2)}, u32[]{:S(2)}) collective-permute-start(f32[2,160,128]{2,1,0:T(8,128)S(1)} %collective-permute-done.2.refs_4_), channel_id=1, source_target_pairs={{0,1},{1,0},{2,3},{3,2},{4,5},{5,4},{6,7},{7,6},{8,9},{9,8},{10,11... | collective-permute-start | bytes 491528 | tf_op jit(solution)/shard_map/ppermute | solution.py:232
  22.3 32.8 %collective-permute-start.24 = (f32[2,160,128]{2,1,0:T(8,128)}, f32[2,160,128]{2,1,0:T(8,128)S(1)}, u32[]{:S(2)}, u32[]{:S(2)}) collective-permute-start(f32[2,160,128]{2,1,0:T(8,128)} %bitcast.59), channel_id=1, source_target_pairs={{16,0},{17,1},{18,2},{19,3},{20,4},{21,5},{22,6},{23,7},{24,8},{25... | collective-permute-start | bytes 491528 | tf_op jit(solution)/shard_map/ppermute | solution.py:221
  26.5 20.8 %collective-permute-start.14 = (f32[2,160,128]{2,1,0:T(8,128)S(1)}, f32[2,160,128]{2,1,0:T(8,128)S(1)}, u32[]{:S(2)}, u32[]{:S(2)}) collective-permute-start(f32[2,160,128]{2,1,0:T(8,128)S(1)} %collective-permute-done.10.refs_3_), channel_id=1, source_target_pairs={{0,1},{1,0},{2,3},{3,2},{4,5},{5,4},{6,7},{7,6},{8,9},{9,8},{10,11... | collective-permute-start | bytes 491528 | tf_op jit(solution)/shard_map/ppermute | solution.py:232
  26.5 21.0 %collective-permute-start.12 = (f32[2,160,128]{2,1,0:T(8,128)S(1)}, f32[2,160,128]{2,1,0:T(8,128)S(1)}, u32[]{:S(2)}, u32[]{:S(2)}) collective-permute-start(f32[2,160,128]{2,1,0:T(8,128)S(1)} %collective-permute-done.8.refs_1_), channel_id=1, source_target_pairs={{0,1},{1,0},{2,3},{3,2},{4,5},{5,4},{6,7},{7,6},{8,9},{9,8},{10,11... | collective-permute-start | bytes 491528 | tf_op jit(solution)/shard_map/ppermute | solution.py:232
  27.0 20.5 %collective-permute-start.15 = (f32[2,160,128]{2,1,0:T(8,128)S(1)}, f32[2,160,128]{2,1,0:T(8,128)S(1)}, u32[]{:S(2)}, u32[]{:S(2)}) collective-permute-start(f32[2,160,128]{2,1,0:T(8,128)S(1)} %collective-permute-done.11.refs_4_), channel_id=1, source_target_pairs={{0,1},{1,0},{2,3},{3,2},{4,5},{5,4},{6,7},{7,6},{8,9},{9,8},{10,11... | collective-permute-start | bytes 491528 | tf_op jit(solution)/shard_map/ppermute | solution.py:232
  27.1 20.4 %collective-permute-start.13 = (f32[2,160,128]{2,1,0:T(8,128)S(1)}, f32[2,160,128]{2,1,0:T(8,128)S(1)}, u32[]{:S(2)}, u32[]{:S(2)}) collective-permute-start(f32[2,160,128]{2,1,0:T(8,128)S(1)} %collective-permute-done.9.refs_2_), channel_id=1, source_target_pairs={{0,1},{1,0},{2,3},{3,2},{4,5},{5,4},{6,7},{7,6},{8,9},{9,8},{10,11... | collective-permute-start | bytes 491528 | tf_op jit(solution)/shard_map/ppermute | solution.py:232
  40.3 7.2 %copy-start.7 = (bf16[768,256]{1,0:T(8,128)(2,1)S(1)}, bf16[768,256]{1,0:T(8,128)(2,1)}, u32[]{:S(2)}) copy-start(bf16[768,256]{1,0:T(8,128)(2,1)} %constant.56.clone.refs_16_) | copy-start | bytes 1179652
  40.3 7.3 %copy-start.9 = (bf16[768,256]{1,0:T(8,128)(2,1)S(1)}, bf16[768,256]{1,0:T(8,128)(2,1)}, u32[]{:S(2)}) copy-start(bf16[768,256]{1,0:T(8,128)(2,1)} %constant.53.clone.refs_13_) | copy-start | bytes 1179652
  40.3 7.3 %copy-start.12 = (bf16[160,480]{1,0:T(8,128)(2,1)S(1)}, bf16[160,480]{1,0:T(8,128)(2,1)}, u32[]{:S(2)}) copy-start(bf16[160,480]{1,0:T(8,128)(2,1)} %constant.58.clone.refs_18_) | copy-start | bytes 460804
  40.3 7.2 %copy-start.14 = (bf16[160,480]{1,0:T(8,128)(2,1)S(1)}, bf16[160,480]{1,0:T(8,128)(2,1)}, u32[]{:S(2)}) copy-start(bf16[160,480]{1,0:T(8,128)(2,1)} %constant.57.clone.refs_17_) | copy-start | bytes 460804
  47.3 11.3 %collective-permute-start.7 = (f32[4,2,160,128]{3,2,1,0:T(8,128)S(1)}, f32[4,2,160,128]{3,2,1,0:T(8,128)S(1)}, u32[]{:S(2)}, u32[]{:S(2)}) collective-permute-start(f32[4,2,160,128]{3,2,1,0:T(8,128)S(1)} %get-tuple-element.10), channel_id=1, source_target_pairs={{0,1},{1,0},{2,3},{3,2},{4,5},{5,4},{6,7},{7,6},{8,9},{9,8},{10,11... | collective-permute-start | bytes 1966088 | tf_op jit(solution)/shard_map/ppermute | solution.py:232
  47.6 7.5 %copy-start.21 = (f32[2,1,160,128]{3,2,1,0:T(8,128)S(1)}, f32[2,1,160,128]{3,2,1,0:T(8,128)}, u32[]{:S(2)}) copy-start(f32[2,1,160,128]{3,2,1,0:T(8,128)} %param.15) | copy-start | bytes 491524
  54.6 6.3 %collective-permute-start.16 = (f32[4,2,160,128]{3,2,1,0:T(8,128)S(1)}, f32[4,2,160,128]{3,2,1,0:T(8,128)S(1)}, u32[]{:S(2)}, u32[]{:S(2)}) collective-permute-start(f32[4,2,160,128]{3,2,1,0:T(8,128)S(1)} %get-tuple-element.13), channel_id=1, source_target_pairs={{0,1},{1,0},{2,3},{3,2},{4,5},{5,4},{6,7},{7,6},{8,9},{9,8},{10,11... | collective-permute-start | bytes 1966088 | tf_op jit(solution)/shard_map/ppermute | solution.py:232
  55.2 18.8 %collective-permute-start.25 = (f32[2,160,128]{2,1,0:T(8,128)S(1)}, f32[2,160,128]{2,1,0:T(8,128)S(1)}, u32[]{:S(2)}, u32[]{:S(2)}) collective-permute-start(f32[2,160,128]{2,1,0:T(8,128)S(1)} %pad_maximum_fusion), channel_id=1, source_target_pairs={{0,16},{1,17},{2,18},{3,19},{4,20},{5,21},{6,22},{7,23},{8,24},{9,... | collective-permute-start | bytes 491528 | tf_op jit(solution)/shard_map/ppermute | solution.py:221
  58.7 24.8 %copy-start.20 = (f32[2,1,160,128]{3,2,1,0:T(8,128)S(1)}, f32[2,1,160,128]{3,2,1,0:T(8,128)}, u32[]{:S(2)}) copy-start(f32[2,1,160,128]{3,2,1,0:T(8,128)} %param.13) | copy-start | bytes 491524
  58.8 15.2 %collective-permute-start.21 = (f32[2,160,128]{2,1,0:T(8,128)S(1)}, f32[2,160,128]{2,1,0:T(8,128)S(1)}, u32[]{:S(2)}, u32[]{:S(2)}) collective-permute-start(f32[2,160,128]{2,1,0:T(8,128)S(1)} %get-tuple-element.22), channel_id=1, source_target_pairs={{0,4},{1,5},{2,6},{3,7},{4,0},{5,1},{6,2},{7,3},{8,12},{9,13},{10,... | collective-permute-start | bytes 491528 | tf_op jit(solution)/shard_map/ppermute | solution.py:232
  60.4 7.8 %collective-permute-start.22 = (f32[2,160,128]{2,1,0:T(8,128)S(1)}, f32[2,160,128]{2,1,0:T(8,128)S(1)}, u32[]{:S(2)}, u32[]{:S(2)}) collective-permute-start(f32[2,160,128]{2,1,0:T(8,128)S(1)} %get-tuple-element.23), channel_id=1, source_target_pairs={{0,4},{1,5},{2,6},{3,7},{4,0},{5,1},{6,2},{7,3},{8,12},{9,13},{10,... | collective-permute-start | bytes 491528 | tf_op jit(solution)/shard_map/ppermute | solution.py:232
  61.0 7.9 %collective-permute-start.17 = (f32[2,160,128]{2,1,0:T(8,128)S(1)}, f32[2,160,128]{2,1,0:T(8,128)S(1)}, u32[]{:S(2)}, u32[]{:S(2)}) collective-permute-start(f32[2,160,128]{2,1,0:T(8,128)S(1)} %get-tuple-element.20), channel_id=1, source_target_pairs={{0,2},{1,3},{2,0},{3,1},{4,6},{5,7},{6,4},{7,5},{8,10},{9,11},{10,... | collective-permute-start | bytes 491528 | tf_op jit(solution)/shard_map/ppermute | solution.py:232
  61.6 8.3 %collective-permute-start.19 = (f32[2,160,128]{2,1,0:T(8,128)S(1)}, f32[2,160,128]{2,1,0:T(8,128)S(1)}, u32[]{:S(2)}, u32[]{:S(2)}) collective-permute-start(f32[2,160,128]{2,1,0:T(8,128)S(1)} %get-tuple-element.21), channel_id=1, source_target_pairs={{0,2},{1,3},{2,0},{3,1},{4,6},{5,7},{6,4},{7,5},{8,10},{9,11},{10,... | collective-permute-start | bytes 491528 | tf_op jit(solution)/shard_map/ppermute | solution.py:232
  68.3 5.7 %collective-permute-start.23 = (f32[2,160,128]{2,1,0:T(8,128)S(1)}, f32[2,160,128]{2,1,0:T(8,128)S(1)}, u32[]{:S(2)}, u32[]{:S(2)}) collective-permute-start(f32[2,160,128]{2,1,0:T(8,128)S(1)} %fusion), channel_id=1, source_target_pairs={{0,2},{1,3},{2,0},{3,1},{4,6},{5,7},{6,4},{7,5},{8,10},{9,11},{10,... | collective-permute-start | bytes 491528 | tf_op jit(solution)/shard_map/ppermute | solution.py:232
  69.9 13.6 %collective-permute-start.18 = (f32[2,160,128]{2,1,0:T(8,128)S(1)}, f32[2,160,128]{2,1,0:T(8,128)S(1)}, u32[]{:S(2)}, u32[]{:S(2)}) collective-permute-start(f32[2,160,128]{2,1,0:T(8,128)S(1)} %get-tuple-element.18), channel_id=1, source_target_pairs={{0,8},{1,9},{2,10},{3,11},{4,12},{5,13},{6,14},{7,15},{8,0},{9,1},... | collective-permute-start | bytes 491528 | tf_op jit(solution)/shard_map/ppermute | solution.py:232
  72.0 11.6 %collective-permute-start.20 = (f32[2,160,128]{2,1,0:T(8,128)S(1)}, f32[2,160,128]{2,1,0:T(8,128)S(1)}, u32[]{:S(2)}, u32[]{:S(2)}) collective-permute-start(f32[2,160,128]{2,1,0:T(8,128)S(1)} %get-tuple-element.19), channel_id=1, source_target_pairs={{0,12},{1,13},{2,14},{3,15},{4,8},{5,9},{6,10},{7,11},{8,4},{9,5},... | collective-permute-start | bytes 491528 | tf_op jit(solution)/shard_map/ppermute | solution.py:232
  (16 other events, 48.9 us)

commit v2 on v1

v2 whole, which is shorter than its diff:
```python
import functools
import math

import jax
import jax.numpy as jnp
import ml_dtypes
import numpy as np
from jax import lax
from jax.experimental import pallas as pl
from jax.experimental.pallas import tpu as pltpu
from jax.sharding import PartitionSpec as P

dual_step = 0.4
primal_step = 0.4
clip_level = 0.5


def split_host(table):
    high = table.astype(ml_dtypes.bfloat16)
    low = (table - high.astype(np.float64)).astype(ml_dtypes.bfloat16)
    return high, low


def column_table(length, sign):
    places = np.arange(length)
    angles = 2.0 * math.pi * (np.outer(places, places) % length) / length
    real = np.cos(angles) / math.sqrt(length)
    imag = sign * np.sin(angles) / math.sqrt(length)
    whole = np.block([[real, imag], [-imag, real]])
    high, low = split_host(whole)
    return np.concatenate([high, high, low], axis=0)


def row_tables(length, sign):
    half = length // 2
    found = []
    for odd in (0, 1):
        lines = np.arange(half)
        cells = 2 * np.arange(half) + odd
        product = np.outer(lines, cells)
        angles = 2.0 * math.pi * (product % length) / length
        real = np.cos(angles) / math.sqrt(length)
        imag = sign * np.sin(angles) / math.sqrt(length)
        if sign > 0:
            real, imag = real.T, imag.T
        whole = np.block([[real, -imag], [imag, real]])
        high, low = split_host(whole)
        found.append(np.concatenate([high, high, low], axis=1))
    return found


def split(values):
    high = values.astype(jnp.bfloat16)
    low = (values - high.astype(jnp.float32)).astype(jnp.bfloat16)
    return high, low


def columns_dft(real, imag, table):
    real_high, real_low = split(real)
    imag_high, imag_low = split(imag)
    left = jnp.concatenate([real_high, imag_high, real_low, imag_low, real_high, imag_high], axis=1)
    return jnp.dot(left, table, preferred_element_type=jnp.float32)


def rows_dft(table, values):
    high, low = split(values)
    return jnp.dot(table, jnp.concatenate([high, low, high], axis=0), preferred_element_type=jnp.float32)


def load_kernel(place, coil, dual, kspace, mask, coil_out, base, gain, ksp_buf, sem):
    count, _, rows, _ = coil_out.shape
    planes = base.shape[2]
    loads = []
    for offset in range(count):
        chip = jnp.bitwise_xor(place[0], offset)
        row0 = pl.multiple_of(chip * rows, rows)
        loads.append([
            pltpu.make_async_copy(
                dual.at[:, 0, 0, pl.ds(chip * planes, planes)], base.at[offset], sem.at[offset, 0]
            ),
            pltpu.make_async_copy(
                kspace.at[:, 0, 0, pl.ds(chip * planes, planes)], ksp_buf.at[offset], sem.at[offset, 1]
            ),
            pltpu.make_async_copy(
                coil.at[:, 0, pl.ds(row0, rows), :], coil_out.at[offset], sem.at[offset, 2]
            ),
        ])
        for load in loads[-1]:
            load.start()
    weight = mask[0].astype(jnp.float32) / (1.0 + dual_step)
    gain[...] = weight * dual_step
    for offset in range(count):
        loads[offset][0].wait()
        loads[offset][1].wait()
        for part in (0, 1):
            for p in range(planes):
                base[offset, part, p] = weight * (
                    base[offset, part, p] - dual_step * ksp_buf[offset, part, p]
                )
    for offset in range(count):
        loads[offset][2].wait()


def coil_kernel(first, count, passing, place, *refs):
    mine, theirs, refs = refs[:count], refs[count:2 * count], refs[2 * count:]
    coil, base, gain = refs[:3]
    col_fwd, even_fwd, odd_fwd, col_bwd, even_bwd, odd_bwd = refs[3:9]
    keep, give, data_new = refs[9 + passing:12 + passing]
    u_buf, v_buf = refs[-2:]
    own = mine[0].shape[1]
    height, depth = gain.shape
    half = height // 2
    planes = base.shape[2]
    core = place[1]
    at = [pl.multiple_of(core * own, own), pl.multiple_of((1 - core) * own, own)]
    for n in reversed(range(count)):
        parts = []
        for block, start in zip((mine[n], theirs[n]), at):
            map_re = coil[first + n, 0, pl.ds(start, own), :]
            map_im = coil[first + n, 1, pl.ds(start, own), :]
            parts.append((map_re * block[0] - map_im * block[1], map_re * block[1] + map_im * block[0]))
        lines = columns_dft(
            jnp.concatenate([parts[0][0], parts[1][0]], axis=0),
            jnp.concatenate([parts[0][1], parts[1][1]], axis=0),
            col_fwd[...],
        )
        for part, start in enumerate(at):
            u_buf[0, pl.ds(start, own), :] = lines[part * own:(part + 1) * own, :depth]
            u_buf[1, pl.ds(start, own), :] = lines[part * own:(part + 1) * own, depth:]
        halves = []
        for odd, table in ((0, even_fwd), (1, odd_fwd)):
            cells = jnp.concatenate([
                jnp.concatenate([u_buf[part, pl.ds(p * height + odd, half, stride=2), :] for part in (0, 1)], axis=0)
                for p in range(planes)
            ], axis=1)
            halves.append(rows_dft(table[...], cells))
        spectrum = (halves[0] + halves[1], halves[0] - halves[1])
        updated = []
        for q in (0, 1):
            span = pl.ds(q * half, half)
            columns = []
            for p in range(planes):
                pieces = []
                for part in (0, 1):
                    value = spectrum[q][part * half:(part + 1) * half, p * depth:(p + 1) * depth]
                    new = gain[span, :] * value + base[first + n, part, p, span, :]
                    data_new[n, part, p, span, :] = new
                    pieces.append(new)
                columns.append(jnp.concatenate(pieces, axis=0))
            updated.append(jnp.concatenate(columns, axis=1))
        for odd, table in ((0, even_bwd), (1, odd_bwd)):
            back = rows_dft(table[...], updated[0] - updated[1] if odd else updated[0] + updated[1])
            for p in range(planes):
                for part in (0, 1):
                    v_buf[part, pl.ds(p * height + odd, half, stride=2), :] = back[
                        part * half:(part + 1) * half, p * depth:(p + 1) * depth
                    ]
        plane = columns_dft(
            jnp.concatenate([v_buf[0, pl.ds(start, own), :] for start in at], axis=0),
            jnp.concatenate([v_buf[1, pl.ds(start, own), :] for start in at], axis=0),
            col_bwd[...],
        )
        for part, (target, start) in enumerate(zip((keep, give), at)):
            map_re = coil[first + n, 0, pl.ds(start, own), :]
            map_im = coil[first + n, 1, pl.ds(start, own), :]
            back_re = plane[part * own:(part + 1) * own, :depth]
            back_im = plane[part * own:(part + 1) * own, depth:]
            target[n, 0] = map_re * back_re + map_im * back_im
            target[n, 1] = map_re * back_im - map_im * back_re


def store_kernel(place, *refs):
    groups, data_new, sem = refs[:-2], refs[-2], refs[-1]
    count, _, planes = groups[0].shape[:3]
    stores = []
    for g, group in enumerate(groups):
        for n in range(count):
            chip = jnp.bitwise_xor(place[0], g * count + n)
            stores.append(pltpu.make_async_copy(
                group.at[n], data_new.at[:, 0, 0, pl.ds(chip * planes, planes)], sem.at[g * count + n]
            ))
            stores[-1].start()
    for store in stores:
        store.wait()


vmem = pl.BlockSpec(memory_space=pltpu.VMEM)
smem = pl.BlockSpec(memory_space=pltpu.SMEM)
hbm = pl.BlockSpec(memory_space=pltpu.HBM)
anywhere = pl.BlockSpec(memory_space=pl.ANY)
mebi = 1024 * 1024


def load_all(place, chips, own, coil, dual, kspace, mask):
    height, depth = mask.shape[1:]
    planes = 2 * own // height
    return pl.pallas_call(
        load_kernel,
        out_shape=[
            jax.ShapeDtypeStruct((chips, 2, 2 * own, depth), jnp.float32),
            jax.ShapeDtypeStruct((chips, 2, planes, height, depth), jnp.float32),
            jax.ShapeDtypeStruct((height, depth), jnp.float32),
        ],
        in_specs=[smem, hbm, hbm, hbm, vmem],
        out_specs=[vmem, vmem, vmem],
        scratch_shapes=[
            pltpu.VMEM((chips, 2, planes, height, depth), jnp.float32),
            pltpu.SemaphoreType.DMA((chips, 3)),
        ],
        compiler_params=pltpu.CompilerParams(vmem_limit_bytes=46 * mebi),
        cost_estimate=pl.CostEstimate(flops=4_000_000, bytes_accessed=8_000_000, transcendentals=0),
        name="load",
    )(place, coil, dual, kspace, mask)


def coil_terms(first, place, mine, theirs, coil, base, gain, constants, passed):
    count = len(mine)
    operands = [place, *mine, *theirs, coil, base, gain, *constants]
    own, depth = mine[0].shape[1:]
    block = (count, 2, own, depth)
    return pl.pallas_call(
        functools.partial(coil_kernel, first, count, len(passed)),
        out_shape=[
            jax.ShapeDtypeStruct(block, jnp.float32),
            jax.ShapeDtypeStruct(block, jnp.float32),
            jax.ShapeDtypeStruct((count,) + base.shape[1:], jnp.float32),
        ] + [jax.ShapeDtypeStruct(value.shape, value.dtype) for value in passed],
        in_specs=[smem] + [vmem] * (len(operands) - 1) + [anywhere] * len(passed),
        out_specs=[vmem, vmem, vmem] + [anywhere] * len(passed),
        input_output_aliases={len(operands) + n: 3 + n for n in range(len(passed))},
        scratch_shapes=[
            pltpu.VMEM((2, 2 * own, depth), jnp.float32),
            pltpu.VMEM((2, 2 * own, depth), jnp.float32),
        ],
        compiler_params=pltpu.CompilerParams(vmem_limit_bytes=20 * mebi),
        cost_estimate=pl.CostEstimate(
            flops=count * 800_000_000, bytes_accessed=count * 100_000, transcendentals=0
        ),
        name="coils",
    )(*operands, *passed)


def store_all(place, groups, kspace):
    count = len(groups) * groups[0].shape[0]
    return pl.pallas_call(
        store_kernel,
        out_shape=jax.ShapeDtypeStruct(kspace.shape, jnp.float32),
        in_specs=[smem] + [vmem] * len(groups),
        out_specs=hbm,
        scratch_shapes=[pltpu.SemaphoreType.DMA((count,))],
        compiler_params=pltpu.CompilerParams(vmem_limit_bytes=20 * mebi),
        cost_estimate=pl.CostEstimate(flops=0, bytes_accessed=2_600_000, transcendentals=0),
        name="store",
    )(place, *groups)


def turned(value, axis, steps):
    count = lax.axis_size(axis)
    return lax.ppermute(value, axis, [(source, (source + steps) % count) for source in range(count)])


def project(moved):
    magnitude = jnp.sqrt(moved[0] * moved[0] + moved[1] * moved[1])
    return moved * (clip_level / jnp.maximum(magnitude, clip_level))


def swapped(value, mask):
    count = lax.axis_size("space")
    return lax.ppermute(value, "space", [(source, source ^ mask) for source in range(count)])


def on_device(image, extrap, tv_dual, data_dual, kspace, coil_maps, sampling):
    height, depth = kspace.shape[4:]
    chips = lax.axis_size("space") // 2
    inner = chips // 4
    here = lax.axis_index("space")
    place = jnp.stack([here // 2, here % 2]).astype(jnp.int32)
    constants = [
        jnp.asarray(table)
        for table in (
            column_table(depth, -1), *row_tables(height, -1), column_table(depth, 1), *row_tables(height, 1)
        )
    ]
    frame_here = lax.axis_index("tm")
    frame_total = lax.axis_size("tm")
    not_first = (frame_here > 0).astype(jnp.float32)
    not_last = (frame_here < frame_total - 1).astype(jnp.float32)
    current = extrap[:, 0]

    later = turned(current, "tm", -1)
    previous = later if frame_total == 2 else turned(current, "tm", 1)
    dual_before = turned(tv_dual[:, 0], "tm", 1)
    tv_here = project(tv_dual[:, 0] + dual_step * not_last * (later - current))
    earlier = not_first * project(dual_before + dual_step * (current - previous))
    start = image[:, 0] - primal_step * (earlier - not_last * tv_here)

    mine = {0: current}
    mine[2 * inner] = swapped(current, 4 * inner)
    for i in range(1, inner):
        mine[i] = swapped(current, 2 * i)
    mine[inner] = swapped(current, 2 * inner)
    mine[3 * inner] = swapped(mine[2 * inner], 2 * inner)
    for z in (1, 2, 3):
        for i in range(1, inner):
            mine[z * inner + i] = swapped(mine[z * inner], 2 * i)
    theirs = {offset: swapped(block, 1) for offset, block in mine.items()}

    coil, base, gain = load_all(place, chips, current.shape[1], coil_maps, data_dual, kspace, sampling)
    sums = {}
    updated = []
    for z in range(4):
        offsets = [z * inner + i for i in range(inner)]
        keep, give, new, *passed = coil_terms(
            z * inner, place, [mine[o] for o in offsets], [theirs[o] for o in offsets],
            coil, base, gain, constants, [start] if z == 0 else [],
        )
        if passed:
            start, = passed
        sums[z] = keep + swapped(give, 1)
        updated.append(new)
    data_new = store_all(place, updated, kspace)

    adjoint = 0.0
    for z in (3, 2):
        term = sums[z][0]
        for i in range(1, inner):
            term = term + swapped(sums[z][i], 2 * i)
        adjoint = adjoint + swapped(term, 2 * z * inner)
    term = sums[0] + swapped(sums[1], 2 * inner)
    adjoint = adjoint + term[0]
    for i in range(1, inner):
        adjoint = adjoint + swapped(term[i], 2 * i)

    image_new = start - primal_step * adjoint
    return (image_new[:, None], tv_here[:, None], data_new)


def solution(mesh):
    in_specs = (
        P(None, "tm", "space", None),
        P(None, "tm", "space", None),
        P(None, "tm", "space", None),
        P(None, "tm", "space", None, None, None),
        P(None, "tm", "space", None, None, None),
        P(None, "space", None, None),
        P("tm", None, None),
    )
    out_specs = (
        P(None, "tm", "space", None),
        P(None, "tm", "space", None),
        P(None, "tm", "space", None, None, None),
    )
    return jax.shard_map(
        on_device, mesh=mesh, in_specs=in_specs, out_specs=out_specs, check_vma=False
    )
```

time: 84.8 us -> 65.6 us (0.77)
  local copies, waits for them, and re-layouts: 12.8 us -> 2.71 us
  waiting for transfers between devices: 29.7 us -> 20.2 us
  starting transfers between devices: 25.9 us -> 22.8 us
  Pallas kernels: 14 us -> 17 us
    unnamed x44 -> x22, local copies, waits for them, and re-layouts: 12.7 us -> 2.67 us
    ppermute x24 -> x25, waiting for transfers between devices: 29.7 us -> 20.2 us  [swapped(): lax.ppermute(value, 'space', [(source, source ^ mask) for source in range...]
    pallas_call x2 -> x6, Pallas kernels: 14 us -> 17 us  [the longest x4 11.6 us: coil_terms(): pl.pallas_call(functools.partial(coil_kernel, first, count, len(passed)),...]
    ppermute x2, starting transfers between devices: 4.72 us -> 2.03 us  [turned(): lax.ppermute(value, axis, [(source, (source + steps) % count) for source...]
    ppermute x24 -> x25, starting transfers between devices: 21.1 us -> 20.7 us  [swapped(): lax.ppermute(value, 'space', [(source, source ^ mask) for source in range...]
  transfers between devices with their start and end apart: 26 -> 27, of which waited for: 6 -> 5; matrix products, arithmetic and copies ran while one was open for 1% -> 2% of each run, Pallas kernels for 17% -> 26%
where the time goes in v2:
time: 65.6 us; the launch traced here: 65.4 us
  starting transfers between devices  22.8 us (35%)
  waiting for transfers between devices  20.2 us (31%)
  Pallas kernels  17 us (26%)
  local copies, waits for them, and re-layouts  2.71 us (4%)
  other arithmetic  1.81 us (3%)
  between operations  0.9 us (1%)
    ppermute x25, starting transfers between devices, swapped(): lax.ppermute(value, 'space', [(source, source ^ mask) for source in range...  20.7 us
    ppermute x25, waiting for transfers between devices, swapped(): lax.ppermute(value, 'space', [(source, source ^ mask) for source in range...  20.2 us
    pallas_call x4, Pallas kernels, coil_terms(): pl.pallas_call(functools.partial(coil_kernel, first, count, len(passed)),...  11.6 us
    pallas_call x1, Pallas kernels, load_all(): pl.pallas_call(load_kernel, out_shape=[jax.ShapeDtypeStruct((chips, 2, 2...  3.37 us
    unnamed x22, local copies, waits for them, and re-layouts  2.67 us
    pallas_call x1, Pallas kernels, store_all(): pl.pallas_call(store_kernel, out_shape=jax.ShapeDtypeStruct(kspace.shape,...  2.09 us
    ppermute x2, starting transfers between devices, turned(): lax.ppermute(value, axis, [(source, (source + steps) % count) for source...  2.03 us
    unnamed x2, other arithmetic  1.42 us
  transfers between devices with their start and end apart: 27, of which 5 were waited for; matrix products, arithmetic and copies ran while one was open for 2% of the time, Pallas kernels for 26%

profile of v2, /device:TPU:0, one launch (start us, length us, event | category | flops | bytes accessed | tf_op | source)
XLA Modules:
  0.0 65.4 jit_solution(5523395646416513460)
XLA Ops:
  0.6 4.1 %collective-permute-start.5 = (f32[2,160,128]{2,1,0:T(8,128)}, f32[2,160,128]{2,1,0:T(8,128)S(1)}, u32[]{:S(2)}, u32[]{:S(2)}) collective-permute-start(f32[2,160,128]{2,1,0:T(8,128)} %bitcast.47), channel_id=1, source_target_pairs={{0,8},{1,9},{2,10},{3,11},{4,12},{5,13},{6,14},{7,15},{8,0},{9,1},... | collective-permute-start | bytes 491528 | tf_op jit(solution)/shard_map/ppermute | solution.py:269
  4.7 1.5 %collective-permute-start.4 = (f32[2,160,128]{2,1,0:T(8,128)}, f32[2,160,128]{2,1,0:T(8,128)S(1)}, u32[]{:S(2)}, u32[]{:S(2)}) collective-permute-start(f32[2,160,128]{2,1,0:T(8,128)} %bitcast.48), channel_id=1, source_target_pairs={{0,16},{16,0},{1,17},{17,1},{2,18},{18,2},{3,19},{19,3},{4,20},{20... | collective-permute-start | bytes 491528 | tf_op jit(solution)/shard_map/ppermute | solution.py:259
  6.3 0.5 collective-permute-start.3
  6.8 1.6 %collective-permute-start.20 = (f32[2,160,128]{2,1,0:T(8,128)}, f32[2,160,128]{2,1,0:T(8,128)S(1)}, u32[]{:S(2)}, u32[]{:S(2)}) collective-permute-start(f32[2,160,128]{2,1,0:T(8,128)} %bitcast.49), channel_id=1, source_target_pairs={{0,4},{1,5},{2,6},{3,7},{4,0},{5,1},{6,2},{7,3},{8,12},{9,13},{10,... | collective-permute-start | bytes 491528 | tf_op jit(solution)/shard_map/ppermute | solution.py:269
  8.3 1.5 %collective-permute-start = (f32[2,160,128]{2,1,0:T(8,128)}, f32[2,160,128]{2,1,0:T(8,128)S(1)}, u32[]{:S(2)}, u32[]{:S(2)}) collective-permute-start(f32[2,160,128]{2,1,0:T(8,128)} %bitcast.50), channel_id=1, source_target_pairs={{0,2},{1,3},{2,0},{3,1},{4,6},{5,7},{6,4},{7,5},{8,10},{9,11},{10,... | collective-permute-start | bytes 491528 | tf_op jit(solution)/shard_map/ppermute | solution.py:269
  9.9 1.7 %copy-done.2 = f32[2,1,2560,128]{3,2,1,0:T(8,128)S(1)} copy-done((f32[2,1,2560,128]{3,2,1,0:T(8,128)S(1)}, f32[2,1,2560,128]{3,2,1,0:T(8,128)}, u32[]{:S(2)}) %copy-start.2) | copy-done | bytes 2621464
  11.6 0.9 %copy-done.8 = s32[1,160,128]{2,1,0:T(8,128)S(1)} copy-done((s32[1,160,128]{2,1,0:T(8,128)S(1)}, s32[1,160,128]{2,1,0:T(8,128)}, u32[]{:S(2)}) %copy-start.8) | copy-done | bytes 81944
  12.6 3.4 %load.1 = (f32[8,2,320,128]{3,2,1,0:T(8,128)S(1)}, f32[8,2,2,160,128]{4,3,2,1,0:T(8,128)S(1)}, f32[160,128]{1,0:T(8,128)S(1)}) custom-call(s32[2]{0:T(128)S(1)} %pad_add_fusion.place, f32[2,1,2560,128]{3,2,1,0:T(8,128)S(1)} %copy-done.2, f32[2,1,1,16,160,128]{5,4,3,2,1,0:T(8,128)} %dual.1, f32[2,1,1,16,160,128]{5,4,3,2,1,0:T(8,128)} %kspace.1, ...), custom_call_target="tpu_custom_call" | custom-call | flops 4000000 | bytes 8000000 | tf_op jit(solution)/shard_map/load/pallas_call | solution.py:197
  16.0 0.5 collective-permute-start.6
  16.5 0.5 collective-permute-start.13
  17.0 1.6 %collective-permute-start.21 = (f32[2,160,128]{2,1,0:T(8,128)S(1)}, f32[2,160,128]{2,1,0:T(8,128)S(1)}, u32[]{:S(2)}, u32[]{:S(2)}) collective-permute-start(f32[2,160,128]{2,1,0:T(8,128)S(1)} %collective-permute-done.20.refs_0_), channel_id=1, source_target_pairs={{0,2},{1,3},{2,0},{3,1},{4,6},{5,7},{6,4},{7,5},{8,10},{9,11},{10,... | collective-permute-start | bytes 491528 | tf_op jit(solution)/shard_map/ppermute | solution.py:269
  18.7 4.8 %collective-permute-done.13.refs_1_ = f32[2,160,128]{2,1,0:T(8,128)S(1)} collective-permute-done((f32[2,160,128]{2,1,0:T(8,128)S(1)}, f32[2,160,128]{2,1,0:T(8,128)S(1)}, u32[]{:S(2)}, u32[]{:S(2)}) %collective-permute-start.13) | collective-permute-done | bytes 163872 | tf_op jit(solution)/shard_map/ppermute | solution.py:269
  23.6 1.8 %collective-permute-done.21.refs_1_ = f32[2,160,128]{2,1,0:T(8,128)S(1)} collective-permute-done((f32[2,160,128]{2,1,0:T(8,128)S(1)}, f32[2,160,128]{2,1,0:T(8,128)S(1)}, u32[]{:S(2)}, u32[]{:S(2)}) %collective-permute-start.21) | collective-permute-done | bytes 163872 | tf_op jit(solution)/shard_map/ppermute | solution.py:269
  25.3 0.5 collective-permute-start.23
  25.8 0.5 collective-permute-start.7
  26.4 2.9 %coils.6 = (f32[2,2,160,128]{3,2,1,0:T(8,128)S(1)}, f32[2,2,160,128]{3,2,1,0:T(8,128)S(1)}, f32[2,2,2,160,128]{4,3,2,1,0:T(8,128)S(1)}) custom-call(s32[2]{0:T(128)S(1)} %pad_add_fusion.place, f32[2,160,128]{2,1,0:T(8,128)S(1)} %collective-permute-done.5.refs_0_, f32[2,160,128]{2,1,0:T(8,128)S(1)} %collective-permute-done.13.refs_1_, ...), custom_call_target="tpu_custom_call" | custom-call | flops 1600000000 | bytes 200000 | tf_op jit(solution)/shard_map/coils/pallas_call | solution.py:221
  29.4 0.7 %multiply_bitcast_fusion = (f32[2,1,160,128]{3,2,1,0:T(8,128)}, f32[2,160,128]{2,1,0:T(8,128)S(1)}) fusion(f32[2,160,128]{2,1,0:T(8,128)S(1)} %get-tuple-element.38, f32[160,128]{1,0:T(8,128)S(1)} %get-tuple-element.42, f32[]{:T(128)S(6)} %convert_element_type.7, f32[2,160,128]{2,1,0:T(8,128)S(1)} %get-tuple-element.39, ...), kind=kLoop, calls=%fused_computation.17 | loop fusion | flops 286720 | bytes 983048
  30.2 0.5 collective-permute-start.1
  31.2 2.9 %coils.7 = (f32[2,2,160,128]{3,2,1,0:T(8,128)S(1)}, f32[2,2,160,128]{3,2,1,0:T(8,128)S(1)}, f32[2,2,2,160,128]{4,3,2,1,0:T(8,128)S(1)}) custom-call(s32[2]{0:T(128)S(1)} %pad_add_fusion.place, f32[2,160,128]{2,1,0:T(8,128)S(1)} %collective-permute-done.20.refs_0_, f32[2,160,128]{2,1,0:T(8,128)S(1)} %collective-permute-done.21.refs_1_, ...), custom_call_target="tpu_custom_call" | custom-call | flops 1600000000 | bytes 200000 | tf_op jit(solution)/shard_map/coils/pallas_call | solution.py:221
  34.7 1.5 %collective-permute-start.17 = (f32[2,160,128]{2,1,0:T(8,128)S(1)}, f32[2,160,128]{2,1,0:T(8,128)S(1)}, u32[]{:S(2)}, u32[]{:S(2)}) collective-permute-start(f32[2,160,128]{2,1,0:T(8,128)S(1)} %slice_bitcast_fusion.2), channel_id=1, source_target_pairs={{0,2},{1,3},{2,0},{3,1},{4,6},{5,7},{6,4},{7,5},{8,10},{9,11},{10,... | collective-permute-start | bytes 491528 | tf_op jit(solution)/shard_map/ppermute | solution.py:269
  36.3 2.9 %coils.5 = (f32[2,2,160,128]{3,2,1,0:T(8,128)S(1)}, f32[2,2,160,128]{3,2,1,0:T(8,128)S(1)}, f32[2,2,2,160,128]{4,3,2,1,0:T(8,128)S(1)}) custom-call(s32[2]{0:T(128)S(1)} %pad_add_fusion.place, f32[2,160,128]{2,1,0:T(8,128)S(1)} %collective-permute-done.6.refs_0_, f32[2,160,128]{2,1,0:T(8,128)S(1)} %collective-permute-done.7.refs_1_, ...), custom_call_target="tpu_custom_call" | custom-call | flops 1600000000 | bytes 200000 | tf_op jit(solution)/shard_map/coils/pallas_call | solution.py:221
  39.2 2.9 %coils.4 = (f32[2,2,160,128]{3,2,1,0:T(8,128)S(1)}, f32[2,2,160,128]{3,2,1,0:T(8,128)S(1)}, f32[2,2,2,160,128]{4,3,2,1,0:T(8,128)S(1)}, f32[2,160,128]{2,1,0:T(8,128)S(1)}) custom-call(s32[2]{0:T(128)S(1)} %pad_add_fusion.place, f32[2,160,128]{2,1,0:T(8,128)S(1)} %bitcast.52, ...), custom_call_target="tpu_custom_call", output_to_operand_aliasing={{3}: (14, {})} | custom-call | flops 1600000000 | bytes 200000 | tf_op jit(solution)/shard_map/coils/pallas_call | solution.py:221
  42.1 0.5 collective-permute-start.19
  42.7 1.6 %collective-permute-start.25 = (f32[2,2,160,128]{3,2,1,0:T(8,128)S(1)}, f32[2,2,160,128]{3,2,1,0:T(8,128)S(1)}, u32[]{:S(2)}, u32[]{:S(2)}) collective-permute-start(f32[2,2,160,128]{3,2,1,0:T(8,128)S(1)} %add.60), channel_id=1, source_target_pairs={{0,4},{1,5},{2,6},{3,7},{4,0},{5,1},{6,2},{7,3},{8,12},{9,13},{10,... | collective-permute-start | bytes 983048 | tf_op jit(solution)/shard_map/ppermute | solution.py:269
  44.9 1.3 %collective-permute-start.11 = (f32[2,160,128]{2,1,0:T(8,128)S(1)}, f32[2,160,128]{2,1,0:T(8,128)S(1)}, u32[]{:S(2)}, u32[]{:S(2)}) collective-permute-start(f32[2,160,128]{2,1,0:T(8,128)S(1)} %slice_bitcast_fusion.4), channel_id=1, source_target_pairs={{0,2},{1,3},{2,0},{3,1},{4,6},{5,7},{6,4},{7,5},{8,10},{9,11},{10,... | collective-permute-start | bytes 491528 | tf_op jit(solution)/shard_map/ppermute | solution.py:269
  46.1 9.8 %collective-permute-done.25 = f32[2,2,160,128]{3,2,1,0:T(8,128)S(1)} collective-permute-done((f32[2,2,160,128]{3,2,1,0:T(8,128)S(1)}, f32[2,2,160,128]{3,2,1,0:T(8,128)S(1)}, u32[]{:S(2)}, u32[]{:S(2)}) %collective-permute-start.25) | collective-permute-done | bytes 327712 | tf_op jit(solution)/shard_map/ppermute | solution.py:269
  56.0 1.4 %collective-permute-start.26 = (f32[2,160,128]{2,1,0:T(8,128)S(1)}, f32[2,160,128]{2,1,0:T(8,128)S(1)}, u32[]{:S(2)}, u32[]{:S(2)}) collective-permute-start(f32[2,160,128]{2,1,0:T(8,128)S(1)} %slice_bitcast_fusion), channel_id=1, source_target_pairs={{0,2},{1,3},{2,0},{3,1},{4,6},{5,7},{6,4},{7,5},{8,10},{9,11},{10,... | collective-permute-start | bytes 491528 | tf_op jit(solution)/shard_map/ppermute | solution.py:269
  57.4 1.4 %collective-permute-start.12 = (f32[2,160,128]{2,1,0:T(8,128)S(1)}, f32[2,160,128]{2,1,0:T(8,128)S(1)}, u32[]{:S(2)}, u32[]{:S(2)}) collective-permute-start(f32[2,160,128]{2,1,0:T(8,128)S(1)} %fusion.6), channel_id=1, source_target_pairs={{0,12},{1,13},{2,14},{3,15},{4,8},{5,9},{6,10},{7,11},{8,4},{9,5},... | collective-permute-start | bytes 491528 | tf_op jit(solution)/shard_map/ppermute | solution.py:269
  58.8 2.1 %store.1 = f32[2,1,1,16,160,128]{5,4,3,2,1,0:T(8,128)} custom-call(s32[2]{0:T(128)S(1)} %pad_add_fusion.place, f32[2,2,2,160,128]{4,3,2,1,0:T(8,128)S(1)} %get-tuple-element.31.refs_0_, f32[2,2,2,160,128]{4,3,2,1,0:T(8,128)S(1)} %get-tuple-element.32.refs_1_, f32[2,2,2,160,128]{4,3,2,1,0:T(8,128)S(1)} %get-tuple-element.33.refs_2_, ...), custom_call_target="tpu_custom_call" | custom-call | bytes 2600000 | tf_op jit(solution)/shard_map/store/pallas_call | solution.py:245
  61.0 0.5 collective-permute-done.26
  61.4 3.3 %collective-permute-done.12 = f32[2,160,128]{2,1,0:T(8,128)S(1)} collective-permute-done((f32[2,160,128]{2,1,0:T(8,128)S(1)}, f32[2,160,128]{2,1,0:T(8,128)S(1)}, u32[]{:S(2)}, u32[]{:S(2)}) %collective-permute-start.12) | collective-permute-done | bytes 163872 | tf_op jit(solution)/shard_map/ppermute | solution.py:269
  64.7 0.7 %fusion.4 = f32[2,1,160,128]{3,2,1,0:T(8,128)} fusion(f32[2,160,128]{2,1,0:T(8,128)S(1)} %get-tuple-element.22, f32[2,160,128]{2,1,0:T(8,128)S(1)} %collective-permute-done.26, f32[2,2,160,128]{3,2,1,0:T(8,128)S(1)} %add_add_fusion, f32[2,160,128]{2,1,0:T(8,128)S(1)} %collective-permute-done.12, f32[2,160,128]{2,1,0:T(8,128)S(1)} %collective-permute-done.18), kind=kLoop, calls=%fused_computation.7 | loop fusion | flops 204800 | bytes 983040
  (64 shorter events, 2.2 us)
Async XLA Ops:
  0.6 15.3 %collective-permute-start.5 = (f32[2,160,128]{2,1,0:T(8,128)}, f32[2,160,128]{2,1,0:T(8,128)S(1)}, u32[]{:S(2)}, u32[]{:S(2)}) collective-permute-start(f32[2,160,128]{2,1,0:T(8,128)} %bitcast.47), channel_id=1, source_target_pairs={{0,8},{1,9},{2,10},{3,11},{4,12},{5,13},{6,14},{7,15},{8,0},{9,1},... | collective-permute-start | bytes 491528 | tf_op jit(solution)/shard_map/ppermute | solution.py:269
  4.7 11.8 %collective-permute-start.4 = (f32[2,160,128]{2,1,0:T(8,128)}, f32[2,160,128]{2,1,0:T(8,128)S(1)}, u32[]{:S(2)}, u32[]{:S(2)}) collective-permute-start(f32[2,160,128]{2,1,0:T(8,128)} %bitcast.48), channel_id=1, source_target_pairs={{0,16},{16,0},{1,17},{17,1},{2,18},{18,2},{3,19},{19,3},{4,20},{20... | collective-permute-start | bytes 491528 | tf_op jit(solution)/shard_map/ppermute | solution.py:259
  6.3 10.8 %collective-permute-start.3 = (f32[2,160,128]{2,1,0:T(8,128)}, f32[2,160,128]{2,1,0:T(8,128)S(1)}, u32[]{:S(2)}, u32[]{:S(2)}) collective-permute-start(f32[2,160,128]{2,1,0:T(8,128)} %bitcast.53), channel_id=1, source_target_pairs={{0,16},{16,0},{1,17},{17,1},{2,18},{18,2},{3,19},{19,3},{4,20},{20... | collective-permute-start | bytes 491528 | tf_op jit(solution)/shard_map/ppermute | solution.py:259
  6.8 10.3 %collective-permute-start.20 = (f32[2,160,128]{2,1,0:T(8,128)}, f32[2,160,128]{2,1,0:T(8,128)S(1)}, u32[]{:S(2)}, u32[]{:S(2)}) collective-permute-start(f32[2,160,128]{2,1,0:T(8,128)} %bitcast.49), channel_id=1, source_target_pairs={{0,4},{1,5},{2,6},{3,7},{4,0},{5,1},{6,2},{7,3},{8,12},{9,13},{10,... | collective-permute-start | bytes 491528 | tf_op jit(solution)/shard_map/ppermute | solution.py:269
  8.3 21.8 %collective-permute-start = (f32[2,160,128]{2,1,0:T(8,128)}, f32[2,160,128]{2,1,0:T(8,128)S(1)}, u32[]{:S(2)}, u32[]{:S(2)}) collective-permute-start(f32[2,160,128]{2,1,0:T(8,128)} %bitcast.50), channel_id=1, source_target_pairs={{0,2},{1,3},{2,0},{3,1},{4,6},{5,7},{6,4},{7,5},{8,10},{9,11},{10,... | collective-permute-start | bytes 491528 | tf_op jit(solution)/shard_map/ppermute | solution.py:269
  12.5 13.9 %copy-start = (bf16[768,256]{1,0:T(8,128)(2,1)S(1)}, bf16[768,256]{1,0:T(8,128)(2,1)}, u32[]{:S(2)}) copy-start(bf16[768,256]{1,0:T(8,128)(2,1)} %constant.54.clone.refs_7_) | copy-start | bytes 1179652
  12.5 13.9 %copy-start.1 = (bf16[768,256]{1,0:T(8,128)(2,1)S(1)}, bf16[768,256]{1,0:T(8,128)(2,1)}, u32[]{:S(2)}) copy-start(bf16[768,256]{1,0:T(8,128)(2,1)} %constant.57.clone.refs_10_) | copy-start | bytes 1179652
  12.5 13.9 %copy-start.3 = (bf16[160,480]{1,0:T(8,128)(2,1)S(1)}, bf16[160,480]{1,0:T(8,128)(2,1)}, u32[]{:S(2)}) copy-start(bf16[160,480]{1,0:T(8,128)(2,1)} %constant.55.clone.refs_8_) | copy-start | bytes 460804
  12.6 13.9 %copy-start.4 = (bf16[160,480]{1,0:T(8,128)(2,1)S(1)}, bf16[160,480]{1,0:T(8,128)(2,1)}, u32[]{:S(2)}) copy-start(bf16[160,480]{1,0:T(8,128)(2,1)} %constant.56.clone.refs_9_) | copy-start | bytes 460804
  12.6 13.8 %copy-start.5 = (bf16[160,480]{1,0:T(8,128)(2,1)S(1)}, bf16[160,480]{1,0:T(8,128)(2,1)}, u32[]{:S(2)}) copy-start(bf16[160,480]{1,0:T(8,128)(2,1)} %constant.58.clone.refs_11_) | copy-start | bytes 460804
  16.0 9.4 %collective-permute-start.6 = (f32[2,160,128]{2,1,0:T(8,128)S(1)}, f32[2,160,128]{2,1,0:T(8,128)S(1)}, u32[]{:S(2)}, u32[]{:S(2)}) collective-permute-start(f32[2,160,128]{2,1,0:T(8,128)S(1)} %collective-permute-done.5.refs_0_), channel_id=1, source_target_pairs={{0,4},{1,5},{2,6},{3,7},{4,0},{5,1},{6,2},{7,3},{8,12},{9,13},{10,... | collective-permute-start | bytes 491528 | tf_op jit(solution)/shard_map/ppermute | solution.py:269
  16.5 7.0 %collective-permute-start.13 = (f32[2,160,128]{2,1,0:T(8,128)S(1)}, f32[2,160,128]{2,1,0:T(8,128)S(1)}, u32[]{:S(2)}, u32[]{:S(2)}) collective-permute-start(f32[2,160,128]{2,1,0:T(8,128)S(1)} %collective-permute-done.5.refs_0_), channel_id=1, source_target_pairs={{0,2},{1,3},{2,0},{3,1},{4,6},{5,7},{6,4},{7,5},{8,10},{9,11},{10,... | collective-permute-start | bytes 491528 | tf_op jit(solution)/shard_map/ppermute | solution.py:269
  17.0 8.8 %collective-permute-start.14 = (f32[2,160,128]{2,1,0:T(8,128)S(1)}, f32[2,160,128]{2,1,0:T(8,128)S(1)}, u32[]{:S(2)}, u32[]{:S(2)}) collective-permute-start(f32[2,160,128]{2,1,0:T(8,128)S(1)} %collective-permute-done.5.refs_0_), channel_id=1, source_target_pairs={{0,1},{1,0},{2,3},{3,2},{4,5},{5,4},{6,7},{7,6},{8,9},{9,8},{10,11... | collective-permute-start | bytes 491528 | tf_op jit(solution)/shard_map/ppermute | solution.py:269
  17.0 8.3 %collective-permute-start.21 = (f32[2,160,128]{2,1,0:T(8,128)S(1)}, f32[2,160,128]{2,1,0:T(8,128)S(1)}, u32[]{:S(2)}, u32[]{:S(2)}) collective-permute-start(f32[2,160,128]{2,1,0:T(8,128)S(1)} %collective-permute-done.20.refs_0_), channel_id=1, source_target_pairs={{0,2},{1,3},{2,0},{3,1},{4,6},{5,7},{6,4},{7,5},{8,10},{9,11},{10,... | collective-permute-start | bytes 491528 | tf_op jit(solution)/shard_map/ppermute | solution.py:269
  23.5 2.9 %collective-permute-start.15 = (f32[2,160,128]{2,1,0:T(8,128)S(1)}, f32[2,160,128]{2,1,0:T(8,128)S(1)}, u32[]{:S(2)}, u32[]{:S(2)}) collective-permute-start(f32[2,160,128]{2,1,0:T(8,128)S(1)} %collective-permute-done.13.refs_1_), channel_id=1, source_target_pairs={{0,1},{1,0},{2,3},{3,2},{4,5},{5,4},{6,7},{7,6},{8,9},{9,8},{10,11... | collective-permute-start | bytes 491528 | tf_op jit(solution)/shard_map/ppermute | solution.py:269
  25.3 5.3 %collective-permute-start.22 = (f32[2,160,128]{2,1,0:T(8,128)S(1)}, f32[2,160,128]{2,1,0:T(8,128)S(1)}, u32[]{:S(2)}, u32[]{:S(2)}) collective-permute-start(f32[2,160,128]{2,1,0:T(8,128)S(1)} %collective-permute-done.20.refs_0_), channel_id=1, source_target_pairs={{0,1},{1,0},{2,3},{3,2},{4,5},{5,4},{6,7},{7,6},{8,9},{9,8},{10,11... | collective-permute-start | bytes 491528 | tf_op jit(solution)/shard_map/ppermute | solution.py:269
  25.3 5.4 %collective-permute-start.23 = (f32[2,160,128]{2,1,0:T(8,128)S(1)}, f32[2,160,128]{2,1,0:T(8,128)S(1)}, u32[]{:S(2)}, u32[]{:S(2)}) collective-permute-start(f32[2,160,128]{2,1,0:T(8,128)S(1)} %collective-permute-done.21.refs_1_), channel_id=1, source_target_pairs={{0,1},{1,0},{2,3},{3,2},{4,5},{5,4},{6,7},{7,6},{8,9},{9,8},{10,11... | collective-permute-start | bytes 491528 | tf_op jit(solution)/shard_map/ppermute | solution.py:269
  25.8 8.2 %collective-permute-start.7 = (f32[2,160,128]{2,1,0:T(8,128)S(1)}, f32[2,160,128]{2,1,0:T(8,128)S(1)}, u32[]{:S(2)}, u32[]{:S(2)}) collective-permute-start(f32[2,160,128]{2,1,0:T(8,128)S(1)} %collective-permute-done.6.refs_0_), channel_id=1, source_target_pairs={{0,2},{1,3},{2,0},{3,1},{4,6},{5,7},{6,4},{7,5},{8,10},{9,11},{10,... | collective-permute-start | bytes 491528 | tf_op jit(solution)/shard_map/ppermute | solution.py:269
  29.4 4.8 %collective-permute-start.16 = (f32[2,2,160,128]{3,2,1,0:T(8,128)S(1)}, f32[2,2,160,128]{3,2,1,0:T(8,128)S(1)}, u32[]{:S(2)}, u32[]{:S(2)}) collective-permute-start(f32[2,2,160,128]{3,2,1,0:T(8,128)S(1)} %get-tuple-element.26), channel_id=1, source_target_pairs={{0,1},{1,0},{2,3},{3,2},{4,5},{5,4},{6,7},{7,6},{8,9},{9,8},{10,11... | collective-permute-start | bytes 983048 | tf_op jit(solution)/shard_map/ppermute | solution.py:269
  30.2 9.1 %collective-permute-start.1 = (f32[2,160,128]{2,1,0:T(8,128)S(1)}, f32[2,160,128]{2,1,0:T(8,128)S(1)}, u32[]{:S(2)}, u32[]{:S(2)}) collective-permute-start(f32[2,160,128]{2,1,0:T(8,128)S(1)} %bitcast.51), channel_id=1, source_target_pairs={{0,1},{1,0},{2,3},{3,2},{4,5},{5,4},{6,7},{7,6},{8,9},{9,8},{10,11... | collective-permute-start | bytes 491528 | tf_op jit(solution)/shard_map/ppermute | solution.py:269
  30.6 8.6 %collective-permute-start.2 = (f32[2,160,128]{2,1,0:T(8,128)S(1)}, f32[2,160,128]{2,1,0:T(8,128)S(1)}, u32[]{:S(2)}, u32[]{:S(2)}) collective-permute-start(f32[2,160,128]{2,1,0:T(8,128)S(1)} %collective-permute-done.refs_1_), channel_id=1, source_target_pairs={{0,1},{1,0},{2,3},{3,2},{4,5},{5,4},{6,7},{7,6},{8,9},{9,8},{10,11... | collective-permute-start | bytes 491528 | tf_op jit(solution)/shard_map/ppermute | solution.py:269
  30.7 4.0 %collective-permute-start.8 = (f32[2,160,128]{2,1,0:T(8,128)S(1)}, f32[2,160,128]{2,1,0:T(8,128)S(1)}, u32[]{:S(2)}, u32[]{:S(2)}) collective-permute-start(f32[2,160,128]{2,1,0:T(8,128)S(1)} %collective-permute-done.6.refs_0_), channel_id=1, source_target_pairs={{0,1},{1,0},{2,3},{3,2},{4,5},{5,4},{6,7},{7,6},{8,9},{9,8},{10,11... | collective-permute-start | bytes 491528 | tf_op jit(solution)/shard_map/ppermute | solution.py:269
  34.1 8.6 %collective-permute-start.24 = (f32[2,2,160,128]{3,2,1,0:T(8,128)S(1)}, f32[2,2,160,128]{3,2,1,0:T(8,128)S(1)}, u32[]{:S(2)}, u32[]{:S(2)}) collective-permute-start(f32[2,2,160,128]{3,2,1,0:T(8,128)S(1)} %get-tuple-element.30), channel_id=1, source_target_pairs={{0,1},{1,0},{2,3},{3,2},{4,5},{5,4},{6,7},{7,6},{8,9},{9,8},{10,11... | collective-permute-start | bytes 983048 | tf_op jit(solution)/shard_map/ppermute | solution.py:269
  34.2 2.1 %collective-permute-start.9 = (f32[2,160,128]{2,1,0:T(8,128)S(1)}, f32[2,160,128]{2,1,0:T(8,128)S(1)}, u32[]{:S(2)}, u32[]{:S(2)}) collective-permute-start(f32[2,160,128]{2,1,0:T(8,128)S(1)} %collective-permute-done.7.refs_1_), channel_id=1, source_target_pairs={{0,1},{1,0},{2,3},{3,2},{4,5},{5,4},{6,7},{7,6},{8,9},{9,8},{10,11... | collective-permute-start | bytes 491528 | tf_op jit(solution)/shard_map/ppermute | solution.py:269
  34.7 9.7 %collective-permute-start.17 = (f32[2,160,128]{2,1,0:T(8,128)S(1)}, f32[2,160,128]{2,1,0:T(8,128)S(1)}, u32[]{:S(2)}, u32[]{:S(2)}) collective-permute-start(f32[2,160,128]{2,1,0:T(8,128)S(1)} %slice_bitcast_fusion.2), channel_id=1, source_target_pairs={{0,2},{1,3},{2,0},{3,1},{4,6},{5,7},{6,4},{7,5},{8,10},{9,11},{10,... | collective-permute-start | bytes 491528 | tf_op jit(solution)/shard_map/ppermute | solution.py:269
  39.1 5.7 %collective-permute-start.10 = (f32[2,2,160,128]{3,2,1,0:T(8,128)S(1)}, f32[2,2,160,128]{3,2,1,0:T(8,128)S(1)}, u32[]{:S(2)}, u32[]{:S(2)}) collective-permute-start(f32[2,2,160,128]{3,2,1,0:T(8,128)S(1)} %get-tuple-element.24), channel_id=1, source_target_pairs={{0,1},{1,0},{2,3},{3,2},{4,5},{5,4},{6,7},{7,6},{8,9},{9,8},{10,11... | collective-permute-start | bytes 983048 | tf_op jit(solution)/shard_map/ppermute | solution.py:269
  42.1 4.0 %collective-permute-start.19 = (f32[2,2,160,128]{3,2,1,0:T(8,128)S(1)}, f32[2,2,160,128]{3,2,1,0:T(8,128)S(1)}, u32[]{:S(2)}, u32[]{:S(2)}) collective-permute-start(f32[2,2,160,128]{3,2,1,0:T(8,128)S(1)} %get-tuple-element.28), channel_id=1, source_target_pairs={{0,1},{1,0},{2,3},{3,2},{4,5},{5,4},{6,7},{7,6},{8,9},{9,8},{10,11... | collective-permute-start | bytes 983048 | tf_op jit(solution)/shard_map/ppermute | solution.py:269
  42.7 13.2 %collective-permute-start.25 = (f32[2,2,160,128]{3,2,1,0:T(8,128)S(1)}, f32[2,2,160,128]{3,2,1,0:T(8,128)S(1)}, u32[]{:S(2)}, u32[]{:S(2)}) collective-permute-start(f32[2,2,160,128]{3,2,1,0:T(8,128)S(1)} %add.60), channel_id=1, source_target_pairs={{0,4},{1,5},{2,6},{3,7},{4,0},{5,1},{6,2},{7,3},{8,12},{9,13},{10,... | collective-permute-start | bytes 983048 | tf_op jit(solution)/shard_map/ppermute | solution.py:269
  44.4 16.5 %collective-permute-start.18 = (f32[2,160,128]{2,1,0:T(8,128)S(1)}, f32[2,160,128]{2,1,0:T(8,128)S(1)}, u32[]{:S(2)}, u32[]{:S(2)}) collective-permute-start(f32[2,160,128]{2,1,0:T(8,128)S(1)} %fusion.5), channel_id=1, source_target_pairs={{0,8},{1,9},{2,10},{3,11},{4,12},{5,13},{6,14},{7,15},{8,0},{9,1},... | collective-permute-start | bytes 491528 | tf_op jit(solution)/shard_map/ppermute | solution.py:269
  44.9 12.5 %collective-permute-start.11 = (f32[2,160,128]{2,1,0:T(8,128)S(1)}, f32[2,160,128]{2,1,0:T(8,128)S(1)}, u32[]{:S(2)}, u32[]{:S(2)}) collective-permute-start(f32[2,160,128]{2,1,0:T(8,128)S(1)} %slice_bitcast_fusion.4), channel_id=1, source_target_pairs={{0,2},{1,3},{2,0},{3,1},{4,6},{5,7},{6,4},{7,5},{8,10},{9,11},{10,... | collective-permute-start | bytes 491528 | tf_op jit(solution)/shard_map/ppermute | solution.py:269
  56.0 5.4 %collective-permute-start.26 = (f32[2,160,128]{2,1,0:T(8,128)S(1)}, f32[2,160,128]{2,1,0:T(8,128)S(1)}, u32[]{:S(2)}, u32[]{:S(2)}) collective-permute-start(f32[2,160,128]{2,1,0:T(8,128)S(1)} %slice_bitcast_fusion), channel_id=1, source_target_pairs={{0,2},{1,3},{2,0},{3,1},{4,6},{5,7},{6,4},{7,5},{8,10},{9,11},{10,... | collective-permute-start | bytes 491528 | tf_op jit(solution)/shard_map/ppermute | solution.py:269
  57.4 7.2 %collective-permute-start.12 = (f32[2,160,128]{2,1,0:T(8,128)S(1)}, f32[2,160,128]{2,1,0:T(8,128)S(1)}, u32[]{:S(2)}, u32[]{:S(2)}) collective-permute-start(f32[2,160,128]{2,1,0:T(8,128)S(1)} %fusion.6), channel_id=1, source_target_pairs={{0,12},{1,13},{2,14},{3,15},{4,8},{5,9},{6,10},{7,11},{8,4},{9,5},... | collective-permute-start | bytes 491528 | tf_op jit(solution)/shard_map/ppermute | solution.py:269
  (6 other events, 31.6 us)

commit v3 on v0

--- a/solution.py
+++ b/solution.py
@@ -1,14 +1,379 @@
+import functools
 import math
 
 import jax
 import jax.numpy as jnp
+import ml_dtypes
+import numpy as np
 from jax import lax
+from jax.experimental import pallas as pl
+from jax.experimental.pallas import tpu as pltpu
 from jax.sharding import PartitionSpec as P
 
 dual_step = 0.4
 primal_step = 0.4
 clip_level = 0.5
-highest = lax.Precision.HIGHEST
+
+
+def split_host(table):
+    high = table.astype(ml_dtypes.bfloat16)
+    low = (table - high.astype(np.float64)).astype(ml_dtypes.bfloat16)
+    return high, low
+
+
+def column_table(length, sign):
+    places = np.arange(length)
+    angles = 2.0 * math.pi * (np.outer(places, places) % length) / length
+    real = np.cos(angles) / math.sqrt(length)
+    imag = sign * np.sin(angles) / math.sqrt(length)
+    whole = np.block([[real, imag], [-imag, real]])
+    high, low = split_host(whole)
+    return np.concatenate([high, high, low], axis=0)
+
+
+def row_tables(length, sign):
+    half = length // 2
+    found = []
+    for odd in (0, 1):
+        lines = np.arange(half)
+        cells = 2 * np.arange(half) + odd
+        product = np.outer(lines, cells)
+        angles = 2.0 * math.pi * (product % length) / length
+        real = np.cos(angles) / math.sqrt(length)
+        imag = sign * np.sin(angles) / math.sqrt(length)
+        if sign > 0:
+            real, imag = real.T, imag.T
+        whole = np.block([[real, -imag], [imag, real]])
+        high, low = split_host(whole)
+        found.append(np.concatenate([high, high, low], axis=1))
+    return found
+
+
+def split(values):
+    high = values.astype(jnp.bfloat16)
+    low = (values - high.astype(jnp.float32)).astype(jnp.bfloat16)
+    return high, low
+
+
+def columns_dft(real, imag, table):
+    real_high, real_low = split(real)
+    imag_high, imag_low = split(imag)
+    left = jnp.concatenate([real_high, imag_high, real_low, imag_low, real_high, imag_high], axis=1)
+    return jnp.dot(left, table, preferred_element_type=jnp.float32)
+
+
+def rows_dft(table, values):
+    high, low = split(values)
+    return jnp.dot(table, jnp.concatenate([high, low, high], axis=0), preferred_element_type=jnp.float32)
+
+
+vmem = pl.BlockSpec(memory_space=pltpu.VMEM)
+hbm = pl.BlockSpec(memory_space=pltpu.HBM)
+anywhere = pl.BlockSpec(memory_space=pl.ANY)
+mebi = 1024 * 1024
+
+
+def call(name, kernel, held, far, passed, outs, scratch, work, limit, shared=None):
+    operands = [
+        *[pltpu.with_memory_space_constraint(value, pltpu.VMEM) for value in held],
+        *[pltpu.with_memory_space_constraint(value, pltpu.HBM) for value in far],
+    ]
+    aliases = {len(operands) + n: len(outs) + n for n in range(len(passed))}
+    if shared is not None:
+        aliases[shared] = len(outs) - 1
+    found = pl.pallas_call(
+        functools.partial(kernel, len(held), len(far), len(passed), len(outs)),
+        out_shape=list(outs) + [jax.ShapeDtypeStruct(value.shape, value.dtype) for value in passed],
+        in_specs=[vmem] * len(held) + [hbm] * len(far) + [anywhere] * len(passed),
+        out_specs=[vmem] * len(outs) + [anywhere] * len(passed),
+        scratch_shapes=scratch,
+        input_output_aliases=aliases,
+        compiler_params=pltpu.CompilerParams(vmem_limit_bytes=limit * mebi),
+        cost_estimate=pl.CostEstimate(flops=work * 1_000, bytes_accessed=100, transcendentals=0),
+        name=name,
+    )(*operands, *passed)
+    return found[:len(outs)], found[len(outs):]
+
+
+def sorted_refs(held, far, passed, outs, refs):
+    after = held + far + passed
+    return refs[:held], refs[held:held + far], refs[after:after + outs], refs[after + outs + passed:]
+
+
+def placed():
+    here = lax.axis_index("space")
+    return here // 2, here % 2, lax.axis_index("tm")
+
+
+def load_kernel(held, far, passed, outs, *refs):
+    _, sources, targets, (ksp_buf, mask_buf, sems, small_sems) = sorted_refs(held, far, passed, outs, refs)
+    tables = far - 7
+    image, extrap, tv_dual, mask, coil, dual, kspace = sources[tables:]
+    token, weight, image_out, here, pair, near, give = targets[tables:]
+    token[...] = jnp.zeros(token.shape, token.dtype)
+    copies = [
+        pltpu.make_async_copy(mask, mask_buf, small_sems.at[tables]),
+        pltpu.make_async_copy(image.at[:, 0], image_out, small_sems.at[tables + 1]),
+        pltpu.make_async_copy(extrap.at[:, 0], here, small_sems.at[tables + 2]),
+        pltpu.make_async_copy(extrap.at[:, 0], pair.at[0:2], small_sems.at[tables + 3]),
+        pltpu.make_async_copy(tv_dual.at[:, 0], pair.at[2:4], small_sems.at[tables + 4]),
+    ]
+    copies += [pltpu.make_async_copy(sources[n], targets[n], small_sems.at[n]) for n in range(tables)]
+    _, chips, _, height, _ = near.shape
+    place = placed()
+    loads = []
+    for other, target in enumerate((near, give)):
+        for offset in range(chips):
+            plane = 2 * jnp.bitwise_xor(place[0], offset) + jnp.bitwise_xor(place[1], other)
+            rows = pl.ds(pl.multiple_of(plane * height, height), height)
+            loads.append([
+                pltpu.make_async_copy(dual.at[:, 0, 0, plane], target.at[1, offset], sems.at[other, offset, 0]),
+                pltpu.make_async_copy(kspace.at[:, 0, 0, plane], ksp_buf.at[other, offset], sems.at[other, offset, 1]),
+                pltpu.make_async_copy(coil.at[:, 0, rows, :], target.at[0, offset], sems.at[other, offset, 2]),
+            ])
+    for load in loads:
+        for copy in load:
+            copy.start()
+    for copy in copies:
+        copy.start()
+    for other, target in enumerate((near, give)):
+        for offset in range(chips):
+            for copy in loads[other * chips + offset]:
+                copy.wait()
+            for part in (0, 1):
+                target[1, offset, part] = target[1, offset, part] - dual_step * ksp_buf[other, offset, part]
+    for copy in copies:
+        copy.wait()
+    weight[...] = mask_buf[0].astype(jnp.float32) / (1.0 + dual_step)
+
+
+def coil_kernel(first, held, far, passed, outs, *refs):
+    values, _, targets, (u_buf, v_buf) = sorted_refs(held, far, passed, outs, refs)
+    count = outs - 2
+    blocks, sides = values[:count], values[count:count + 2]
+    weight, col_fwd, even_fwd, odd_fwd, col_bwd, even_bwd, odd_bwd = values[count + 2:count + 9]
+    totals, (new_own, new_all) = targets[:count], targets[count:]
+    new_other = new_all.at[first:first + count]
+    height, depth = weight.shape
+    half = height // 2
+    for n in range(count):
+
+        def maps():
+            return [(side[0, first + n, 0], side[0, first + n, 1]) for side in sides]
+
+        image_re, image_im = blocks[n][0], blocks[n][1]
+        real, imag = [], []
+        for map_re, map_im in maps():
+            real.append(map_re * image_re - map_im * image_im)
+            imag.append(map_re * image_im + map_im * image_re)
+        lines = columns_dft(jnp.concatenate(real, axis=0), jnp.concatenate(imag, axis=0), col_fwd[...])
+        u_buf[0] = lines[:, :depth]
+        u_buf[1] = lines[:, depth:]
+        halves = []
+        for odd, table in ((0, even_fwd), (1, odd_fwd)):
+            cells = jnp.concatenate([
+                jnp.concatenate([u_buf[part, pl.ds(c * height + odd, half, stride=2), :] for part in (0, 1)], axis=0)
+                for c in (0, 1)
+            ], axis=1)
+            halves.append(rows_dft(table[...], cells))
+        spectrum = (halves[0] + halves[1], halves[0] - halves[1])
+        updated = []
+        for q in (0, 1):
+            span = pl.ds(q * half, half)
+            columns = []
+            for c, new in enumerate((new_own, new_other)):
+                pieces = []
+                for part in (0, 1):
+                    value = spectrum[q][part * half:(part + 1) * half, c * depth:(c + 1) * depth]
+                    piece = weight[span, :] * (sides[c][1, first + n, part, span, :] + dual_step * value)
+                    new[n, part, span, :] = piece
+                    pieces.append(piece)
+                columns.append(jnp.concatenate(pieces, axis=0))
+            updated.append(jnp.concatenate(columns, axis=1))
+        for odd, table in ((0, even_bwd), (1, odd_bwd)):
+            back = rows_dft(table[...], updated[0] - updated[1] if odd else updated[0] + updated[1])
+            for c in (0, 1):
+                for part in (0, 1):
+                    v_buf[part, pl.ds(c * height + odd, half, stride=2), :] = back[
+                        part * half:(part + 1) * half, c * depth:(c + 1) * depth
+                    ]
+        back = columns_dft(v_buf[0], v_buf[1], col_bwd[...])
+        total_re, total_im = 0.0, 0.0
+        for c, (map_re, map_im) in enumerate(maps()):
+            back_re = back[c * height:(c + 1) * height, :depth]
+            back_im = back[c * height:(c + 1) * height, depth:]
+            total_re = total_re + map_re * back_re + map_im * back_im
+            total_im = total_im + map_re * back_im - map_im * back_re
+        totals[n][0] = total_re
+        totals[n][1] = total_im
+
+
+def project(moved):
+    magnitude = jnp.sqrt(moved[0] * moved[0] + moved[1] * moved[1])
+    factor = clip_level / jnp.maximum(magnitude, clip_level)
+    return [value * factor for value in moved]
+
+
+def temporal_kernel(total, held, far, passed, outs, *refs):
+    (image, pair, pair_before, *others), _, (tv_new, begin), _ = sorted_refs(held, far, passed, outs, refs)
+    current, dual = pair.at[0:2], pair.at[2:4]
+    previous, dual_before = pair_before.at[0:2], pair_before.at[2:4]
+    later = others[0] if others else previous
+    place = placed()
+    not_first = jnp.where(place[2] > 0, 1.0, 0.0)
+    not_last = jnp.where(place[2] < total - 1, 1.0, 0.0)
+    own = project([
+        dual[part] + (dual_step * not_last) * (later[part] - current[part]) for part in (0, 1)
+    ])
+    earlier = project([
+        dual_before[part] + dual_step * (current[part] - previous[part]) for part in (0, 1)
+    ])
+    for part in (0, 1):
+        tv_new[part] = own[part]
+        begin[part] = image[part] - primal_step * (not_first * earlier[part] - not_last * own[part])
+
+
+def pass_kernel(held, far, passed, outs, *refs):
+    pass
+
+
+def sum_kernel(begun, held, far, passed, outs, *refs):
+    values, _, (target,), _ = sorted_refs(held, far, passed, outs, refs)
+    for part in (0, 1):
+        total = 0.0
+        for value in values[:held - begun]:
+            total = total + value[part]
+        target[part] = values[-1][part] - primal_step * total if begun else total
+
+
+def store_kernel(*refs):
+    groups, new_other, _, data_new, sems = refs[:-4], *refs[-4:]
+    place = placed()
+    count = groups[0].shape[0]
+    stores = []
+    for offset in range(new_other.shape[0]):
+        for other, source in enumerate((groups[offset // count].at[offset % count], new_other.at[offset])):
+            plane = 2 * jnp.bitwise_xor(place[0], offset) + jnp.bitwise_xor(place[1], other)
+            stores.append(pltpu.make_async_copy(source, data_new.at[:, 0, 0, plane], sems.at[other, offset]))
+            stores[-1].start()
+    for store in stores:
+        store.wait()
+
+
+def turned(value, axis, steps):
+    count = lax.axis_size(axis)
+    return lax.ppermute(value, axis, [(source, (source + steps) % count) for source in range(count)])
+
+
+def swapped(value, mask):
+    count = lax.axis_size("space")
+    return lax.ppermute(value, "space", [(source, source ^ mask) for source in range(count)])
+
+
+def on_device(image, extrap, tv_dual, data_dual, kspace, coil_maps, sampling):
+    height, depth = kspace.shape[4:]
+    chips = lax.axis_size("space") // 2
+    inner = chips // 4
+    frame_total = lax.axis_size("tm")
+    tables = [
+        jnp.asarray(table)
+        for table in (
+            column_table(depth, -1), *row_tables(height, -1), column_table(depth, 1), *row_tables(height, 1)
+        )
+    ]
+    block = pltpu.VMEM((2, height, depth), jnp.float32)
+    result = jax.ShapeDtypeStruct((2, height, depth), jnp.float32)
+
+    def ahead(work, token, *values):
+        _, (token, *values) = call("ahead", pass_kernel, [], [], [token, *values], [], [], work, 2)
+        return (token, *values)
+
+    blocks = {i: swapped(extrap[:, 0], 2 * i) for i in range(1, inner + 1)}
+    blocks[2 * inner] = swapped(extrap[:, 0], 4 * inner)
+
+    half = pltpu.VMEM((2, chips, 2, height, depth), jnp.float32)
+    (*tables, token, weight, image_here, blocks[0], pair, near, give), _ = call(
+        "load", load_kernel, [], [*tables, image, extrap, tv_dual, sampling, coil_maps, data_dual, kspace], [],
+        [pltpu.VMEM(value.shape, value.dtype) for value in tables]
+        + [pltpu.VMEM((8, 128), jnp.float32), pltpu.VMEM((height, depth), jnp.float32)]
+        + [block, block, pltpu.VMEM((4, height, depth), jnp.float32), half, half],
+        [
+            pltpu.VMEM((2, chips, 2, height, depth), jnp.float32),
+            pltpu.VMEM((1, height, depth), jnp.int32),
+            pltpu.SemaphoreType.DMA((2, chips, 3)),
+            pltpu.SemaphoreType.DMA((len(tables) + 5,)),
+        ],
+        1, 4,
+    )
+    other = swapped(give, 1)
+    pair_before = turned(pair, "tm", 1)
+    later = [] if frame_total == 2 else [turned(blocks[0], "tm", -1)]
+
+    totals, new_own = {}, {}
+
+    def coils(z, token, new_other):
+        held = [blocks[z * inner + i] for i in range(inner)] + [near, other, weight, *tables]
+        found, (token,) = call(
+            "coils", functools.partial(coil_kernel, z * inner), held + new_other, [], [token],
+            [block] * inner + [
+                pltpu.VMEM((inner, 2, height, depth), jnp.float32), pltpu.VMEM((chips, 2, height, depth), jnp.float32)
+            ],
+            [pltpu.VMEM((2, 2 * height, depth), jnp.float32)] * 2,
+            100_000, 8, len(held) if new_other else None,
+        )
+        totals[z], new_own[z] = found[:inner], found[inner]
+        arrived[z] = [swapped(totals[z][i], 2 * i) for i in range(1, inner)]
+        return token, [found[inner + 1]]
+
+    def onward(z, token):
+        (found,), (token,) = call(
+            "sums", functools.partial(sum_kernel, 0), [totals[z][0], *arrived[z]], [], [token], [block], [],
+            50, 2,
+        )
+        return found, token
+
+    arrived, parts = {}, {}
+    token, *found = ahead(30_000_000, token, *[blocks[i] for i in range(1, inner + 1)], blocks[2 * inner])
+    blocks.update(zip([*range(1, inner + 1), 2 * inner], found))
+    blocks[3 * inner] = swapped(blocks[2 * inner], 2 * inner)
+    for z in (1, 2):
+        for i in range(1, inner):
+            blocks[z * inner + i] = swapped(blocks[z * inner], 2 * i)
+    token, new_other = coils(0, token, [])
+    token, blocks[3 * inner] = ahead(1, token, blocks[3 * inner])
+    for i in range(1, inner):
+        blocks[3 * inner + i] = swapped(blocks[3 * inner], 2 * i)
+    for z in (2, 1, 3):
+        token, new_other = coils(z, token, new_other)
+    parts[2], token = onward(2, token)
+    (tv_here, begin), (token,) = call(
+        "temporal", functools.partial(temporal_kernel, frame_total), [image_here, pair, pair_before, *later], [], [token],
+        [result, block], [], 50, 4,
+    )
+    for z in (1, 3):
+        parts[z], token = onward(z, token)
+    parts = [swapped(parts[z], 2 * z * inner) for z in (1, 2, 3)]
+    new_other = swapped(new_other[0], 1)
+    (begin,), (token,) = call(
+        "sums", functools.partial(sum_kernel, 1), [totals[0][0], *parts[:2], begin], [], [token], [block], [],
+        20_000_000, 2,
+    )
+    (image_new,), _ = call(
+        "sums", functools.partial(sum_kernel, 1), [*arrived[0], parts[2], begin], [], [], [result], [], 1, 2,
+    )
+
+    groups = [new_own[z] for z in range(4)] + [new_other, token]
+    data_new = pl.pallas_call(
+        store_kernel,
+        out_shape=jax.ShapeDtypeStruct(kspace.shape, jnp.float32),
+        in_specs=[vmem] * len(groups),
+        out_specs=hbm,
+        scratch_shapes=[pltpu.SemaphoreType.DMA((2, chips))],
+        compiler_params=pltpu.CompilerParams(vmem_limit_bytes=2 * mebi),
+        cost_estimate=pl.CostEstimate(flops=1_000, bytes_accessed=100, transcendentals=0),
+        name="store",
+    )(*groups)
+    return (image_new[:, None], tv_here[:, None], data_new)
 
 
 def passed_along(value, axis, steps):
@@ -17,7 +382,7 @@
     return lax.ppermute(value, axis, [(source, source + steps) for source in range(initial, last)])
 
 
-def tables(length):
+def plain_tables(length):
     places = lax.iota(jnp.int32, length)
     product = places[:, None] * places[None, :] % length
     angles = product.astype(jnp.float32) * (2.0 * math.pi / length)
@@ -25,37 +390,31 @@
     return (jnp.cos(angles) * factor, jnp.sin(angles) * factor)
 
 
-def project(real_part, imag_part):
-    magnitude = jnp.sqrt(real_part * real_part + imag_part * imag_part)
-    factor = clip_level / jnp.maximum(magnitude, clip_level)
-    return (real_part * factor, imag_part * factor)
-
-
 def right_mult(values, table):
-    return jnp.dot(values, table, precision=highest, preferred_element_type=jnp.float32)
+    return jnp.dot(values, table, precision=lax.Precision.HIGHEST, preferred_element_type=jnp.float32)
 
 
 def left_mult(table, values):
     return jnp.einsum(
-        "ky,cxyz->cxkz", table, values, precision=highest, preferred_element_type=jnp.float32
-    )
-
-
-def on_device(image, extrap, tv_dual, data_dual, kspace, coil_maps, sampling):
+        "ky,cxyz->cxkz", table, values, precision=lax.Precision.HIGHEST, preferred_element_type=jnp.float32
+    )
+
+
+def on_any(image, extrap, tv_dual, data_dual, kspace, coil_maps, sampling):
     readout = kspace.shape[3]
     height = kspace.shape[4]
     depth = kspace.shape[5]
     coil_count = kspace.shape[2]
     own_rows = image.shape[2]
-    cos_cols, sin_cols = tables(depth)
-    cos_rows, sin_rows = tables(height)
+    cos_cols, sin_cols = plain_tables(depth)
+    cos_rows, sin_rows = plain_tables(height)
     frame_here = lax.axis_index("tm")
     frame_total = lax.axis_size("tm")
     not_last = (frame_here < frame_total - 1).astype(jnp.float32)
     current = extrap[:, 0]
     later = passed_along(current, "tm", -1)
     moved = tv_dual[:, 0] + dual_step * not_last * (later - current)
-    tv_real, tv_imag = project(moved[0], moved[1])
+    tv_real, tv_imag = project(moved)
     tv_here = jnp.stack([tv_real, tv_imag])
     piece = lax.all_gather(current, "space", axis=1, tiled=True)
     piece_real = piece[0][None]
@@ -105,6 +464,13 @@
         P(None, "tm", "space", None),
         P(None, "tm", "space", None, None, None),
     )
+
+    def either(*local):
+        kspace = local[4]
+        one_plane = local[0].shape[2] == kspace.shape[4] and mesh.shape["space"] == kspace.shape[3]
+        paired = mesh.shape["space"] % 8 == 0 and mesh.shape["space"] & (mesh.shape["space"] - 1) == 0
+        return (on_device if one_plane and paired else on_any)(*local)
+
     return jax.shard_map(
-        on_device, mesh=mesh, in_specs=in_specs, out_specs=out_specs, check_vma=False
-    )
+        either, mesh=mesh, in_specs=in_specs, out_specs=out_specs, check_vma=False
+    )

time: 198 us -> 51.8 us (0.26)
  waiting for transfers between devices: 142 us -> 12.8 us
  matrix products: 28.5 us -> 0 us
  starting transfers between devices: 2.81 us -> 20.2 us
  Pallas kernels: 0 us -> 17.2 us
  between operations: 14.3 us -> 0.76 us
  other arithmetic: 8.8 us -> 0 us
    psum x1 -> x0, waiting for transfers between devices: 85.5 us -> none  [on_device(): combined = lax.psum(coil_term, 'space')]
    all_gather x1 -> x0, waiting for transfers between devices: 47.4 us -> none  [on_device(): piece = lax.all_gather(current, 'space', axis=1, tiled=True)]
    dot_general x16 -> x0, matrix products: 28.5 us -> none  [the longest x8 16.3 us: left_mult(): jnp.einsum('ky,cxyz->cxkz', table, values, precision=highest, preferred_e...]
    ppermute x2 -> x17, starting transfers between devices: 2.74 us -> 20.2 us  [the longest x16 18.7 us: swapped(): lax.ppermute(value, 'space', [(source, source ^ mask) for source in range...]
    pallas_call x0 -> x14, Pallas kernels: none -> 17.2 us  [the longest x13 15.6 us: call(): pl.pallas_call(functools.partial(kernel, len(held), len(far), len(passed)...]
    ppermute x2 -> x17, waiting for transfers between devices: 8.51 us -> 12.8 us  [the longest x16 12.8 us: swapped(): lax.ppermute(value, 'space', [(source, source ^ mask) for source in range...]
    unnamed x2 -> x0, other arithmetic: 3.34 us -> none
    add x2 -> x0, other arithmetic: 2.8 us -> none  [the longest x1 2.77 us: on_device(): coil_imag = coil_maps[0] * piece_imag + coil_maps[1] * piece_real]
  transfers between devices with their start and end apart: 4 -> 17, of which waited for: 4 -> 6; matrix products, arithmetic and copies ran while one was open for 1% -> 0% of each run, Pallas kernels for 0% -> 31%
where the time goes in v3:
time: 51.8 us; the launch traced here: 50.9 us
  starting transfers between devices  20.2 us (39%)
  Pallas kernels  17.2 us (33%)
  waiting for transfers between devices  12.8 us (25%)
  between operations  0.76 us (1%)
    ppermute x16, starting transfers between devices, swapped(): lax.ppermute(value, 'space', [(source, source ^ mask) for source in range...  18.7 us
    pallas_call x13, Pallas kernels, call(): pl.pallas_call(functools.partial(kernel, len(held), len(far), len(passed)...  15.6 us
    ppermute x16, waiting for transfers between devices, swapped(): lax.ppermute(value, 'space', [(source, source ^ mask) for source in range...  12.8 us
    pallas_call x1, Pallas kernels, on_device(): pl.pallas_call(store_kernel, out_shape=jax.ShapeDtypeStruct(kspace.shape,...  1.61 us
    ppermute x1, starting transfers between devices, turned(): lax.ppermute(value, axis, [(source, (source + steps) % count) for source...  1.52 us
  transfers between devices with their start and end apart: 17, of which 6 were waited for; matrix products, arithmetic and copies ran while one was open for 0% of the time, Pallas kernels for 31%

profile of v3, /device:TPU:0, one launch (start us, length us, event | category | flops | bytes accessed | tf_op | source)
XLA Modules:
  0.0 50.9 jit_solution(3380963134160333447)
XLA Ops:
  0.6 3.0 %collective-permute-start = (f32[2,160,128]{2,1,0:T(8,128)}, f32[2,160,128]{2,1,0:T(8,128)S(1)}, u32[]{:S(2)}, u32[]{:S(2)}) collective-permute-start(f32[2,160,128]{2,1,0:T(8,128)} %bitcast.8), channel_id=1, source_target_pairs={{0,2},{1,3},{2,0},{3,1},{4,6},{5,7},{6,4},{7,5},{8,10},{9,11},{10,... | collective-permute-start | bytes 491528 | tf_op jit(solution)/shard_map/ppermute | solution.py:270
  3.6 1.6 %collective-permute-start.1 = (f32[2,160,128]{2,1,0:T(8,128)}, f32[2,160,128]{2,1,0:T(8,128)S(1)}, u32[]{:S(2)}, u32[]{:S(2)}) collective-permute-start(f32[2,160,128]{2,1,0:T(8,128)} %bitcast.9), channel_id=1, source_target_pairs={{0,4},{1,5},{2,6},{3,7},{4,0},{5,1},{6,2},{7,3},{8,12},{9,13},{10,... | collective-permute-start | bytes 491528 | tf_op jit(solution)/shard_map/ppermute | solution.py:270
  5.2 2.6 %collective-permute-start.2 = (f32[2,160,128]{2,1,0:T(8,128)}, f32[2,160,128]{2,1,0:T(8,128)S(1)}, u32[]{:S(2)}, u32[]{:S(2)}) collective-permute-start(f32[2,160,128]{2,1,0:T(8,128)} %bitcast.10), channel_id=1, source_target_pairs={{0,8},{1,9},{2,10},{3,11},{4,12},{5,13},{6,14},{7,15},{8,0},{9,1},... | collective-permute-start | bytes 491528 | tf_op jit(solution)/shard_map/ppermute | solution.py:270
  7.8 4.5 %load.1 = (bf16[768,256]{1,0:T(8,128)(2,1)S(1)}, bf16[160,480]{1,0:T(8,128)(2,1)S(1)}, bf16[160,480]{1,0:T(8,128)(2,1)S(1)}, bf16[768,256]{1,0:T(8,128)(2,1)S(1)...) custom-call(bf16[768,256]{1,0:T(8,128)(2,1)} %constant.12.clone.refs, ...), custom_call_target="tpu_custom_call" | custom-call | flops 1000 | bytes 100 | tf_op jit(solution)/shard_map/load/pallas_call | solution.py:84
  12.3 0.1 collective-permute-start.3
  12.4 0.2 collective-permute-done.1.refs_2_
  12.6 2.7 %collective-permute-done.2.refs_3_ = f32[2,160,128]{2,1,0:T(8,128)S(1)} collective-permute-done((f32[2,160,128]{2,1,0:T(8,128)}, f32[2,160,128]{2,1,0:T(8,128)S(1)}, u32[]{:S(2)}, u32[]{:S(2)}) %collective-permute-start.2) | collective-permute-done | bytes 163872 | tf_op jit(solution)/shard_map/ppermute | solution.py:270
  15.3 0.4 collective-permute-start.5
  15.7 0.5 %collective-permute-start.8 = (f32[2,160,128]{2,1,0:T(8,128)S(1)}, f32[2,160,128]{2,1,0:T(8,128)S(1)}, u32[]{:S(2)}, u32[]{:S(2)}) collective-permute-start(f32[2,160,128]{2,1,0:T(8,128)S(1)} %get-tuple-element.68.refs_0_), channel_id=1, source_target_pairs={{0,2},{1,3},{2,0},{3,1},{4,6},{5,7},{6,4},{7,5},{8,10},{9,11},{10,... | collective-permute-start | bytes 491528 | tf_op jit(solution)/shard_map/ppermute | solution.py:270
  16.2 1.5 %collective-permute-start.7 = (f32[2,160,128]{2,1,0:T(8,128)S(1)}, f32[2,160,128]{2,1,0:T(8,128)S(1)}, u32[]{:S(2)}, u32[]{:S(2)}) collective-permute-start(f32[2,160,128]{2,1,0:T(8,128)S(1)} %get-tuple-element.70.refs_0_), channel_id=1, source_target_pairs={{0,2},{1,3},{2,0},{3,1},{4,6},{5,7},{6,4},{7,5},{8,10},{9,11},{10,... | collective-permute-start | bytes 491528 | tf_op jit(solution)/shard_map/ppermute | solution.py:270
  17.7 1.5 %collective-permute-start.11 = (f32[4,160,128]{2,1,0:T(8,128)S(1)}, f32[4,160,128]{2,1,0:T(8,128)S(1)}, u32[]{:S(2)}, u32[]{:S(2)}) collective-permute-start(f32[4,160,128]{2,1,0:T(8,128)S(1)} %get-tuple-element.82.refs_1_), channel_id=1, source_target_pairs={{0,16},{16,0},{1,17},{17,1},{2,18},{18,2},{3,19},{19,3},{4,20},{20... | collective-permute-start | bytes 983048 | tf_op jit(solution)/shard_map/ppermute | solution.py:265
  19.3 0.0 collective-permute-done.3.refs_3_
  19.3 2.4 %coils.4 = (f32[2,160,128]{2,1,0:T(8,128)S(1)}, f32[2,160,128]{2,1,0:T(8,128)S(1)}, f32[2,2,160,128]{3,2,1,0:T(8,128)S(1)}, f32[8,2,160,128]{3,2,1,0:T(8,128)S(1)}, f32[8,128]{1,0:T(8,128)S(1)}) custom-call(f32[2,160,128]{2,1,0:T(8,128)S(1)} %get-tuple-element.53.refs_0_, ...), custom_call_target="tpu_custom_call", output_to_operand_aliasing={{4}: (11, {})} | custom-call | flops 100000000 | bytes 100 | tf_op jit(solution)/shard_map/coils/pallas_call | solution.py:84
  21.7 0.0 collective-permute-done.5.refs_1_
  21.7 0.6 %collective-permute-start.6 = (f32[2,160,128]{2,1,0:T(8,128)S(1)}, f32[2,160,128]{2,1,0:T(8,128)S(1)}, u32[]{:S(2)}, u32[]{:S(2)}) collective-permute-start(f32[2,160,128]{2,1,0:T(8,128)S(1)} %get-tuple-element.69.refs_0_), channel_id=1, source_target_pairs={{0,2},{1,3},{2,0},{3,1},{4,6},{5,7},{6,4},{7,5},{8,10},{9,11},{10,... | collective-permute-start | bytes 491528 | tf_op jit(solution)/shard_map/ppermute | solution.py:270
  22.3 2.4 %coils.5 = (f32[2,160,128]{2,1,0:T(8,128)S(1)}, f32[2,160,128]{2,1,0:T(8,128)S(1)}, f32[2,2,160,128]{3,2,1,0:T(8,128)S(1)}, f32[8,2,160,128]{3,2,1,0:T(8,128)S(1)}, f32[8,128]{1,0:T(8,128)S(1)}) custom-call(f32[2,160,128]{2,1,0:T(8,128)S(1)} %get-tuple-element.68.refs_0_, ...), custom_call_target="tpu_custom_call", output_to_operand_aliasing={{4}: (12, {}), {3}: (11, {})} | custom-call | flops 100000000 | bytes 100 | tf_op jit(solution)/shard_map/coils/pallas_call | solution.py:84
  24.7 1.6 %collective-permute-start.12 = (f32[2,160,128]{2,1,0:T(8,128)S(1)}, f32[2,160,128]{2,1,0:T(8,128)S(1)}, u32[]{:S(2)}, u32[]{:S(2)}) collective-permute-start(f32[2,160,128]{2,1,0:T(8,128)S(1)} %get-tuple-element.84), channel_id=1, source_target_pairs={{0,2},{1,3},{2,0},{3,1},{4,6},{5,7},{6,4},{7,5},{8,10},{9,11},{10,... | collective-permute-start | bytes 491528 | tf_op jit(solution)/shard_map/ppermute | solution.py:270
  26.2 2.4 %coils.6 = (f32[2,160,128]{2,1,0:T(8,128)S(1)}, f32[2,160,128]{2,1,0:T(8,128)S(1)}, f32[2,2,160,128]{3,2,1,0:T(8,128)S(1)}, f32[8,2,160,128]{3,2,1,0:T(8,128)S(1)}, f32[8,128]{1,0:T(8,128)S(1)}) custom-call(f32[2,160,128]{2,1,0:T(8,128)S(1)} %get-tuple-element.70.refs_0_, ...), custom_call_target="tpu_custom_call", output_to_operand_aliasing={{4}: (12, {}), {3}: (11, {})} | custom-call | flops 100000000 | bytes 100 | tf_op jit(solution)/shard_map/coils/pallas_call | solution.py:84
  28.6 0.6 %collective-permute-start.10 = (f32[2,160,128]{2,1,0:T(8,128)S(1)}, f32[2,160,128]{2,1,0:T(8,128)S(1)}, u32[]{:S(2)}, u32[]{:S(2)}) collective-permute-start(f32[2,160,128]{2,1,0:T(8,128)S(1)} %get-tuple-element.80), channel_id=1, source_target_pairs={{0,2},{1,3},{2,0},{3,1},{4,6},{5,7},{6,4},{7,5},{8,10},{9,11},{10,... | collective-permute-start | bytes 491528 | tf_op jit(solution)/shard_map/ppermute | solution.py:270
  29.2 2.4 %coils.7 = (f32[2,160,128]{2,1,0:T(8,128)S(1)}, f32[2,160,128]{2,1,0:T(8,128)S(1)}, f32[2,2,160,128]{3,2,1,0:T(8,128)S(1)}, f32[8,2,160,128]{3,2,1,0:T(8,128)S(1)}, f32[8,128]{1,0:T(8,128)S(1)}) custom-call(f32[2,160,128]{2,1,0:T(8,128)S(1)} %get-tuple-element.69.refs_0_, ...), custom_call_target="tpu_custom_call", output_to_operand_aliasing={{4}: (12, {}), {3}: (11, {})} | custom-call | flops 100000000 | bytes 100 | tf_op jit(solution)/shard_map/coils/pallas_call | solution.py:84
  31.6 1.6 %collective-permute-start.9 = (f32[2,160,128]{2,1,0:T(8,128)S(1)}, f32[2,160,128]{2,1,0:T(8,128)S(1)}, u32[]{:S(2)}, u32[]{:S(2)}) collective-permute-start(f32[2,160,128]{2,1,0:T(8,128)S(1)} %get-tuple-element.78), channel_id=1, source_target_pairs={{0,2},{1,3},{2,0},{3,1},{4,6},{5,7},{6,4},{7,5},{8,10},{9,11},{10,... | collective-permute-start | bytes 491528 | tf_op jit(solution)/shard_map/ppermute | solution.py:270
  33.2 0.8 %temporal.1 = (f32[2,160,128]{2,1,0:T(8,128)}, f32[2,160,128]{2,1,0:T(8,128)S(1)}, f32[8,128]{1,0:T(8,128)S(1)}) custom-call(f32[2,160,128]{2,1,0:T(8,128)S(1)} %get-tuple-element.81.refs_0_, f32[4,160,128]{2,1,0:T(8,128)S(1)} %get-tuple-element.82.refs_1_, f32[4,160,128]{2,1,0:T(8,128)S(1)} %collective-permute-done.11.refs_2_, ...), custom_call_target="tpu_custom_call", output_to_operand_aliasing={{2}: (3, {})} | custom-call | flops 50000 | bytes 100 | tf_op jit(solution)/shard_map/temporal/pallas_call | solution.py:84
  34.0 1.8 %collective-permute-done.10.refs_1_ = f32[2,160,128]{2,1,0:T(8,128)S(1)} collective-permute-done((f32[2,160,128]{2,1,0:T(8,128)S(1)}, f32[2,160,128]{2,1,0:T(8,128)S(1)}, u32[]{:S(2)}, u32[]{:S(2)}) %collective-permute-start.10) | collective-permute-done | bytes 163872 | tf_op jit(solution)/shard_map/ppermute | solution.py:270
  35.8 0.9 %collective-permute-start.14 = (f32[2,160,128]{2,1,0:T(8,128)S(1)}, f32[2,160,128]{2,1,0:T(8,128)S(1)}, u32[]{:S(2)}, u32[]{:S(2)}) collective-permute-start(f32[2,160,128]{2,1,0:T(8,128)S(1)} %get-tuple-element.91), channel_id=1, source_target_pairs={{0,4},{1,5},{2,6},{3,7},{4,0},{5,1},{6,2},{7,3},{8,12},{9,13},{10,... | collective-permute-start | bytes 491528 | tf_op jit(solution)/shard_map/ppermute | solution.py:270
  36.8 1.4 %collective-permute-start.15 = (f32[2,160,128]{2,1,0:T(8,128)S(1)}, f32[2,160,128]{2,1,0:T(8,128)S(1)}, u32[]{:S(2)}, u32[]{:S(2)}) collective-permute-start(f32[2,160,128]{2,1,0:T(8,128)S(1)} %get-tuple-element.92), channel_id=1, source_target_pairs={{0,8},{1,9},{2,10},{3,11},{4,12},{5,13},{6,14},{7,15},{8,0},{9,1},... | collective-permute-start | bytes 491528 | tf_op jit(solution)/shard_map/ppermute | solution.py:270
  38.1 0.6 %collective-permute-start.4 = (f32[2,160,128]{2,1,0:T(8,128)S(1)}, f32[2,160,128]{2,1,0:T(8,128)S(1)}, u32[]{:S(2)}, u32[]{:S(2)}) collective-permute-start(f32[2,160,128]{2,1,0:T(8,128)S(1)} %get-tuple-element.66), channel_id=1, source_target_pairs={{0,2},{1,3},{2,0},{3,1},{4,6},{5,7},{6,4},{7,5},{8,10},{9,11},{10,... | collective-permute-start | bytes 491528 | tf_op jit(solution)/shard_map/ppermute | solution.py:270
  38.8 0.2 collective-permute-done.9.refs_1_
  39.0 1.7 %collective-permute-start.13 = (f32[2,160,128]{2,1,0:T(8,128)S(1)}, f32[2,160,128]{2,1,0:T(8,128)S(1)}, u32[]{:S(2)}, u32[]{:S(2)}) collective-permute-start(f32[2,160,128]{2,1,0:T(8,128)S(1)} %get-tuple-element.89), channel_id=1, source_target_pairs={{0,12},{1,13},{2,14},{3,15},{4,8},{5,9},{6,10},{7,11},{8,4},{9,5},... | collective-permute-start | bytes 491528 | tf_op jit(solution)/shard_map/ppermute | solution.py:270
  40.7 2.3 %collective-permute-done.14.refs_1_ = f32[2,160,128]{2,1,0:T(8,128)S(1)} collective-permute-done((f32[2,160,128]{2,1,0:T(8,128)S(1)}, f32[2,160,128]{2,1,0:T(8,128)S(1)}, u32[]{:S(2)}, u32[]{:S(2)}) %collective-permute-start.14) | collective-permute-done | bytes 163872 | tf_op jit(solution)/shard_map/ppermute | solution.py:270
  43.1 5.5 %collective-permute-done.15.refs_2_ = f32[2,160,128]{2,1,0:T(8,128)S(1)} collective-permute-done((f32[2,160,128]{2,1,0:T(8,128)S(1)}, f32[2,160,128]{2,1,0:T(8,128)S(1)}, u32[]{:S(2)}, u32[]{:S(2)}) %collective-permute-start.15) | collective-permute-done | bytes 163872 | tf_op jit(solution)/shard_map/ppermute | solution.py:270
  48.6 0.7 %sums.9 = f32[2,160,128]{2,1,0:T(8,128)} custom-call(f32[2,160,128]{2,1,0:T(8,128)S(1)} %collective-permute-done.4.refs_0_, f32[2,160,128]{2,1,0:T(8,128)S(1)} %collective-permute-done.13.refs_1_, f32[2,160,128]{2,1,0:T(8,128)S(1)} %get-tuple-element.95.refs_2_), custom_call_target="tpu_custom_call" | custom-call | flops 1000 | bytes 100 | tf_op jit(solution)/shard_map/sums/pallas_call | solution.py:84
  49.3 1.6 %store.1 = f32[2,1,1,16,160,128]{5,4,3,2,1,0:T(8,128)} custom-call(f32[2,2,160,128]{3,2,1,0:T(8,128)S(1)} %get-tuple-element.97.refs_0_, f32[2,2,160,128]{3,2,1,0:T(8,128)S(1)} %get-tuple-element.98.refs_1_, f32[2,2,160,128]{3,2,1,0:T(8,128)S(1)} %get-tuple-element.99.refs_2_, f32[2,2,160,128]{3,2,1,0:T(8,128)S(1)} %get-tuple-element.100.refs_3_, ...), custom_call_target="tpu_custom_call" | custom-call | flops 1000 | bytes 100 | tf_op jit(solution)/shard_map/store/pallas_call | solution.py:366
  (16 shorter events, 0.1 us)
Async XLA Ops:
  0.6 11.7 %collective-permute-start = (f32[2,160,128]{2,1,0:T(8,128)}, f32[2,160,128]{2,1,0:T(8,128)S(1)}, u32[]{:S(2)}, u32[]{:S(2)}) collective-permute-start(f32[2,160,128]{2,1,0:T(8,128)} %bitcast.8), channel_id=1, source_target_pairs={{0,2},{1,3},{2,0},{3,1},{4,6},{5,7},{6,4},{7,5},{8,10},{9,11},{10,... | collective-permute-start | bytes 491528 | tf_op jit(solution)/shard_map/ppermute | solution.py:270
  3.6 8.9 %collective-permute-start.1 = (f32[2,160,128]{2,1,0:T(8,128)}, f32[2,160,128]{2,1,0:T(8,128)S(1)}, u32[]{:S(2)}, u32[]{:S(2)}) collective-permute-start(f32[2,160,128]{2,1,0:T(8,128)} %bitcast.9), channel_id=1, source_target_pairs={{0,4},{1,5},{2,6},{3,7},{4,0},{5,1},{6,2},{7,3},{8,12},{9,13},{10,... | collective-permute-start | bytes 491528 | tf_op jit(solution)/shard_map/ppermute | solution.py:270
  5.2 10.1 %collective-permute-start.2 = (f32[2,160,128]{2,1,0:T(8,128)}, f32[2,160,128]{2,1,0:T(8,128)S(1)}, u32[]{:S(2)}, u32[]{:S(2)}) collective-permute-start(f32[2,160,128]{2,1,0:T(8,128)} %bitcast.10), channel_id=1, source_target_pairs={{0,8},{1,9},{2,10},{3,11},{4,12},{5,13},{6,14},{7,15},{8,0},{9,1},... | collective-permute-start | bytes 491528 | tf_op jit(solution)/shard_map/ppermute | solution.py:270
  12.3 7.0 %collective-permute-start.3 = (f32[2,8,2,160,128]{4,3,2,1,0:T(8,128)S(1)}, f32[2,8,2,160,128]{4,3,2,1,0:T(8,128)S(1)}, u32[]{:S(2)}, u32[]{:S(2)}) collective-permute-start(f32[2,8,2,160,128]{4,3,2,1,0:T(8,128)S(1)} %get-tuple-element.57), channel_id=1, source_target_pairs={{0,1},{1,0},{2,3},{3,2},{4,5},{5,4},{6,7},{7,6},{8,9},{9,8},{10,11... | collective-permute-start | bytes 7864328 | tf_op jit(solution)/shard_map/ppermute | solution.py:270
  15.3 6.4 %collective-permute-start.5 = (f32[2,160,128]{2,1,0:T(8,128)S(1)}, f32[2,160,128]{2,1,0:T(8,128)S(1)}, u32[]{:S(2)}, u32[]{:S(2)}) collective-permute-start(f32[2,160,128]{2,1,0:T(8,128)S(1)} %get-tuple-element.68.refs_0_), channel_id=1, source_target_pairs={{0,4},{1,5},{2,6},{3,7},{4,0},{5,1},{6,2},{7,3},{8,12},{9,13},{10,... | collective-permute-start | bytes 491528 | tf_op jit(solution)/shard_map/ppermute | solution.py:270
  15.7 6.6 %collective-permute-start.8 = (f32[2,160,128]{2,1,0:T(8,128)S(1)}, f32[2,160,128]{2,1,0:T(8,128)S(1)}, u32[]{:S(2)}, u32[]{:S(2)}) collective-permute-start(f32[2,160,128]{2,1,0:T(8,128)S(1)} %get-tuple-element.68.refs_0_), channel_id=1, source_target_pairs={{0,2},{1,3},{2,0},{3,1},{4,6},{5,7},{6,4},{7,5},{8,10},{9,11},{10,... | collective-permute-start | bytes 491528 | tf_op jit(solution)/shard_map/ppermute | solution.py:270
  16.2 10.0 %collective-permute-start.7 = (f32[2,160,128]{2,1,0:T(8,128)S(1)}, f32[2,160,128]{2,1,0:T(8,128)S(1)}, u32[]{:S(2)}, u32[]{:S(2)}) collective-permute-start(f32[2,160,128]{2,1,0:T(8,128)S(1)} %get-tuple-element.70.refs_0_), channel_id=1, source_target_pairs={{0,2},{1,3},{2,0},{3,1},{4,6},{5,7},{6,4},{7,5},{8,10},{9,11},{10,... | collective-permute-start | bytes 491528 | tf_op jit(solution)/shard_map/ppermute | solution.py:270
  17.7 15.5 %collective-permute-start.11 = (f32[4,160,128]{2,1,0:T(8,128)S(1)}, f32[4,160,128]{2,1,0:T(8,128)S(1)}, u32[]{:S(2)}, u32[]{:S(2)}) collective-permute-start(f32[4,160,128]{2,1,0:T(8,128)S(1)} %get-tuple-element.82.refs_1_), channel_id=1, source_target_pairs={{0,16},{16,0},{1,17},{17,1},{2,18},{18,2},{3,19},{19,3},{4,20},{20... | collective-permute-start | bytes 983048 | tf_op jit(solution)/shard_map/ppermute | solution.py:265
  21.7 7.5 %collective-permute-start.6 = (f32[2,160,128]{2,1,0:T(8,128)S(1)}, f32[2,160,128]{2,1,0:T(8,128)S(1)}, u32[]{:S(2)}, u32[]{:S(2)}) collective-permute-start(f32[2,160,128]{2,1,0:T(8,128)S(1)} %get-tuple-element.69.refs_0_), channel_id=1, source_target_pairs={{0,2},{1,3},{2,0},{3,1},{4,6},{5,7},{6,4},{7,5},{8,10},{9,11},{10,... | collective-permute-start | bytes 491528 | tf_op jit(solution)/shard_map/ppermute | solution.py:270
  24.7 8.5 %collective-permute-start.12 = (f32[2,160,128]{2,1,0:T(8,128)S(1)}, f32[2,160,128]{2,1,0:T(8,128)S(1)}, u32[]{:S(2)}, u32[]{:S(2)}) collective-permute-start(f32[2,160,128]{2,1,0:T(8,128)S(1)} %get-tuple-element.84), channel_id=1, source_target_pairs={{0,2},{1,3},{2,0},{3,1},{4,6},{5,7},{6,4},{7,5},{8,10},{9,11},{10,... | collective-permute-start | bytes 491528 | tf_op jit(solution)/shard_map/ppermute | solution.py:270
  28.6 7.2 %collective-permute-start.10 = (f32[2,160,128]{2,1,0:T(8,128)S(1)}, f32[2,160,128]{2,1,0:T(8,128)S(1)}, u32[]{:S(2)}, u32[]{:S(2)}) collective-permute-start(f32[2,160,128]{2,1,0:T(8,128)S(1)} %get-tuple-element.80), channel_id=1, source_target_pairs={{0,2},{1,3},{2,0},{3,1},{4,6},{5,7},{6,4},{7,5},{8,10},{9,11},{10,... | collective-permute-start | bytes 491528 | tf_op jit(solution)/shard_map/ppermute | solution.py:270
  31.6 7.4 %collective-permute-start.9 = (f32[2,160,128]{2,1,0:T(8,128)S(1)}, f32[2,160,128]{2,1,0:T(8,128)S(1)}, u32[]{:S(2)}, u32[]{:S(2)}) collective-permute-start(f32[2,160,128]{2,1,0:T(8,128)S(1)} %get-tuple-element.78), channel_id=1, source_target_pairs={{0,2},{1,3},{2,0},{3,1},{4,6},{5,7},{6,4},{7,5},{8,10},{9,11},{10,... | collective-permute-start | bytes 491528 | tf_op jit(solution)/shard_map/ppermute | solution.py:270
  35.8 7.2 %collective-permute-start.14 = (f32[2,160,128]{2,1,0:T(8,128)S(1)}, f32[2,160,128]{2,1,0:T(8,128)S(1)}, u32[]{:S(2)}, u32[]{:S(2)}) collective-permute-start(f32[2,160,128]{2,1,0:T(8,128)S(1)} %get-tuple-element.91), channel_id=1, source_target_pairs={{0,4},{1,5},{2,6},{3,7},{4,0},{5,1},{6,2},{7,3},{8,12},{9,13},{10,... | collective-permute-start | bytes 491528 | tf_op jit(solution)/shard_map/ppermute | solution.py:270
  36.8 11.8 %collective-permute-start.15 = (f32[2,160,128]{2,1,0:T(8,128)S(1)}, f32[2,160,128]{2,1,0:T(8,128)S(1)}, u32[]{:S(2)}, u32[]{:S(2)}) collective-permute-start(f32[2,160,128]{2,1,0:T(8,128)S(1)} %get-tuple-element.92), channel_id=1, source_target_pairs={{0,8},{1,9},{2,10},{3,11},{4,12},{5,13},{6,14},{7,15},{8,0},{9,1},... | collective-permute-start | bytes 491528 | tf_op jit(solution)/shard_map/ppermute | solution.py:270
  38.1 10.4 %collective-permute-start.4 = (f32[2,160,128]{2,1,0:T(8,128)S(1)}, f32[2,160,128]{2,1,0:T(8,128)S(1)}, u32[]{:S(2)}, u32[]{:S(2)}) collective-permute-start(f32[2,160,128]{2,1,0:T(8,128)S(1)} %get-tuple-element.66), channel_id=1, source_target_pairs={{0,2},{1,3},{2,0},{3,1},{4,6},{5,7},{6,4},{7,5},{8,10},{9,11},{10,... | collective-permute-start | bytes 491528 | tf_op jit(solution)/shard_map/ppermute | solution.py:270
  38.7 10.5 %collective-permute-start.16 = (f32[8,2,160,128]{3,2,1,0:T(8,128)S(1)}, f32[8,2,160,128]{3,2,1,0:T(8,128)S(1)}, u32[]{:S(2)}, u32[]{:S(2)}) collective-permute-start(f32[8,2,160,128]{3,2,1,0:T(8,128)S(1)} %get-tuple-element.101), channel_id=1, source_target_pairs={{0,1},{1,0},{2,3},{3,2},{4,5},{5,4},{6,7},{7,6},{8,9},{9,8},{10,11... | collective-permute-start | bytes 3932168 | tf_op jit(solution)/shard_map/ppermute | solution.py:270
  39.0 9.6 %collective-permute-start.13 = (f32[2,160,128]{2,1,0:T(8,128)S(1)}, f32[2,160,128]{2,1,0:T(8,128)S(1)}, u32[]{:S(2)}, u32[]{:S(2)}) collective-permute-start(f32[2,160,128]{2,1,0:T(8,128)S(1)} %get-tuple-element.89), channel_id=1, source_target_pairs={{0,12},{1,13},{2,14},{3,15},{4,8},{5,9},{6,10},{7,11},{8,4},{9,5},... | collective-permute-start | bytes 491528 | tf_op jit(solution)/shard_map/ppermute | solution.py:270

commit v4 on v3

--- a/solution.py
+++ b/solution.py
@@ -147,12 +147,15 @@
     weight[...] = mask_buf[0].astype(jnp.float32) / (1.0 + dual_step)
 
 
-def coil_kernel(first, held, far, passed, outs, *refs):
+def coil_kernel(first, count, held, far, passed, outs, *refs):
     values, _, targets, (u_buf, v_buf) = sorted_refs(held, far, passed, outs, refs)
-    count = outs - 2
-    blocks, sides = values[:count], values[count:count + 2]
-    weight, col_fwd, even_fwd, odd_fwd, col_bwd, even_bwd, odd_bwd = values[count + 2:count + 9]
-    totals, (new_own, new_all) = targets[:count], targets[count:]
+    sides = values[:2]
+    weight, col_fwd, even_fwd, odd_fwd, col_bwd, even_bwd, odd_bwd = values[2:9]
+    blocks = values[9:9 + count] if values[9].ndim == 3 else [values[9].at[n] for n in range(count)]
+    totals, (new_own, *packed, new_all) = targets[:count], targets[count:]
+    if packed:
+        for n in range(count):
+            packed[0][n] = blocks[n][...]
     new_other = new_all.at[first:first + count]
     height, depth = weight.shape
     half = height // 2
@@ -246,15 +249,15 @@
         target[part] = values[-1][part] - primal_step * total if begun else total
 
 
-def store_kernel(*refs):
-    groups, new_other, _, data_new, sems = refs[:-4], *refs[-4:]
+def store_kernel(other, count, *refs):
+    groups, data_new, sems = refs[:count], refs[-3], refs[-1]
     place = placed()
-    count = groups[0].shape[0]
     stores = []
-    for offset in range(new_other.shape[0]):
-        for other, source in enumerate((groups[offset // count].at[offset % count], new_other.at[offset])):
+    for g, group in enumerate(groups):
+        for n in range(group.shape[0]):
+            offset = g * group.shape[0] + n
             plane = 2 * jnp.bitwise_xor(place[0], offset) + jnp.bitwise_xor(place[1], other)
-            stores.append(pltpu.make_async_copy(source, data_new.at[:, 0, 0, plane], sems.at[other, offset]))
+            stores.append(pltpu.make_async_copy(group.at[n], data_new.at[:, 0, 0, plane], sems.at[offset]))
             stores[-1].start()
     for store in stores:
         store.wait()
@@ -288,8 +291,9 @@
         _, (token, *values) = call("ahead", pass_kernel, [], [], [token, *values], [], [], work, 2)
         return (token, *values)
 
-    blocks = {i: swapped(extrap[:, 0], 2 * i) for i in range(1, inner + 1)}
-    blocks[2 * inner] = swapped(extrap[:, 0], 4 * inner)
+    blocks = {2 * inner: swapped(extrap[:, 0], 4 * inner)}
+    for i in range(1, inner):
+        blocks[i] = swapped(extrap[:, 0], 2 * i)
 
     half = pltpu.VMEM((2, chips, 2, height, depth), jnp.float32)
     (*tables, token, weight, image_here, blocks[0], pair, near, give), _ = call(
@@ -309,70 +313,73 @@
     pair_before = turned(pair, "tm", 1)
     later = [] if frame_total == 2 else [turned(blocks[0], "tm", -1)]
 
+    def store(name, whose, groups, before, token):
+        operands = [pltpu.with_memory_space_constraint(value, pltpu.VMEM) for value in groups]
+        operands += [pltpu.with_memory_space_constraint(value, pltpu.HBM) for value in before] + [token]
+        return pl.pallas_call(
+            functools.partial(store_kernel, whose, len(groups)),
+            out_shape=[
+                jax.ShapeDtypeStruct(kspace.shape, jnp.float32), jax.ShapeDtypeStruct(token.shape, token.dtype)
+            ],
+            in_specs=[vmem] * len(groups) + [hbm] * len(before) + [anywhere],
+            out_specs=[hbm, anywhere],
+            scratch_shapes=[pltpu.SemaphoreType.DMA((chips,))],
+            input_output_aliases={len(groups) + n: n for n in (range(2) if before else ())} or {len(groups): 1},
+            compiler_params=pltpu.CompilerParams(vmem_limit_bytes=2 * mebi),
+            cost_estimate=pl.CostEstimate(flops=1_000, bytes_accessed=100, transcendentals=0),
+            name=name,
+        )(*operands)
+
     totals, new_own = {}, {}
 
-    def coils(z, token, new_other):
-        held = [blocks[z * inner + i] for i in range(inner)] + [near, other, weight, *tables]
+    def coils(z, token, arrays, new_other, packs=False):
+        held = [near, other, weight, *tables, *arrays, *new_other]
         found, (token,) = call(
-            "coils", functools.partial(coil_kernel, z * inner), held + new_other, [], [token],
-            [block] * inner + [
-                pltpu.VMEM((inner, 2, height, depth), jnp.float32), pltpu.VMEM((chips, 2, height, depth), jnp.float32)
-            ],
+            "coils", functools.partial(coil_kernel, z * inner, inner), held, [], [token],
+            [block] * inner + [pltpu.VMEM((inner, 2, height, depth), jnp.float32)] * (2 if packs else 1)
+            + [pltpu.VMEM((chips, 2, height, depth), jnp.float32)],
             [pltpu.VMEM((2, 2 * height, depth), jnp.float32)] * 2,
-            100_000, 8, len(held) if new_other else None,
+            100_000, 8, len(held) - 1 if new_other else None,
         )
-        totals[z], new_own[z] = found[:inner], found[inner]
-        arrived[z] = [swapped(totals[z][i], 2 * i) for i in range(1, inner)]
-        return token, [found[inner + 1]]
-
-    def onward(z, token):
-        (found,), (token,) = call(
-            "sums", functools.partial(sum_kernel, 0), [totals[z][0], *arrived[z]], [], [token], [block], [],
-            50, 2,
-        )
-        return found, token
-
-    arrived, parts = {}, {}
-    token, *found = ahead(30_000_000, token, *[blocks[i] for i in range(1, inner + 1)], blocks[2 * inner])
-    blocks.update(zip([*range(1, inner + 1), 2 * inner], found))
-    blocks[3 * inner] = swapped(blocks[2 * inner], 2 * inner)
-    for z in (1, 2):
-        for i in range(1, inner):
-            blocks[z * inner + i] = swapped(blocks[z * inner], 2 * i)
-    token, new_other = coils(0, token, [])
-    token, blocks[3 * inner] = ahead(1, token, blocks[3 * inner])
+        totals[z], new_own[z] = list(found[:inner]), found[inner]
+        return (token, found[-1:], *(found[inner + 1:-1]))
+
+    def beside(z):
+        return [swapped(totals[z][i], 2 * i) for i in range(1, inner)]
+
+    def sums(values, passed, work):
+        (found,), passed = call("sums", functools.partial(sum_kernel, 0), values, [], passed, [block], [], work, 2)
+        return (found, *passed)
+
+    token, blocks[2 * inner] = ahead(30_000_000, token, blocks[2 * inner])
+    for i in range(inner):
+        blocks[3 * inner + i] = swapped(blocks[2 * inner], 2 * (inner + i))
     for i in range(1, inner):
-        blocks[3 * inner + i] = swapped(blocks[3 * inner], 2 * i)
-    for z in (2, 1, 3):
-        token, new_other = coils(z, token, new_other)
-    parts[2], token = onward(2, token)
+        blocks[2 * inner + i] = swapped(blocks[2 * inner], 2 * i)
+    token, new_other, pack = coils(0, token, [blocks[i] for i in range(inner)], [], True)
+    pack = swapped(pack, 2 * inner)
+    for z in (2, 3):
+        token, new_other = coils(z, token, [blocks[z * inner + i] for i in range(inner)], new_other)
+    beside_far = beside(3)
+    part, token = sums([totals[2][0], *beside(2)], [token], 1_900_000)
+    from_2 = swapped(part, 4 * inner)
+    token, new_other = coils(1, token, [pack], new_other)
+    part, token, *totals[1][1:] = sums([totals[3][0], *beside_far], [token, *totals[1][1:]], 50)
+    from_3 = swapped(part, 6 * inner)
+    total, token, *totals[0][1:] = sums([totals[0][0], from_2], [token, *totals[0][1:]], 300_000)
+    part, token = sums([totals[1][0], *beside(1)], [token], 50)
+    from_1 = swapped(part, 2 * inner)
     (tv_here, begin), (token,) = call(
         "temporal", functools.partial(temporal_kernel, frame_total), [image_here, pair, pair_before, *later], [], [token],
         [result, block], [], 50, 4,
     )
-    for z in (1, 3):
-        parts[z], token = onward(z, token)
-    parts = [swapped(parts[z], 2 * z * inner) for z in (1, 2, 3)]
-    new_other = swapped(new_other[0], 1)
-    (begin,), (token,) = call(
-        "sums", functools.partial(sum_kernel, 1), [totals[0][0], *parts[:2], begin], [], [token], [block], [],
+    data_new, token = store("store", 0, [new_own[z] for z in range(4)], [], token)
+    total, token = sums([total, from_3], [token], 50_000)
+    (image_new,), (token,) = call(
+        "sums", functools.partial(sum_kernel, 1), [total, from_1, *beside(0), begin], [], [token], [result], [],
         20_000_000, 2,
     )
-    (image_new,), _ = call(
-        "sums", functools.partial(sum_kernel, 1), [*arrived[0], parts[2], begin], [], [], [result], [], 1, 2,
-    )
-
-    groups = [new_own[z] for z in range(4)] + [new_other, token]
-    data_new = pl.pallas_call(
-        store_kernel,
-        out_shape=jax.ShapeDtypeStruct(kspace.shape, jnp.float32),
-        in_specs=[vmem] * len(groups),
-        out_specs=hbm,
-        scratch_shapes=[pltpu.SemaphoreType.DMA((2, chips))],
-        compiler_params=pltpu.CompilerParams(vmem_limit_bytes=2 * mebi),
-        cost_estimate=pl.CostEstimate(flops=1_000, bytes_accessed=100, transcendentals=0),
-        name="store",
-    )(*groups)
+    data_new, _ = store("store", 1, [swapped(new_other[0], 1)], [data_new], token)
     return (image_new[:, None], tv_here[:, None], data_new)
 
 

time: 51.8 us -> 48.7 us (0.940); the launches traced: 50.9 us -> 48.6 us
  waiting for transfers between devices: 12.8 us -> 6.44 us
  starting transfers between devices: 20.2 us -> 23.6 us
  Pallas kernels: 17.2 us -> 17.8 us
    ppermute x16 -> x15, waiting for transfers between devices: 12.8 us -> 6.43 us  [swapped(): lax.ppermute(value, 'space', [(source, source ^ mask) for source in range...]
    ppermute x16 -> x15, starting transfers between devices: 18.7 us -> 22 us  [swapped(): lax.ppermute(value, 'space', [(source, source ^ mask) for source in range...]
    pallas_call x1 -> x2, Pallas kernels: 1.61 us -> 2.22 us  [store(): pl.pallas_call(functools.partial(store_kernel, whose, len(groups)), out_s...]
  transfers between devices with their start and end apart: 17 -> 16, of which waited for: 6 -> 5; matrix products, arithmetic and copies ran while one was open for 0% -> 0% of each run, Pallas kernels for 31% -> 34%
where the time goes in v4:
time: 48.7 us; the launch traced here: 48.6 us
  starting transfers between devices  23.6 us (48%)
  Pallas kernels  17.8 us (37%)
  waiting for transfers between devices  6.44 us (13%)
  between operations  0.76 us (2%)
    ppermute x15, starting transfers between devices, swapped(): lax.ppermute(value, 'space', [(source, source ^ mask) for source in range...  22 us
    pallas_call x13, Pallas kernels, call(): pl.pallas_call(functools.partial(kernel, len(held), len(far), len(passed)...  15.6 us
    ppermute x15, waiting for transfers between devices, swapped(): lax.ppermute(value, 'space', [(source, source ^ mask) for source in range...  6.43 us
    pallas_call x2, Pallas kernels, store(): pl.pallas_call(functools.partial(store_kernel, whose, len(groups)), out_s...  2.22 us
    ppermute x1, starting transfers between devices, turned(): lax.ppermute(value, axis, [(source, (source + steps) % count) for source...  1.52 us
  transfers between devices with their start and end apart: 16, of which 5 were waited for; matrix products, arithmetic and copies ran while one was open for 0% of the time, Pallas kernels for 34%

profile of v4, /device:TPU:0, one launch (start us, length us, event | category | flops | bytes accessed | tf_op | source)
XLA Modules:
  0.0 48.6 jit_solution(5764226950656048963)
XLA Ops:
  0.6 4.1 %collective-permute-start.2 = (f32[2,160,128]{2,1,0:T(8,128)}, f32[2,160,128]{2,1,0:T(8,128)S(1)}, u32[]{:S(2)}, u32[]{:S(2)}) collective-permute-start(f32[2,160,128]{2,1,0:T(8,128)} %bitcast.7), channel_id=1, source_target_pairs={{0,8},{1,9},{2,10},{3,11},{4,12},{5,13},{6,14},{7,15},{8,0},{9,1},... | collective-permute-start | bytes 491528 | tf_op jit(solution)/shard_map/ppermute | solution.py:273
  4.7 1.5 %collective-permute-start.1 = (f32[2,160,128]{2,1,0:T(8,128)}, f32[2,160,128]{2,1,0:T(8,128)S(1)}, u32[]{:S(2)}, u32[]{:S(2)}) collective-permute-start(f32[2,160,128]{2,1,0:T(8,128)} %bitcast.8), channel_id=1, source_target_pairs={{0,2},{1,3},{2,0},{3,1},{4,6},{5,7},{6,4},{7,5},{8,10},{9,11},{10,... | collective-permute-start | bytes 491528 | tf_op jit(solution)/shard_map/ppermute | solution.py:273
  6.2 4.5 %load.1 = (bf16[768,256]{1,0:T(8,128)(2,1)S(1)}, bf16[160,480]{1,0:T(8,128)(2,1)S(1)}, bf16[160,480]{1,0:T(8,128)(2,1)S(1)}, bf16[768,256]{1,0:T(8,128)(2,1)S(1)...) custom-call(bf16[768,256]{1,0:T(8,128)(2,1)} %constant.12.clone.refs, ...), custom_call_target="tpu_custom_call" | custom-call | flops 1000 | bytes 100 | tf_op jit(solution)/shard_map/load/pallas_call | solution.py:84
  10.7 0.1 collective-permute-start
  10.8 1.9 %collective-permute-done.2.refs_1_ = f32[2,160,128]{2,1,0:T(8,128)S(1)} collective-permute-done((f32[2,160,128]{2,1,0:T(8,128)}, f32[2,160,128]{2,1,0:T(8,128)S(1)}, u32[]{:S(2)}, u32[]{:S(2)}) %collective-permute-start.2) | collective-permute-done | bytes 163872 | tf_op jit(solution)/shard_map/ppermute | solution.py:273
  12.7 1.5 %collective-permute-start.3 = (f32[2,160,128]{2,1,0:T(8,128)S(1)}, f32[2,160,128]{2,1,0:T(8,128)S(1)}, u32[]{:S(2)}, u32[]{:S(2)}) collective-permute-start(f32[2,160,128]{2,1,0:T(8,128)S(1)} %get-tuple-element.72.refs_9_), channel_id=1, source_target_pairs={{0,2},{1,3},{2,0},{3,1},{4,6},{5,7},{6,4},{7,5},{8,10},{9,11},{10,... | collective-permute-start | bytes 491528 | tf_op jit(solution)/shard_map/ppermute | solution.py:273
  14.2 0.8 %collective-permute-start.5 = (f32[2,160,128]{2,1,0:T(8,128)S(1)}, f32[2,160,128]{2,1,0:T(8,128)S(1)}, u32[]{:S(2)}, u32[]{:S(2)}) collective-permute-start(f32[2,160,128]{2,1,0:T(8,128)S(1)} %get-tuple-element.72.refs_9_), channel_id=1, source_target_pairs={{0,4},{1,5},{2,6},{3,7},{4,0},{5,1},{6,2},{7,3},{8,12},{9,13},{10,... | collective-permute-start | bytes 491528 | tf_op jit(solution)/shard_map/ppermute | solution.py:273
  15.0 1.2 %collective-permute-start.6 = (f32[2,160,128]{2,1,0:T(8,128)S(1)}, f32[2,160,128]{2,1,0:T(8,128)S(1)}, u32[]{:S(2)}, u32[]{:S(2)}) collective-permute-start(f32[2,160,128]{2,1,0:T(8,128)S(1)} %get-tuple-element.72.refs_9_), channel_id=1, source_target_pairs={{0,6},{1,7},{2,4},{3,5},{4,2},{5,3},{6,0},{7,1},{8,14},{9,15},{10,... | collective-permute-start | bytes 491528 | tf_op jit(solution)/shard_map/ppermute | solution.py:273
  16.1 0.0 collective-permute-done.refs_1_
  16.2 2.4 %coils.4 = (f32[2,160,128]{2,1,0:T(8,128)S(1)}, f32[2,160,128]{2,1,0:T(8,128)S(1)}, f32[2,2,160,128]{3,2,1,0:T(8,128)S(1)}, f32[2,2,160,128]{3,2,1,0:T(8,128)S(1...) custom-call(f32[2,8,2,160,128]{4,3,2,1,0:T(8,128)S(1)} %get-tuple-element.59.refs_0_, ...), custom_call_target="tpu_custom_call", output_to_operand_aliasing={{5}: (11, {})} | custom-call | flops 100000000 | bytes 100 | tf_op jit(solution)/shard_map/coils/pallas_call | solution.py:84
  18.6 2.4 %coils.5 = (f32[2,160,128]{2,1,0:T(8,128)S(1)}, f32[2,160,128]{2,1,0:T(8,128)S(1)}, f32[2,2,160,128]{3,2,1,0:T(8,128)S(1)}, f32[8,2,160,128]{3,2,1,0:T(8,128)S(1)}, f32[8,128]{1,0:T(8,128)S(1)}) custom-call(f32[2,8,2,160,128]{4,3,2,1,0:T(8,128)S(1)} %get-tuple-element.59.refs_0_, ...), custom_call_target="tpu_custom_call", output_to_operand_aliasing={{4}: (12, {}), {3}: (11, {})} | custom-call | flops 100000000 | bytes 100 | tf_op jit(solution)/shard_map/coils/pallas_call | solution.py:84
  20.9 2.3 %collective-permute-start.4 = (f32[2,160,128]{2,1,0:T(8,128)S(1)}, f32[2,160,128]{2,1,0:T(8,128)S(1)}, u32[]{:S(2)}, u32[]{:S(2)}) collective-permute-start(f32[2,160,128]{2,1,0:T(8,128)S(1)} %get-tuple-element.76), channel_id=1, source_target_pairs={{0,2},{1,3},{2,0},{3,1},{4,6},{5,7},{6,4},{7,5},{8,10},{9,11},{10,... | collective-permute-start | bytes 491528 | tf_op jit(solution)/shard_map/ppermute | solution.py:273
  23.2 0.4 collective-permute-start.9
  23.6 2.4 %coils.6 = (f32[2,160,128]{2,1,0:T(8,128)S(1)}, f32[2,160,128]{2,1,0:T(8,128)S(1)}, f32[2,2,160,128]{3,2,1,0:T(8,128)S(1)}, f32[8,2,160,128]{3,2,1,0:T(8,128)S(1)}, f32[8,128]{1,0:T(8,128)S(1)}) custom-call(f32[2,8,2,160,128]{4,3,2,1,0:T(8,128)S(1)} %get-tuple-element.59.refs_0_, ...), custom_call_target="tpu_custom_call", output_to_operand_aliasing={{4}: (12, {}), {3}: (11, {})} | custom-call | flops 100000000 | bytes 100 | tf_op jit(solution)/shard_map/coils/pallas_call | solution.py:84
  26.0 0.6 %collective-permute-start.8 = (f32[2,160,128]{2,1,0:T(8,128)S(1)}, f32[2,160,128]{2,1,0:T(8,128)S(1)}, u32[]{:S(2)}, u32[]{:S(2)}) collective-permute-start(f32[2,160,128]{2,1,0:T(8,128)S(1)} %get-tuple-element.82), channel_id=1, source_target_pairs={{0,2},{1,3},{2,0},{3,1},{4,6},{5,7},{6,4},{7,5},{8,10},{9,11},{10,... | collective-permute-start | bytes 491528 | tf_op jit(solution)/shard_map/ppermute | solution.py:273
  26.6 0.2 collective-permute-done.4.refs_1_
  26.8 3.2 %collective-permute-start.7 = (f32[2,160,128]{2,1,0:T(8,128)S(1)}, f32[2,160,128]{2,1,0:T(8,128)S(1)}, u32[]{:S(2)}, u32[]{:S(2)}) collective-permute-start(f32[2,160,128]{2,1,0:T(8,128)S(1)} %get-tuple-element.80), channel_id=1, source_target_pairs={{0,8},{1,9},{2,10},{3,11},{4,12},{5,13},{6,14},{7,15},{8,0},{9,1},... | collective-permute-start | bytes 491528 | tf_op jit(solution)/shard_map/ppermute | solution.py:273
  30.0 1.5 %collective-permute-start.11 = (f32[4,160,128]{2,1,0:T(8,128)S(1)}, f32[4,160,128]{2,1,0:T(8,128)S(1)}, u32[]{:S(2)}, u32[]{:S(2)}) collective-permute-start(f32[4,160,128]{2,1,0:T(8,128)S(1)} %get-tuple-element.97.refs_1_), channel_id=1, source_target_pairs={{0,16},{16,0},{1,17},{17,1},{2,18},{18,2},{3,19},{19,3},{4,20},{20... | collective-permute-start | bytes 983048 | tf_op jit(solution)/shard_map/ppermute | solution.py:268
  31.5 1.4 %collective-permute-done.9.refs_9_ = f32[2,2,160,128]{3,2,1,0:T(8,128)S(1)} collective-permute-done((f32[2,2,160,128]{3,2,1,0:T(8,128)S(1)}, f32[2,2,160,128]{3,2,1,0:T(8,128)S(1)}, u32[]{:S(2)}, u32[]{:S(2)}) %collective-permute-start.9) | collective-permute-done | bytes 327712 | tf_op jit(solution)/shard_map/ppermute | solution.py:273
  32.9 2.4 %coils.7 = (f32[2,160,128]{2,1,0:T(8,128)S(1)}, f32[2,160,128]{2,1,0:T(8,128)S(1)}, f32[2,2,160,128]{3,2,1,0:T(8,128)S(1)}, f32[8,2,160,128]{3,2,1,0:T(8,128)S(1)}, f32[8,128]{1,0:T(8,128)S(1)}) custom-call(f32[2,8,2,160,128]{4,3,2,1,0:T(8,128)S(1)} %get-tuple-element.59.refs_0_, ...), custom_call_target="tpu_custom_call", output_to_operand_aliasing={{4}: (11, {}), {3}: (10, {})} | custom-call | flops 100000000 | bytes 100 | tf_op jit(solution)/shard_map/coils/pallas_call | solution.py:84
  35.3 0.9 %collective-permute-start.12 = (f32[2,160,128]{2,1,0:T(8,128)S(1)}, f32[2,160,128]{2,1,0:T(8,128)S(1)}, u32[]{:S(2)}, u32[]{:S(2)}) collective-permute-start(f32[2,160,128]{2,1,0:T(8,128)S(1)} %get-tuple-element.99), channel_id=1, source_target_pairs={{0,2},{1,3},{2,0},{3,1},{4,6},{5,7},{6,4},{7,5},{8,10},{9,11},{10,... | collective-permute-start | bytes 491528 | tf_op jit(solution)/shard_map/ppermute | solution.py:273
  36.2 2.9 %collective-permute-start.10 = (f32[2,160,128]{2,1,0:T(8,128)S(1)}, f32[2,160,128]{2,1,0:T(8,128)S(1)}, u32[]{:S(2)}, u32[]{:S(2)}) collective-permute-start(f32[2,160,128]{2,1,0:T(8,128)S(1)} %get-tuple-element.91), channel_id=1, source_target_pairs={{0,12},{1,13},{2,14},{3,15},{4,8},{5,9},{6,10},{7,11},{8,4},{9,5},... | collective-permute-start | bytes 491528 | tf_op jit(solution)/shard_map/ppermute | solution.py:273
  39.1 0.0 collective-permute-done.7.refs_1_
  39.1 1.3 %collective-permute-start.14 = (f32[2,160,128]{2,1,0:T(8,128)S(1)}, f32[2,160,128]{2,1,0:T(8,128)S(1)}, u32[]{:S(2)}, u32[]{:S(2)}) collective-permute-start(f32[2,160,128]{2,1,0:T(8,128)S(1)} %get-tuple-element.106), channel_id=1, source_target_pairs={{0,2},{1,3},{2,0},{3,1},{4,6},{5,7},{6,4},{7,5},{8,10},{9,11},{10,... | collective-permute-start | bytes 491528 | tf_op jit(solution)/shard_map/ppermute | solution.py:273
  40.4 0.9 %collective-permute-done.12.refs_1_ = f32[2,160,128]{2,1,0:T(8,128)S(1)} collective-permute-done((f32[2,160,128]{2,1,0:T(8,128)S(1)}, f32[2,160,128]{2,1,0:T(8,128)S(1)}, u32[]{:S(2)}, u32[]{:S(2)}) %collective-permute-start.12) | collective-permute-done | bytes 163872 | tf_op jit(solution)/shard_map/ppermute | solution.py:273
  41.4 1.4 %collective-permute-start.13 = (f32[2,160,128]{2,1,0:T(8,128)S(1)}, f32[2,160,128]{2,1,0:T(8,128)S(1)}, u32[]{:S(2)}, u32[]{:S(2)}) collective-permute-start(f32[2,160,128]{2,1,0:T(8,128)S(1)} %get-tuple-element.105), channel_id=1, source_target_pairs={{0,4},{1,5},{2,6},{3,7},{4,0},{5,1},{6,2},{7,3},{8,12},{9,13},{10,... | collective-permute-start | bytes 491528 | tf_op jit(solution)/shard_map/ppermute | solution.py:273
  42.7 0.0 collective-permute-start.15
  42.7 0.8 %temporal.1 = (f32[2,160,128]{2,1,0:T(8,128)}, f32[2,160,128]{2,1,0:T(8,128)S(1)}, f32[8,128]{1,0:T(8,128)S(1)}) custom-call(f32[2,160,128]{2,1,0:T(8,128)S(1)} %get-tuple-element.96.refs_0_, f32[4,160,128]{2,1,0:T(8,128)S(1)} %get-tuple-element.97.refs_1_, f32[4,160,128]{2,1,0:T(8,128)S(1)} %collective-permute-done.11.refs_2_, ...), custom_call_target="tpu_custom_call", output_to_operand_aliasing={{2}: (3, {})} | custom-call | flops 50000 | bytes 100 | tf_op jit(solution)/shard_map/temporal/pallas_call | solution.py:84
  43.5 1.1 %store.2 = (f32[2,1,1,16,160,128]{5,4,3,2,1,0:T(8,128)}, f32[8,128]{1,0:T(8,128)S(1)}) custom-call(f32[2,2,160,128]{3,2,1,0:T(8,128)S(1)} %get-tuple-element.92.refs_0_, f32[2,2,160,128]{3,2,1,0:T(8,128)S(1)} %get-tuple-element.93.refs_1_, f32[2,2,160,128]{3,2,1,0:T(8,128)S(1)} %get-tuple-element.94.refs_2_, ...), custom_call_target="tpu_custom_call", output_to_operand_aliasing={{1}: (4, {})} | custom-call | flops 1000 | bytes 100 | tf_op jit(solution)/shard_map/store/pallas_call | solution.py:319
  44.7 2.1 %collective-permute-done.13.refs_1_ = f32[2,160,128]{2,1,0:T(8,128)S(1)} collective-permute-done((f32[2,160,128]{2,1,0:T(8,128)S(1)}, f32[2,160,128]{2,1,0:T(8,128)S(1)}, u32[]{:S(2)}, u32[]{:S(2)}) %collective-permute-start.13) | collective-permute-done | bytes 163872 | tf_op jit(solution)/shard_map/ppermute | solution.py:273
  46.7 0.7 %sums.11 = (f32[2,160,128]{2,1,0:T(8,128)}, f32[8,128]{1,0:T(8,128)S(1)}) custom-call(f32[2,160,128]{2,1,0:T(8,128)S(1)} %get-tuple-element.104.refs_0_, f32[2,160,128]{2,1,0:T(8,128)S(1)} %collective-permute-done.13.refs_1_, f32[2,160,128]{2,1,0:T(8,128)S(1)} %collective-permute-done.14.refs_2_, ...), custom_call_target="tpu_custom_call", output_to_operand_aliasing={{1}: (4, {})} | custom-call | flops 20000000000 | bytes 100 | tf_op jit(solution)/shard_map/sums/pallas_call | solution.py:84
  47.4 1.1 %store.3 = (f32[2,1,1,16,160,128]{5,4,3,2,1,0:T(8,128)}, f32[8,128]{1,0:T(8,128)S(1)}) custom-call(f32[8,2,160,128]{3,2,1,0:T(8,128)S(1)} %collective-permute-done.15.refs_0_, f32[2,1,1,16,160,128]{5,4,3,2,1,0:T(8,128)} %get-tuple-element.112.refs_1_, f32[8,128]{1,0:T(8,128)S(1)} %get-tuple-element.113.refs_2_), custom_call_target="tpu_custom_call", output_to_operand_aliasing={{0}: (1, {}), {1}: (2, {})} | custom-call | flops 1000 | bytes 100 | tf_op jit(solution)/shard_map/store/pallas_call | solution.py:319
  (15 shorter events, 0.1 us)
Async XLA Ops:
  0.6 12.0 %collective-permute-start.2 = (f32[2,160,128]{2,1,0:T(8,128)}, f32[2,160,128]{2,1,0:T(8,128)S(1)}, u32[]{:S(2)}, u32[]{:S(2)}) collective-permute-start(f32[2,160,128]{2,1,0:T(8,128)} %bitcast.7), channel_id=1, source_target_pairs={{0,8},{1,9},{2,10},{3,11},{4,12},{5,13},{6,14},{7,15},{8,0},{9,1},... | collective-permute-start | bytes 491528 | tf_op jit(solution)/shard_map/ppermute | solution.py:273
  4.7 11.4 %collective-permute-start.1 = (f32[2,160,128]{2,1,0:T(8,128)}, f32[2,160,128]{2,1,0:T(8,128)S(1)}, u32[]{:S(2)}, u32[]{:S(2)}) collective-permute-start(f32[2,160,128]{2,1,0:T(8,128)} %bitcast.8), channel_id=1, source_target_pairs={{0,2},{1,3},{2,0},{3,1},{4,6},{5,7},{6,4},{7,5},{8,10},{9,11},{10,... | collective-permute-start | bytes 491528 | tf_op jit(solution)/shard_map/ppermute | solution.py:273
  10.7 5.4 %collective-permute-start = (f32[2,8,2,160,128]{4,3,2,1,0:T(8,128)S(1)}, f32[2,8,2,160,128]{4,3,2,1,0:T(8,128)S(1)}, u32[]{:S(2)}, u32[]{:S(2)}) collective-permute-start(f32[2,8,2,160,128]{4,3,2,1,0:T(8,128)S(1)} %get-tuple-element.60), channel_id=1, source_target_pairs={{0,1},{1,0},{2,3},{3,2},{4,5},{5,4},{6,7},{7,6},{8,9},{9,8},{10,11... | collective-permute-start | bytes 7864328 | tf_op jit(solution)/shard_map/ppermute | solution.py:273
  12.7 5.9 %collective-permute-start.3 = (f32[2,160,128]{2,1,0:T(8,128)S(1)}, f32[2,160,128]{2,1,0:T(8,128)S(1)}, u32[]{:S(2)}, u32[]{:S(2)}) collective-permute-start(f32[2,160,128]{2,1,0:T(8,128)S(1)} %get-tuple-element.72.refs_9_), channel_id=1, source_target_pairs={{0,2},{1,3},{2,0},{3,1},{4,6},{5,7},{6,4},{7,5},{8,10},{9,11},{10,... | collective-permute-start | bytes 491528 | tf_op jit(solution)/shard_map/ppermute | solution.py:273
  14.2 9.4 %collective-permute-start.5 = (f32[2,160,128]{2,1,0:T(8,128)S(1)}, f32[2,160,128]{2,1,0:T(8,128)S(1)}, u32[]{:S(2)}, u32[]{:S(2)}) collective-permute-start(f32[2,160,128]{2,1,0:T(8,128)S(1)} %get-tuple-element.72.refs_9_), channel_id=1, source_target_pairs={{0,4},{1,5},{2,6},{3,7},{4,0},{5,1},{6,2},{7,3},{8,12},{9,13},{10,... | collective-permute-start | bytes 491528 | tf_op jit(solution)/shard_map/ppermute | solution.py:273
  15.0 8.7 %collective-permute-start.6 = (f32[2,160,128]{2,1,0:T(8,128)S(1)}, f32[2,160,128]{2,1,0:T(8,128)S(1)}, u32[]{:S(2)}, u32[]{:S(2)}) collective-permute-start(f32[2,160,128]{2,1,0:T(8,128)S(1)} %get-tuple-element.72.refs_9_), channel_id=1, source_target_pairs={{0,6},{1,7},{2,4},{3,5},{4,2},{5,3},{6,0},{7,1},{8,14},{9,15},{10,... | collective-permute-start | bytes 491528 | tf_op jit(solution)/shard_map/ppermute | solution.py:273
  20.9 5.8 %collective-permute-start.4 = (f32[2,160,128]{2,1,0:T(8,128)S(1)}, f32[2,160,128]{2,1,0:T(8,128)S(1)}, u32[]{:S(2)}, u32[]{:S(2)}) collective-permute-start(f32[2,160,128]{2,1,0:T(8,128)S(1)} %get-tuple-element.76), channel_id=1, source_target_pairs={{0,2},{1,3},{2,0},{3,1},{4,6},{5,7},{6,4},{7,5},{8,10},{9,11},{10,... | collective-permute-start | bytes 491528 | tf_op jit(solution)/shard_map/ppermute | solution.py:273
  23.2 9.7 %collective-permute-start.9 = (f32[2,2,160,128]{3,2,1,0:T(8,128)S(1)}, f32[2,2,160,128]{3,2,1,0:T(8,128)S(1)}, u32[]{:S(2)}, u32[]{:S(2)}) collective-permute-start(f32[2,2,160,128]{3,2,1,0:T(8,128)S(1)} %get-tuple-element.83), channel_id=1, source_target_pairs={{0,4},{1,5},{2,6},{3,7},{4,0},{5,1},{6,2},{7,3},{8,12},{9,13},{10,... | collective-permute-start | bytes 983048 | tf_op jit(solution)/shard_map/ppermute | solution.py:273
  26.0 9.2 %collective-permute-start.8 = (f32[2,160,128]{2,1,0:T(8,128)S(1)}, f32[2,160,128]{2,1,0:T(8,128)S(1)}, u32[]{:S(2)}, u32[]{:S(2)}) collective-permute-start(f32[2,160,128]{2,1,0:T(8,128)S(1)} %get-tuple-element.82), channel_id=1, source_target_pairs={{0,2},{1,3},{2,0},{3,1},{4,6},{5,7},{6,4},{7,5},{8,10},{9,11},{10,... | collective-permute-start | bytes 491528 | tf_op jit(solution)/shard_map/ppermute | solution.py:273
  26.8 12.3 %collective-permute-start.7 = (f32[2,160,128]{2,1,0:T(8,128)S(1)}, f32[2,160,128]{2,1,0:T(8,128)S(1)}, u32[]{:S(2)}, u32[]{:S(2)}) collective-permute-start(f32[2,160,128]{2,1,0:T(8,128)S(1)} %get-tuple-element.80), channel_id=1, source_target_pairs={{0,8},{1,9},{2,10},{3,11},{4,12},{5,13},{6,14},{7,15},{8,0},{9,1},... | collective-permute-start | bytes 491528 | tf_op jit(solution)/shard_map/ppermute | solution.py:273
  30.0 12.7 %collective-permute-start.11 = (f32[4,160,128]{2,1,0:T(8,128)S(1)}, f32[4,160,128]{2,1,0:T(8,128)S(1)}, u32[]{:S(2)}, u32[]{:S(2)}) collective-permute-start(f32[4,160,128]{2,1,0:T(8,128)S(1)} %get-tuple-element.97.refs_1_), channel_id=1, source_target_pairs={{0,16},{16,0},{1,17},{17,1},{2,18},{18,2},{3,19},{19,3},{4,20},{20... | collective-permute-start | bytes 983048 | tf_op jit(solution)/shard_map/ppermute | solution.py:268
  35.3 6.0 %collective-permute-start.12 = (f32[2,160,128]{2,1,0:T(8,128)S(1)}, f32[2,160,128]{2,1,0:T(8,128)S(1)}, u32[]{:S(2)}, u32[]{:S(2)}) collective-permute-start(f32[2,160,128]{2,1,0:T(8,128)S(1)} %get-tuple-element.99), channel_id=1, source_target_pairs={{0,2},{1,3},{2,0},{3,1},{4,6},{5,7},{6,4},{7,5},{8,10},{9,11},{10,... | collective-permute-start | bytes 491528 | tf_op jit(solution)/shard_map/ppermute | solution.py:273
  36.2 8.4 %collective-permute-start.10 = (f32[2,160,128]{2,1,0:T(8,128)S(1)}, f32[2,160,128]{2,1,0:T(8,128)S(1)}, u32[]{:S(2)}, u32[]{:S(2)}) collective-permute-start(f32[2,160,128]{2,1,0:T(8,128)S(1)} %get-tuple-element.91), channel_id=1, source_target_pairs={{0,12},{1,13},{2,14},{3,15},{4,8},{5,9},{6,10},{7,11},{8,4},{9,5},... | collective-permute-start | bytes 491528 | tf_op jit(solution)/shard_map/ppermute | solution.py:273
  39.1 5.5 %collective-permute-start.14 = (f32[2,160,128]{2,1,0:T(8,128)S(1)}, f32[2,160,128]{2,1,0:T(8,128)S(1)}, u32[]{:S(2)}, u32[]{:S(2)}) collective-permute-start(f32[2,160,128]{2,1,0:T(8,128)S(1)} %get-tuple-element.106), channel_id=1, source_target_pairs={{0,2},{1,3},{2,0},{3,1},{4,6},{5,7},{6,4},{7,5},{8,10},{9,11},{10,... | collective-permute-start | bytes 491528 | tf_op jit(solution)/shard_map/ppermute | solution.py:273
  41.4 5.4 %collective-permute-start.13 = (f32[2,160,128]{2,1,0:T(8,128)S(1)}, f32[2,160,128]{2,1,0:T(8,128)S(1)}, u32[]{:S(2)}, u32[]{:S(2)}) collective-permute-start(f32[2,160,128]{2,1,0:T(8,128)S(1)} %get-tuple-element.105), channel_id=1, source_target_pairs={{0,4},{1,5},{2,6},{3,7},{4,0},{5,1},{6,2},{7,3},{8,12},{9,13},{10,... | collective-permute-start | bytes 491528 | tf_op jit(solution)/shard_map/ppermute | solution.py:273
  42.7 4.7 %collective-permute-start.15 = (f32[8,2,160,128]{3,2,1,0:T(8,128)S(1)}, f32[8,2,160,128]{3,2,1,0:T(8,128)S(1)}, u32[]{:S(2)}, u32[]{:S(2)}) collective-permute-start(f32[8,2,160,128]{3,2,1,0:T(8,128)S(1)} %get-tuple-element.111), channel_id=1, source_target_pairs={{0,1},{1,0},{2,3},{3,2},{4,5},{5,4},{6,7},{7,6},{8,9},{9,8},{10,11... | collective-permute-start | bytes 3932168 | tf_op jit(solution)/shard_map/ppermute | solution.py:273

commit v5 on v4

--- a/solution.py
+++ b/solution.py
@@ -159,52 +159,56 @@
     new_other = new_all.at[first:first + count]
     height, depth = weight.shape
     half = height // 2
+    kinds = [(n, c) for n in range(count) for c in (0, 1)]
+
+    def maps(n, c):
+        return sides[c][0, first + n, 0], sides[c][0, first + n, 1]
+
+    real, imag = [], []
+    for n, c in kinds:
+        map_re, map_im = maps(n, c)
+        image_re, image_im = blocks[n][0], blocks[n][1]
+        real.append(map_re * image_re - map_im * image_im)
+        imag.append(map_re * image_im + map_im * image_re)
+    lines = columns_dft(jnp.concatenate(real, axis=0), jnp.concatenate(imag, axis=0), col_fwd[...])
+    u_buf[0] = lines[:, :depth]
+    u_buf[1] = lines[:, depth:]
+    halves = []
+    for odd, table in ((0, even_fwd), (1, odd_fwd)):
+        cells = jnp.concatenate([
+            jnp.concatenate([u_buf[part, pl.ds(k * height + odd, half, stride=2), :] for part in (0, 1)], axis=0)
+            for k in range(len(kinds))
+        ], axis=1)
+        halves.append(rows_dft(table[...], cells))
+    spectrum = (halves[0] + halves[1], halves[0] - halves[1])
+    updated = []
+    for q in (0, 1):
+        span = pl.ds(q * half, half)
+        columns = []
+        for k, (n, c) in enumerate(kinds):
+            new = (new_own, new_other)[c]
+            pieces = []
+            for part in (0, 1):
+                value = spectrum[q][part * half:(part + 1) * half, k * depth:(k + 1) * depth]
+                piece = weight[span, :] * (sides[c][1, first + n, part, span, :] + dual_step * value)
+                new[n, part, span, :] = piece
+                pieces.append(piece)
+            columns.append(jnp.concatenate(pieces, axis=0))
+        updated.append(jnp.concatenate(columns, axis=1))
+    for odd, table in ((0, even_bwd), (1, odd_bwd)):
+        back = rows_dft(table[...], updated[0] - updated[1] if odd else updated[0] + updated[1])
+        for k in range(len(kinds)):
+            for part in (0, 1):
+                v_buf[part, pl.ds(k * height + odd, half, stride=2), :] = back[
+                    part * half:(part + 1) * half, k * depth:(k + 1) * depth
+                ]
+    back = columns_dft(v_buf[0], v_buf[1], col_bwd[...])
     for n in range(count):
-
-        def maps():
-            return [(side[0, first + n, 0], side[0, first + n, 1]) for side in sides]
-
-        image_re, image_im = blocks[n][0], blocks[n][1]
-        real, imag = [], []
-        for map_re, map_im in maps():
-            real.append(map_re * image_re - map_im * image_im)
-            imag.append(map_re * image_im + map_im * image_re)
-        lines = columns_dft(jnp.concatenate(real, axis=0), jnp.concatenate(imag, axis=0), col_fwd[...])
-        u_buf[0] = lines[:, :depth]
-        u_buf[1] = lines[:, depth:]
-        halves = []
-        for odd, table in ((0, even_fwd), (1, odd_fwd)):
-            cells = jnp.concatenate([
-                jnp.concatenate([u_buf[part, pl.ds(c * height + odd, half, stride=2), :] for part in (0, 1)], axis=0)
-                for c in (0, 1)
-            ], axis=1)
-            halves.append(rows_dft(table[...], cells))
-        spectrum = (halves[0] + halves[1], halves[0] - halves[1])
-        updated = []
-        for q in (0, 1):
-            span = pl.ds(q * half, half)
-            columns = []
-            for c, new in enumerate((new_own, new_other)):
-                pieces = []
-                for part in (0, 1):
-                    value = spectrum[q][part * half:(part + 1) * half, c * depth:(c + 1) * depth]
-                    piece = weight[span, :] * (sides[c][1, first + n, part, span, :] + dual_step * value)
-                    new[n, part, span, :] = piece
-                    pieces.append(piece)
-                columns.append(jnp.concatenate(pieces, axis=0))
-            updated.append(jnp.concatenate(columns, axis=1))
-        for odd, table in ((0, even_bwd), (1, odd_bwd)):
-            back = rows_dft(table[...], updated[0] - updated[1] if odd else updated[0] + updated[1])
-            for c in (0, 1):
-                for part in (0, 1):
-                    v_buf[part, pl.ds(c * height + odd, half, stride=2), :] = back[
-                        part * half:(part + 1) * half, c * depth:(c + 1) * depth
-                    ]
-        back = columns_dft(v_buf[0], v_buf[1], col_bwd[...])
         total_re, total_im = 0.0, 0.0
-        for c, (map_re, map_im) in enumerate(maps()):
-            back_re = back[c * height:(c + 1) * height, :depth]
-            back_im = back[c * height:(c + 1) * height, depth:]
+        for c in (0, 1):
+            map_re, map_im = maps(n, c)
+            rows = slice((2 * n + c) * height, (2 * n + c + 1) * height)
+            back_re, back_im = back[rows, :depth], back[rows, depth:]
             total_re = total_re + map_re * back_re + map_im * back_im
             total_im = total_im + map_re * back_im - map_im * back_re
         totals[n][0] = total_re
@@ -338,7 +342,7 @@
             "coils", functools.partial(coil_kernel, z * inner, inner), held, [], [token],
             [block] * inner + [pltpu.VMEM((inner, 2, height, depth), jnp.float32)] * (2 if packs else 1)
             + [pltpu.VMEM((chips, 2, height, depth), jnp.float32)],
-            [pltpu.VMEM((2, 2 * height, depth), jnp.float32)] * 2,
+            [pltpu.VMEM((2, 2 * inner * height, depth), jnp.float32)] * 2,
             100_000, 8, len(held) - 1 if new_other else None,
         )
         totals[z], new_own[z] = list(found[:inner]), found[inner]
@@ -352,21 +356,22 @@
         return (found, *passed)
 
     token, blocks[2 * inner] = ahead(30_000_000, token, blocks[2 * inner])
-    for i in range(inner):
-        blocks[3 * inner + i] = swapped(blocks[2 * inner], 2 * (inner + i))
+    blocks[3 * inner] = swapped(blocks[2 * inner], 2 * inner)
     for i in range(1, inner):
         blocks[2 * inner + i] = swapped(blocks[2 * inner], 2 * i)
     token, new_other, pack = coils(0, token, [blocks[i] for i in range(inner)], [], True)
     pack = swapped(pack, 2 * inner)
+    token, blocks[3 * inner] = ahead(1, token, blocks[3 * inner])
+    for i in range(1, inner):
+        blocks[3 * inner + i] = swapped(blocks[3 * inner], 2 * i)
     for z in (2, 3):
         token, new_other = coils(z, token, [blocks[z * inner + i] for i in range(inner)], new_other)
     beside_far = beside(3)
-    part, token = sums([totals[2][0], *beside(2)], [token], 1_900_000)
+    token, new_other = coils(1, token, [pack], new_other)
+    part, token, *totals[1][1:] = sums([totals[2][0], *beside(2)], [token, *totals[1][1:]], 50)
     from_2 = swapped(part, 4 * inner)
-    token, new_other = coils(1, token, [pack], new_other)
-    part, token, *totals[1][1:] = sums([totals[3][0], *beside_far], [token, *totals[1][1:]], 50)
+    part, token = sums([totals[3][0], *beside_far], [token], 50)
     from_3 = swapped(part, 6 * inner)
-    total, token, *totals[0][1:] = sums([totals[0][0], from_2], [token, *totals[0][1:]], 300_000)
     part, token = sums([totals[1][0], *beside(1)], [token], 50)
     from_1 = swapped(part, 2 * inner)
     (tv_here, begin), (token,) = call(
@@ -374,7 +379,8 @@
         [result, block], [], 50, 4,
     )
     data_new, token = store("store", 0, [new_own[z] for z in range(4)], [], token)
-    total, token = sums([total, from_3], [token], 50_000)
+    total, token = sums([totals[0][0], from_2], [token], 100000)
+    total, token = sums([total, from_3], [token], 50000)
     (image_new,), (token,) = call(
         "sums", functools.partial(sum_kernel, 1), [total, from_1, *beside(0), begin], [], [token], [result], [],
         20_000_000, 2,

time: 48.7 us -> 47.4 us (0.973)
  waiting for transfers between devices: 6.44 us -> 9.86 us
  starting transfers between devices: 23.6 us -> 21.1 us
  Pallas kernels: 17.8 us -> 15.5 us
    ppermute x15, waiting for transfers between devices: 6.43 us -> 9.86 us  [swapped(): lax.ppermute(value, 'space', [(source, source ^ mask) for source in range...]
    ppermute x15, starting transfers between devices: 22 us -> 19.5 us  [swapped(): lax.ppermute(value, 'space', [(source, source ^ mask) for source in range...]
    pallas_call x13 -> x14, Pallas kernels: 15.6 us -> 13.3 us  [call(): pl.pallas_call(functools.partial(kernel, len(held), len(far), len(passed)...]
  transfers between devices with their start and end apart: 16 -> 16, of which waited for: 5 -> 6; matrix products, arithmetic and copies ran while one was open for 0% -> 0% of each run, Pallas kernels for 34% -> 30%
where the time goes in v5:
time: 47.4 us; the launch traced here: 47.2 us
  starting transfers between devices  21.1 us (45%)
  Pallas kernels  15.5 us (33%)
  waiting for transfers between devices  9.86 us (21%)
  between operations  0.79 us (2%)
    ppermute x15, starting transfers between devices, swapped(): lax.ppermute(value, 'space', [(source, source ^ mask) for source in range...  19.5 us
    pallas_call x14, Pallas kernels, call(): pl.pallas_call(functools.partial(kernel, len(held), len(far), len(passed)...  13.3 us
    ppermute x15, waiting for transfers between devices, swapped(): lax.ppermute(value, 'space', [(source, source ^ mask) for source in range...  9.86 us
    pallas_call x2, Pallas kernels, store(): pl.pallas_call(functools.partial(store_kernel, whose, len(groups)), out_s...  2.22 us
    ppermute x1, starting transfers between devices, turned(): lax.ppermute(value, axis, [(source, (source + steps) % count) for source...  1.53 us
  transfers between devices with their start and end apart: 16, of which 6 were waited for; matrix products, arithmetic and copies ran while one was open for 0% of the time, Pallas kernels for 30%

profile of v5, /device:TPU:0, one launch (start us, length us, event | category | flops | bytes accessed | tf_op | source)
XLA Modules:
  0.0 47.2 jit_solution(1783029996986243893)
XLA Ops:
  0.6 4.1 %collective-permute-start.2 = (f32[2,160,128]{2,1,0:T(8,128)}, f32[2,160,128]{2,1,0:T(8,128)S(1)}, u32[]{:S(2)}, u32[]{:S(2)}) collective-permute-start(f32[2,160,128]{2,1,0:T(8,128)} %bitcast.7), channel_id=1, source_target_pairs={{0,8},{1,9},{2,10},{3,11},{4,12},{5,13},{6,14},{7,15},{8,0},{9,1},... | collective-permute-start | bytes 491528 | tf_op jit(solution)/shard_map/ppermute | solution.py:277
  4.7 1.5 %collective-permute-start.1 = (f32[2,160,128]{2,1,0:T(8,128)}, f32[2,160,128]{2,1,0:T(8,128)S(1)}, u32[]{:S(2)}, u32[]{:S(2)}) collective-permute-start(f32[2,160,128]{2,1,0:T(8,128)} %bitcast.8), channel_id=1, source_target_pairs={{0,2},{1,3},{2,0},{3,1},{4,6},{5,7},{6,4},{7,5},{8,10},{9,11},{10,... | collective-permute-start | bytes 491528 | tf_op jit(solution)/shard_map/ppermute | solution.py:277
  6.2 4.5 %load.1 = (bf16[768,256]{1,0:T(8,128)(2,1)S(1)}, bf16[160,480]{1,0:T(8,128)(2,1)S(1)}, bf16[160,480]{1,0:T(8,128)(2,1)S(1)}, bf16[768,256]{1,0:T(8,128)(2,1)S(1)...) custom-call(bf16[768,256]{1,0:T(8,128)(2,1)} %constant.12.clone.refs, ...), custom_call_target="tpu_custom_call" | custom-call | flops 1000 | bytes 100 | tf_op jit(solution)/shard_map/load/pallas_call | solution.py:84
  10.7 0.1 collective-permute-start
  10.8 1.9 %collective-permute-done.2.refs_1_ = f32[2,160,128]{2,1,0:T(8,128)S(1)} collective-permute-done((f32[2,160,128]{2,1,0:T(8,128)}, f32[2,160,128]{2,1,0:T(8,128)S(1)}, u32[]{:S(2)}, u32[]{:S(2)}) %collective-permute-start.2) | collective-permute-done | bytes 163872 | tf_op jit(solution)/shard_map/ppermute | solution.py:277
  12.7 0.8 %collective-permute-start.4 = (f32[2,160,128]{2,1,0:T(8,128)S(1)}, f32[2,160,128]{2,1,0:T(8,128)S(1)}, u32[]{:S(2)}, u32[]{:S(2)}) collective-permute-start(f32[2,160,128]{2,1,0:T(8,128)S(1)} %get-tuple-element.73.refs_9_), channel_id=1, source_target_pairs={{0,4},{1,5},{2,6},{3,7},{4,0},{5,1},{6,2},{7,3},{8,12},{9,13},{10,... | collective-permute-start | bytes 491528 | tf_op jit(solution)/shard_map/ppermute | solution.py:277
  13.5 1.5 %collective-permute-start.3 = (f32[2,160,128]{2,1,0:T(8,128)S(1)}, f32[2,160,128]{2,1,0:T(8,128)S(1)}, u32[]{:S(2)}, u32[]{:S(2)}) collective-permute-start(f32[2,160,128]{2,1,0:T(8,128)S(1)} %get-tuple-element.73.refs_9_), channel_id=1, source_target_pairs={{0,2},{1,3},{2,0},{3,1},{4,6},{5,7},{6,4},{7,5},{8,10},{9,11},{10,... | collective-permute-start | bytes 491528 | tf_op jit(solution)/shard_map/ppermute | solution.py:277
  15.0 0.7 %collective-permute-done.refs_1_ = f32[2,8,2,160,128]{4,3,2,1,0:T(8,128)S(1)} collective-permute-done((f32[2,8,2,160,128]{4,3,2,1,0:T(8,128)S(1)}, f32[2,8,2,160,128]{4,3,2,1,0:T(8,128)S(1)}, u32[]{:S(2)}, u32[]{:S(2)}) %collective-permute-start) | collective-permute-done | bytes 2621472 | tf_op jit(solution)/shard_map/ppermute | solution.py:277
  15.7 1.8 %coils.4 = (f32[2,160,128]{2,1,0:T(8,128)S(1)}, f32[2,160,128]{2,1,0:T(8,128)S(1)}, f32[2,2,160,128]{3,2,1,0:T(8,128)S(1)}, f32[2,2,160,128]{3,2,1,0:T(8,128)S(1...) custom-call(f32[2,8,2,160,128]{4,3,2,1,0:T(8,128)S(1)} %get-tuple-element.60.refs_0_, ...), custom_call_target="tpu_custom_call", output_to_operand_aliasing={{5}: (11, {})} | custom-call | flops 100000000 | bytes 100 | tf_op jit(solution)/shard_map/coils/pallas_call | solution.py:84
  17.5 1.6 %collective-permute-start.6 = (f32[2,2,160,128]{3,2,1,0:T(8,128)S(1)}, f32[2,2,160,128]{3,2,1,0:T(8,128)S(1)}, u32[]{:S(2)}, u32[]{:S(2)}) collective-permute-start(f32[2,2,160,128]{3,2,1,0:T(8,128)S(1)} %get-tuple-element.79), channel_id=1, source_target_pairs={{0,4},{1,5},{2,6},{3,7},{4,0},{5,1},{6,2},{7,3},{8,12},{9,13},{10,... | collective-permute-start | bytes 983048 | tf_op jit(solution)/shard_map/ppermute | solution.py:277
  19.1 0.5 %collective-permute-start.7 = (f32[2,160,128]{2,1,0:T(8,128)S(1)}, f32[2,160,128]{2,1,0:T(8,128)S(1)}, u32[]{:S(2)}, u32[]{:S(2)}) collective-permute-start(f32[2,160,128]{2,1,0:T(8,128)S(1)} %get-tuple-element.80.refs_9_), channel_id=1, source_target_pairs={{0,2},{1,3},{2,0},{3,1},{4,6},{5,7},{6,4},{7,5},{8,10},{9,11},{10,... | collective-permute-start | bytes 491528 | tf_op jit(solution)/shard_map/ppermute | solution.py:277
  19.7 0.0 collective-permute-done.3.refs_10_
  19.7 1.8 %coils.5 = (f32[2,160,128]{2,1,0:T(8,128)S(1)}, f32[2,160,128]{2,1,0:T(8,128)S(1)}, f32[2,2,160,128]{3,2,1,0:T(8,128)S(1)}, f32[8,2,160,128]{3,2,1,0:T(8,128)S(1)}, f32[8,128]{1,0:T(8,128)S(1)}) custom-call(f32[2,8,2,160,128]{4,3,2,1,0:T(8,128)S(1)} %get-tuple-element.60.refs_0_, ...), custom_call_target="tpu_custom_call", output_to_operand_aliasing={{4}: (12, {}), {3}: (11, {})} | custom-call | flops 100000000 | bytes 100 | tf_op jit(solution)/shard_map/coils/pallas_call | solution.py:84
  21.5 1.6 %collective-permute-start.5 = (f32[2,160,128]{2,1,0:T(8,128)S(1)}, f32[2,160,128]{2,1,0:T(8,128)S(1)}, u32[]{:S(2)}, u32[]{:S(2)}) collective-permute-start(f32[2,160,128]{2,1,0:T(8,128)S(1)} %get-tuple-element.78), channel_id=1, source_target_pairs={{0,2},{1,3},{2,0},{3,1},{4,6},{5,7},{6,4},{7,5},{8,10},{9,11},{10,... | collective-permute-start | bytes 491528 | tf_op jit(solution)/shard_map/ppermute | solution.py:277
  23.1 1.5 %collective-permute-start.9 = (f32[4,160,128]{2,1,0:T(8,128)S(1)}, f32[4,160,128]{2,1,0:T(8,128)S(1)}, u32[]{:S(2)}, u32[]{:S(2)}) collective-permute-start(f32[4,160,128]{2,1,0:T(8,128)S(1)} %get-tuple-element.93.refs_1_), channel_id=1, source_target_pairs={{0,16},{16,0},{1,17},{17,1},{2,18},{18,2},{3,19},{19,3},{4,20},{20... | collective-permute-start | bytes 983048 | tf_op jit(solution)/shard_map/ppermute | solution.py:272
  24.6 1.7 %collective-permute-done.7.refs_10_ = f32[2,160,128]{2,1,0:T(8,128)S(1)} collective-permute-done((f32[2,160,128]{2,1,0:T(8,128)S(1)}, f32[2,160,128]{2,1,0:T(8,128)S(1)}, u32[]{:S(2)}, u32[]{:S(2)}) %collective-permute-start.7) | collective-permute-done | bytes 163872 | tf_op jit(solution)/shard_map/ppermute | solution.py:277
  26.2 1.8 %coils.6 = (f32[2,160,128]{2,1,0:T(8,128)S(1)}, f32[2,160,128]{2,1,0:T(8,128)S(1)}, f32[2,2,160,128]{3,2,1,0:T(8,128)S(1)}, f32[8,2,160,128]{3,2,1,0:T(8,128)S(1)}, f32[8,128]{1,0:T(8,128)S(1)}) custom-call(f32[2,8,2,160,128]{4,3,2,1,0:T(8,128)S(1)} %get-tuple-element.60.refs_0_, ...), custom_call_target="tpu_custom_call", output_to_operand_aliasing={{4}: (12, {}), {3}: (11, {})} | custom-call | flops 100000000 | bytes 100 | tf_op jit(solution)/shard_map/coils/pallas_call | solution.py:84
  28.0 0.1 collective-permute-start.11
  28.1 1.8 %coils.7 = (f32[2,160,128]{2,1,0:T(8,128)S(1)}, f32[2,160,128]{2,1,0:T(8,128)S(1)}, f32[2,2,160,128]{3,2,1,0:T(8,128)S(1)}, f32[8,2,160,128]{3,2,1,0:T(8,128)S(1)}, f32[8,128]{1,0:T(8,128)S(1)}) custom-call(f32[2,8,2,160,128]{4,3,2,1,0:T(8,128)S(1)} %get-tuple-element.60.refs_0_, ...), custom_call_target="tpu_custom_call", output_to_operand_aliasing={{4}: (11, {}), {3}: (10, {})} | custom-call | flops 100000000 | bytes 100 | tf_op jit(solution)/shard_map/coils/pallas_call | solution.py:84
  30.0 2.1 %collective-permute-start.10 = (f32[2,160,128]{2,1,0:T(8,128)S(1)}, f32[2,160,128]{2,1,0:T(8,128)S(1)}, u32[]{:S(2)}, u32[]{:S(2)}) collective-permute-start(f32[2,160,128]{2,1,0:T(8,128)S(1)} %get-tuple-element.95), channel_id=1, source_target_pairs={{0,2},{1,3},{2,0},{3,1},{4,6},{5,7},{6,4},{7,5},{8,10},{9,11},{10,... | collective-permute-start | bytes 491528 | tf_op jit(solution)/shard_map/ppermute | solution.py:277
  32.1 1.3 %collective-permute-start.8 = (f32[2,160,128]{2,1,0:T(8,128)S(1)}, f32[2,160,128]{2,1,0:T(8,128)S(1)}, u32[]{:S(2)}, u32[]{:S(2)}) collective-permute-start(f32[2,160,128]{2,1,0:T(8,128)S(1)} %get-tuple-element.87), channel_id=1, source_target_pairs={{0,8},{1,9},{2,10},{3,11},{4,12},{5,13},{6,14},{7,15},{8,0},{9,1},... | collective-permute-start | bytes 491528 | tf_op jit(solution)/shard_map/ppermute | solution.py:277
  33.3 1.3 %collective-permute-done.11.refs_1_ = f32[2,160,128]{2,1,0:T(8,128)S(1)} collective-permute-done((f32[2,160,128]{2,1,0:T(8,128)S(1)}, f32[2,160,128]{2,1,0:T(8,128)S(1)}, u32[]{:S(2)}, u32[]{:S(2)}) %collective-permute-start.11) | collective-permute-done | bytes 163872 | tf_op jit(solution)/shard_map/ppermute | solution.py:277
  34.7 2.8 %collective-permute-start.12 = (f32[2,160,128]{2,1,0:T(8,128)S(1)}, f32[2,160,128]{2,1,0:T(8,128)S(1)}, u32[]{:S(2)}, u32[]{:S(2)}) collective-permute-start(f32[2,160,128]{2,1,0:T(8,128)S(1)} %get-tuple-element.104), channel_id=1, source_target_pairs={{0,12},{1,13},{2,14},{3,15},{4,8},{5,9},{6,10},{7,11},{8,4},{9,5},... | collective-permute-start | bytes 491528 | tf_op jit(solution)/shard_map/ppermute | solution.py:277
  37.5 1.5 %collective-permute-start.14 = (f32[2,160,128]{2,1,0:T(8,128)S(1)}, f32[2,160,128]{2,1,0:T(8,128)S(1)}, u32[]{:S(2)}, u32[]{:S(2)}) collective-permute-start(f32[2,160,128]{2,1,0:T(8,128)S(1)} %get-tuple-element.108), channel_id=1, source_target_pairs={{0,2},{1,3},{2,0},{3,1},{4,6},{5,7},{6,4},{7,5},{8,10},{9,11},{10,... | collective-permute-start | bytes 491528 | tf_op jit(solution)/shard_map/ppermute | solution.py:277
  39.0 0.1 collective-permute-start.13
  39.1 0.1 collective-permute-start.15
  39.2 0.8 %temporal.1 = (f32[2,160,128]{2,1,0:T(8,128)}, f32[2,160,128]{2,1,0:T(8,128)S(1)}, f32[8,128]{1,0:T(8,128)S(1)}) custom-call(f32[2,160,128]{2,1,0:T(8,128)S(1)} %get-tuple-element.92.refs_0_, f32[4,160,128]{2,1,0:T(8,128)S(1)} %get-tuple-element.93.refs_1_, f32[4,160,128]{2,1,0:T(8,128)S(1)} %collective-permute-done.9.refs_2_, ...), custom_call_target="tpu_custom_call", output_to_operand_aliasing={{2}: (3, {})} | custom-call | flops 50000 | bytes 100 | tf_op jit(solution)/shard_map/temporal/pallas_call | solution.py:84
  39.9 1.1 %store.2 = (f32[2,1,1,16,160,128]{5,4,3,2,1,0:T(8,128)}, f32[8,128]{1,0:T(8,128)S(1)}) custom-call(f32[2,2,160,128]{3,2,1,0:T(8,128)S(1)} %get-tuple-element.88.refs_0_, f32[2,2,160,128]{3,2,1,0:T(8,128)S(1)} %get-tuple-element.89.refs_1_, f32[2,2,160,128]{3,2,1,0:T(8,128)S(1)} %get-tuple-element.90.refs_2_, ...), custom_call_target="tpu_custom_call", output_to_operand_aliasing={{1}: (4, {})} | custom-call | flops 1000 | bytes 100 | tf_op jit(solution)/shard_map/store/pallas_call | solution.py:323
  41.0 3.1 %collective-permute-done.8.refs_1_ = f32[2,160,128]{2,1,0:T(8,128)S(1)} collective-permute-done((f32[2,160,128]{2,1,0:T(8,128)S(1)}, f32[2,160,128]{2,1,0:T(8,128)S(1)}, u32[]{:S(2)}, u32[]{:S(2)}) %collective-permute-start.8) | collective-permute-done | bytes 163872 | tf_op jit(solution)/shard_map/ppermute | solution.py:277
  44.2 1.2 %collective-permute-done.13.refs_1_ = f32[2,160,128]{2,1,0:T(8,128)S(1)} collective-permute-done((f32[2,160,128]{2,1,0:T(8,128)S(1)}, f32[2,160,128]{2,1,0:T(8,128)S(1)}, u32[]{:S(2)}, u32[]{:S(2)}) %collective-permute-start.13) | collective-permute-done | bytes 163872 | tf_op jit(solution)/shard_map/ppermute | solution.py:277
  45.4 0.7 %sums.11 = (f32[2,160,128]{2,1,0:T(8,128)}, f32[8,128]{1,0:T(8,128)S(1)}) custom-call(f32[2,160,128]{2,1,0:T(8,128)S(1)} %get-tuple-element.106.refs_0_, f32[2,160,128]{2,1,0:T(8,128)S(1)} %collective-permute-done.13.refs_1_, f32[2,160,128]{2,1,0:T(8,128)S(1)} %collective-permute-done.14.refs_2_, ...), custom_call_target="tpu_custom_call", output_to_operand_aliasing={{1}: (4, {})} | custom-call | flops 20000000000 | bytes 100 | tf_op jit(solution)/shard_map/sums/pallas_call | solution.py:84
  46.1 1.1 %store.3 = (f32[2,1,1,16,160,128]{5,4,3,2,1,0:T(8,128)}, f32[8,128]{1,0:T(8,128)S(1)}) custom-call(f32[8,2,160,128]{3,2,1,0:T(8,128)S(1)} %collective-permute-done.15.refs_0_, f32[2,1,1,16,160,128]{5,4,3,2,1,0:T(8,128)} %get-tuple-element.114.refs_1_, f32[8,128]{1,0:T(8,128)S(1)} %get-tuple-element.115.refs_2_), custom_call_target="tpu_custom_call", output_to_operand_aliasing={{0}: (1, {}), {1}: (2, {})} | custom-call | flops 1000 | bytes 100 | tf_op jit(solution)/shard_map/store/pallas_call | solution.py:323
  (16 shorter events, 0.1 us)
Async XLA Ops:
  0.6 12.0 %collective-permute-start.2 = (f32[2,160,128]{2,1,0:T(8,128)}, f32[2,160,128]{2,1,0:T(8,128)S(1)}, u32[]{:S(2)}, u32[]{:S(2)}) collective-permute-start(f32[2,160,128]{2,1,0:T(8,128)} %bitcast.7), channel_id=1, source_target_pairs={{0,8},{1,9},{2,10},{3,11},{4,12},{5,13},{6,14},{7,15},{8,0},{9,1},... | collective-permute-start | bytes 491528 | tf_op jit(solution)/shard_map/ppermute | solution.py:277
  4.7 10.2 %collective-permute-start.1 = (f32[2,160,128]{2,1,0:T(8,128)}, f32[2,160,128]{2,1,0:T(8,128)S(1)}, u32[]{:S(2)}, u32[]{:S(2)}) collective-permute-start(f32[2,160,128]{2,1,0:T(8,128)} %bitcast.8), channel_id=1, source_target_pairs={{0,2},{1,3},{2,0},{3,1},{4,6},{5,7},{6,4},{7,5},{8,10},{9,11},{10,... | collective-permute-start | bytes 491528 | tf_op jit(solution)/shard_map/ppermute | solution.py:277
  10.7 5.0 %collective-permute-start = (f32[2,8,2,160,128]{4,3,2,1,0:T(8,128)S(1)}, f32[2,8,2,160,128]{4,3,2,1,0:T(8,128)S(1)}, u32[]{:S(2)}, u32[]{:S(2)}) collective-permute-start(f32[2,8,2,160,128]{4,3,2,1,0:T(8,128)S(1)} %get-tuple-element.61), channel_id=1, source_target_pairs={{0,1},{1,0},{2,3},{3,2},{4,5},{5,4},{6,7},{7,6},{8,9},{9,8},{10,11... | collective-permute-start | bytes 7864328 | tf_op jit(solution)/shard_map/ppermute | solution.py:277
  12.7 6.5 %collective-permute-start.4 = (f32[2,160,128]{2,1,0:T(8,128)S(1)}, f32[2,160,128]{2,1,0:T(8,128)S(1)}, u32[]{:S(2)}, u32[]{:S(2)}) collective-permute-start(f32[2,160,128]{2,1,0:T(8,128)S(1)} %get-tuple-element.73.refs_9_), channel_id=1, source_target_pairs={{0,4},{1,5},{2,6},{3,7},{4,0},{5,1},{6,2},{7,3},{8,12},{9,13},{10,... | collective-permute-start | bytes 491528 | tf_op jit(solution)/shard_map/ppermute | solution.py:277
  13.5 6.2 %collective-permute-start.3 = (f32[2,160,128]{2,1,0:T(8,128)S(1)}, f32[2,160,128]{2,1,0:T(8,128)S(1)}, u32[]{:S(2)}, u32[]{:S(2)}) collective-permute-start(f32[2,160,128]{2,1,0:T(8,128)S(1)} %get-tuple-element.73.refs_9_), channel_id=1, source_target_pairs={{0,2},{1,3},{2,0},{3,1},{4,6},{5,7},{6,4},{7,5},{8,10},{9,11},{10,... | collective-permute-start | bytes 491528 | tf_op jit(solution)/shard_map/ppermute | solution.py:277
  17.5 10.6 %collective-permute-start.6 = (f32[2,2,160,128]{3,2,1,0:T(8,128)S(1)}, f32[2,2,160,128]{3,2,1,0:T(8,128)S(1)}, u32[]{:S(2)}, u32[]{:S(2)}) collective-permute-start(f32[2,2,160,128]{3,2,1,0:T(8,128)S(1)} %get-tuple-element.79), channel_id=1, source_target_pairs={{0,4},{1,5},{2,6},{3,7},{4,0},{5,1},{6,2},{7,3},{8,12},{9,13},{10,... | collective-permute-start | bytes 983048 | tf_op jit(solution)/shard_map/ppermute | solution.py:277
  19.1 7.1 %collective-permute-start.7 = (f32[2,160,128]{2,1,0:T(8,128)S(1)}, f32[2,160,128]{2,1,0:T(8,128)S(1)}, u32[]{:S(2)}, u32[]{:S(2)}) collective-permute-start(f32[2,160,128]{2,1,0:T(8,128)S(1)} %get-tuple-element.80.refs_9_), channel_id=1, source_target_pairs={{0,2},{1,3},{2,0},{3,1},{4,6},{5,7},{6,4},{7,5},{8,10},{9,11},{10,... | collective-permute-start | bytes 491528 | tf_op jit(solution)/shard_map/ppermute | solution.py:277
  21.5 8.5 %collective-permute-start.5 = (f32[2,160,128]{2,1,0:T(8,128)S(1)}, f32[2,160,128]{2,1,0:T(8,128)S(1)}, u32[]{:S(2)}, u32[]{:S(2)}) collective-permute-start(f32[2,160,128]{2,1,0:T(8,128)S(1)} %get-tuple-element.78), channel_id=1, source_target_pairs={{0,2},{1,3},{2,0},{3,1},{4,6},{5,7},{6,4},{7,5},{8,10},{9,11},{10,... | collective-permute-start | bytes 491528 | tf_op jit(solution)/shard_map/ppermute | solution.py:277
  23.1 16.0 %collective-permute-start.9 = (f32[4,160,128]{2,1,0:T(8,128)S(1)}, f32[4,160,128]{2,1,0:T(8,128)S(1)}, u32[]{:S(2)}, u32[]{:S(2)}) collective-permute-start(f32[4,160,128]{2,1,0:T(8,128)S(1)} %get-tuple-element.93.refs_1_), channel_id=1, source_target_pairs={{0,16},{16,0},{1,17},{17,1},{2,18},{18,2},{3,19},{19,3},{4,20},{20... | collective-permute-start | bytes 983048 | tf_op jit(solution)/shard_map/ppermute | solution.py:272
  28.0 6.6 %collective-permute-start.11 = (f32[2,160,128]{2,1,0:T(8,128)S(1)}, f32[2,160,128]{2,1,0:T(8,128)S(1)}, u32[]{:S(2)}, u32[]{:S(2)}) collective-permute-start(f32[2,160,128]{2,1,0:T(8,128)S(1)} %get-tuple-element.97), channel_id=1, source_target_pairs={{0,2},{1,3},{2,0},{3,1},{4,6},{5,7},{6,4},{7,5},{8,10},{9,11},{10,... | collective-permute-start | bytes 491528 | tf_op jit(solution)/shard_map/ppermute | solution.py:277
  30.0 9.0 %collective-permute-start.10 = (f32[2,160,128]{2,1,0:T(8,128)S(1)}, f32[2,160,128]{2,1,0:T(8,128)S(1)}, u32[]{:S(2)}, u32[]{:S(2)}) collective-permute-start(f32[2,160,128]{2,1,0:T(8,128)S(1)} %get-tuple-element.95), channel_id=1, source_target_pairs={{0,2},{1,3},{2,0},{3,1},{4,6},{5,7},{6,4},{7,5},{8,10},{9,11},{10,... | collective-permute-start | bytes 491528 | tf_op jit(solution)/shard_map/ppermute | solution.py:277
  32.1 12.1 %collective-permute-start.8 = (f32[2,160,128]{2,1,0:T(8,128)S(1)}, f32[2,160,128]{2,1,0:T(8,128)S(1)}, u32[]{:S(2)}, u32[]{:S(2)}) collective-permute-start(f32[2,160,128]{2,1,0:T(8,128)S(1)} %get-tuple-element.87), channel_id=1, source_target_pairs={{0,8},{1,9},{2,10},{3,11},{4,12},{5,13},{6,14},{7,15},{8,0},{9,1},... | collective-permute-start | bytes 491528 | tf_op jit(solution)/shard_map/ppermute | solution.py:277
  34.7 9.5 %collective-permute-start.12 = (f32[2,160,128]{2,1,0:T(8,128)S(1)}, f32[2,160,128]{2,1,0:T(8,128)S(1)}, u32[]{:S(2)}, u32[]{:S(2)}) collective-permute-start(f32[2,160,128]{2,1,0:T(8,128)S(1)} %get-tuple-element.104), channel_id=1, source_target_pairs={{0,12},{1,13},{2,14},{3,15},{4,8},{5,9},{6,10},{7,11},{8,4},{9,5},... | collective-permute-start | bytes 491528 | tf_op jit(solution)/shard_map/ppermute | solution.py:277
  37.5 6.8 %collective-permute-start.14 = (f32[2,160,128]{2,1,0:T(8,128)S(1)}, f32[2,160,128]{2,1,0:T(8,128)S(1)}, u32[]{:S(2)}, u32[]{:S(2)}) collective-permute-start(f32[2,160,128]{2,1,0:T(8,128)S(1)} %get-tuple-element.108), channel_id=1, source_target_pairs={{0,2},{1,3},{2,0},{3,1},{4,6},{5,7},{6,4},{7,5},{8,10},{9,11},{10,... | collective-permute-start | bytes 491528 | tf_op jit(solution)/shard_map/ppermute | solution.py:277
  39.0 6.4 %collective-permute-start.13 = (f32[2,160,128]{2,1,0:T(8,128)S(1)}, f32[2,160,128]{2,1,0:T(8,128)S(1)}, u32[]{:S(2)}, u32[]{:S(2)}) collective-permute-start(f32[2,160,128]{2,1,0:T(8,128)S(1)} %get-tuple-element.107), channel_id=1, source_target_pairs={{0,4},{1,5},{2,6},{3,7},{4,0},{5,1},{6,2},{7,3},{8,12},{9,13},{10,... | collective-permute-start | bytes 491528 | tf_op jit(solution)/shard_map/ppermute | solution.py:277
  39.1 7.0 %collective-permute-start.15 = (f32[8,2,160,128]{3,2,1,0:T(8,128)S(1)}, f32[8,2,160,128]{3,2,1,0:T(8,128)S(1)}, u32[]{:S(2)}, u32[]{:S(2)}) collective-permute-start(f32[8,2,160,128]{3,2,1,0:T(8,128)S(1)} %get-tuple-element.113), channel_id=1, source_target_pairs={{0,1},{1,0},{2,3},{3,2},{4,5},{5,4},{6,7},{7,6},{8,9},{9,8},{10,11... | collective-permute-start | bytes 3932168 | tf_op jit(solution)/shard_map/ppermute | solution.py:277

commit v6 on v5

--- a/solution.py
+++ b/solution.py
@@ -253,16 +253,21 @@
         target[part] = values[-1][part] - primal_step * total if begun else total
 
 
-def store_kernel(other, count, *refs):
-    groups, data_new, sems = refs[:count], refs[-3], refs[-1]
+def store_kernel(other, count, extra, *refs):
+    groups, values = refs[:count], refs[len(refs) - 3 - 2 * extra:len(refs) - 3 - extra]
+    data_new, targets, sems = refs[-3 - extra], refs[-1 - extra:-1], refs[-1]
     place = placed()
-    stores = []
+    stores = [
+        pltpu.make_async_copy(value, target, sems.at[sems.shape[0] - 1 - n])
+        for n, (value, target) in enumerate(zip(values, targets))
+    ]
     for g, group in enumerate(groups):
         for n in range(group.shape[0]):
             offset = g * group.shape[0] + n
             plane = 2 * jnp.bitwise_xor(place[0], offset) + jnp.bitwise_xor(place[1], other)
             stores.append(pltpu.make_async_copy(group.at[n], data_new.at[:, 0, 0, plane], sems.at[offset]))
-            stores[-1].start()
+    for store in stores:
+        store.start()
     for store in stores:
         store.wait()
 
@@ -317,17 +322,18 @@
     pair_before = turned(pair, "tm", 1)
     later = [] if frame_total == 2 else [turned(blocks[0], "tm", -1)]
 
-    def store(name, whose, groups, before, token):
+    def store(name, whose, groups, before, token, *extra):
         operands = [pltpu.with_memory_space_constraint(value, pltpu.VMEM) for value in groups]
         operands += [pltpu.with_memory_space_constraint(value, pltpu.HBM) for value in before] + [token]
+        operands += [pltpu.with_memory_space_constraint(value, pltpu.VMEM) for value in extra]
         return pl.pallas_call(
-            functools.partial(store_kernel, whose, len(groups)),
+            functools.partial(store_kernel, whose, len(groups), len(extra)),
             out_shape=[
                 jax.ShapeDtypeStruct(kspace.shape, jnp.float32), jax.ShapeDtypeStruct(token.shape, token.dtype)
-            ],
-            in_specs=[vmem] * len(groups) + [hbm] * len(before) + [anywhere],
-            out_specs=[hbm, anywhere],
-            scratch_shapes=[pltpu.SemaphoreType.DMA((chips,))],
+            ] + [jax.ShapeDtypeStruct(value.shape, value.dtype) for value in extra],
+            in_specs=[vmem] * len(groups) + [hbm] * len(before) + [anywhere] + [vmem] * len(extra),
+            out_specs=[hbm, anywhere] + [hbm] * len(extra),
+            scratch_shapes=[pltpu.SemaphoreType.DMA((chips + len(extra),))],
             input_output_aliases={len(groups) + n: n for n in (range(2) if before else ())} or {len(groups): 1},
             compiler_params=pltpu.CompilerParams(vmem_limit_bytes=2 * mebi),
             cost_estimate=pl.CostEstimate(flops=1_000, bytes_accessed=100, transcendentals=0),
@@ -382,10 +388,10 @@
     total, token = sums([totals[0][0], from_2], [token], 100000)
     total, token = sums([total, from_3], [token], 50000)
     (image_new,), (token,) = call(
-        "sums", functools.partial(sum_kernel, 1), [total, from_1, *beside(0), begin], [], [token], [result], [],
+        "sums", functools.partial(sum_kernel, 1), [total, from_1, *beside(0), begin], [], [token], [block], [],
         20_000_000, 2,
     )
-    data_new, _ = store("store", 1, [swapped(new_other[0], 1)], [data_new], token)
+    data_new, _, image_new = store("store", 1, [swapped(new_other[0], 1)], [data_new], token, image_new)
     return (image_new[:, None], tv_here[:, None], data_new)
 
 

time: 47.4 us -> 46.8 us (0.987)
  Pallas kernels: 15.5 us -> 14.9 us
    pallas_call x14, Pallas kernels: 13.3 us -> 12.6 us  [call(): pl.pallas_call(functools.partial(kernel, len(held), len(far), len(passed)...]
  transfers between devices with their start and end apart: 16 -> 16, of which waited for: 6 -> 6; matrix products, arithmetic and copies ran while one was open for 0% -> 0% of each run, Pallas kernels for 30% -> 29%
where the time goes in v6:
time: 46.8 us; the launch traced here: 46.6 us
  starting transfers between devices  21.1 us (45%)
  Pallas kernels  14.9 us (32%)
  waiting for transfers between devices  9.86 us (21%)
  between operations  0.8 us (2%)
    ppermute x15, starting transfers between devices, swapped(): lax.ppermute(value, 'space', [(source, source ^ mask) for source in range...  19.5 us
    pallas_call x14, Pallas kernels, call(): pl.pallas_call(functools.partial(kernel, len(held), len(far), len(passed)...  12.6 us
    ppermute x15, waiting for transfers between devices, swapped(): lax.ppermute(value, 'space', [(source, source ^ mask) for source in range...  9.86 us
    pallas_call x2, Pallas kernels, store(): pl.pallas_call(functools.partial(store_kernel, whose, len(groups), len(ex...  2.29 us
    ppermute x1, starting transfers between devices, turned(): lax.ppermute(value, axis, [(source, (source + steps) % count) for source...  1.52 us
  transfers between devices with their start and end apart: 16, of which 6 were waited for; matrix products, arithmetic and copies ran while one was open for 0% of the time, Pallas kernels for 29%

profile of v6, /device:TPU:0, one launch (start us, length us, event | category | flops | bytes accessed | tf_op | source)
XLA Modules:
  0.0 46.6 jit_solution(3144139252549347119)
XLA Ops:
  0.6 4.1 %collective-permute-start.2 = (f32[2,160,128]{2,1,0:T(8,128)}, f32[2,160,128]{2,1,0:T(8,128)S(1)}, u32[]{:S(2)}, u32[]{:S(2)}) collective-permute-start(f32[2,160,128]{2,1,0:T(8,128)} %bitcast.7), channel_id=1, source_target_pairs={{0,8},{1,9},{2,10},{3,11},{4,12},{5,13},{6,14},{7,15},{8,0},{9,1},... | collective-permute-start | bytes 491528 | tf_op jit(solution)/shard_map/ppermute | solution.py:282
  4.7 1.5 %collective-permute-start.1 = (f32[2,160,128]{2,1,0:T(8,128)}, f32[2,160,128]{2,1,0:T(8,128)S(1)}, u32[]{:S(2)}, u32[]{:S(2)}) collective-permute-start(f32[2,160,128]{2,1,0:T(8,128)} %bitcast.8), channel_id=1, source_target_pairs={{0,2},{1,3},{2,0},{3,1},{4,6},{5,7},{6,4},{7,5},{8,10},{9,11},{10,... | collective-permute-start | bytes 491528 | tf_op jit(solution)/shard_map/ppermute | solution.py:282
  6.2 4.5 %load.1 = (bf16[768,256]{1,0:T(8,128)(2,1)S(1)}, bf16[160,480]{1,0:T(8,128)(2,1)S(1)}, bf16[160,480]{1,0:T(8,128)(2,1)S(1)}, bf16[768,256]{1,0:T(8,128)(2,1)S(1)...) custom-call(bf16[768,256]{1,0:T(8,128)(2,1)} %constant.12.clone.refs, ...), custom_call_target="tpu_custom_call" | custom-call | flops 1000 | bytes 100 | tf_op jit(solution)/shard_map/load/pallas_call | solution.py:84
  10.7 0.1 collective-permute-start
  10.8 1.9 %collective-permute-done.2.refs_1_ = f32[2,160,128]{2,1,0:T(8,128)S(1)} collective-permute-done((f32[2,160,128]{2,1,0:T(8,128)}, f32[2,160,128]{2,1,0:T(8,128)S(1)}, u32[]{:S(2)}, u32[]{:S(2)}) %collective-permute-start.2) | collective-permute-done | bytes 163872 | tf_op jit(solution)/shard_map/ppermute | solution.py:282
  12.7 0.8 %collective-permute-start.4 = (f32[2,160,128]{2,1,0:T(8,128)S(1)}, f32[2,160,128]{2,1,0:T(8,128)S(1)}, u32[]{:S(2)}, u32[]{:S(2)}) collective-permute-start(f32[2,160,128]{2,1,0:T(8,128)S(1)} %get-tuple-element.75.refs_9_), channel_id=1, source_target_pairs={{0,4},{1,5},{2,6},{3,7},{4,0},{5,1},{6,2},{7,3},{8,12},{9,13},{10,... | collective-permute-start | bytes 491528 | tf_op jit(solution)/shard_map/ppermute | solution.py:282
  13.5 1.5 %collective-permute-start.6 = (f32[2,160,128]{2,1,0:T(8,128)S(1)}, f32[2,160,128]{2,1,0:T(8,128)S(1)}, u32[]{:S(2)}, u32[]{:S(2)}) collective-permute-start(f32[2,160,128]{2,1,0:T(8,128)S(1)} %get-tuple-element.75.refs_9_), channel_id=1, source_target_pairs={{0,2},{1,3},{2,0},{3,1},{4,6},{5,7},{6,4},{7,5},{8,10},{9,11},{10,... | collective-permute-start | bytes 491528 | tf_op jit(solution)/shard_map/ppermute | solution.py:282
  15.0 0.0 collective-permute-done.1.refs_10_
  15.0 0.7 %collective-permute-done.refs_1_ = f32[2,8,2,160,128]{4,3,2,1,0:T(8,128)S(1)} collective-permute-done((f32[2,8,2,160,128]{4,3,2,1,0:T(8,128)S(1)}, f32[2,8,2,160,128]{4,3,2,1,0:T(8,128)S(1)}, u32[]{:S(2)}, u32[]{:S(2)}) %collective-permute-start) | collective-permute-done | bytes 2621472 | tf_op jit(solution)/shard_map/ppermute | solution.py:282
  15.7 1.8 %coils.4 = (f32[2,160,128]{2,1,0:T(8,128)S(1)}, f32[2,160,128]{2,1,0:T(8,128)S(1)}, f32[2,2,160,128]{3,2,1,0:T(8,128)S(1)}, f32[2,2,160,128]{3,2,1,0:T(8,128)S(1...) custom-call(f32[2,8,2,160,128]{4,3,2,1,0:T(8,128)S(1)} %get-tuple-element.61.refs_0_, ...), custom_call_target="tpu_custom_call", output_to_operand_aliasing={{5}: (11, {})} | custom-call | flops 100000000 | bytes 100 | tf_op jit(solution)/shard_map/coils/pallas_call | solution.py:84
  17.5 1.6 %collective-permute-start.3 = (f32[2,2,160,128]{3,2,1,0:T(8,128)S(1)}, f32[2,2,160,128]{3,2,1,0:T(8,128)S(1)}, u32[]{:S(2)}, u32[]{:S(2)}) collective-permute-start(f32[2,2,160,128]{3,2,1,0:T(8,128)S(1)} %get-tuple-element.73), channel_id=1, source_target_pairs={{0,4},{1,5},{2,6},{3,7},{4,0},{5,1},{6,2},{7,3},{8,12},{9,13},{10,... | collective-permute-start | bytes 983048 | tf_op jit(solution)/shard_map/ppermute | solution.py:282
  19.1 0.0 collective-permute-done.4.refs_1_
  19.1 0.5 %collective-permute-start.5 = (f32[2,160,128]{2,1,0:T(8,128)S(1)}, f32[2,160,128]{2,1,0:T(8,128)S(1)}, u32[]{:S(2)}, u32[]{:S(2)}) collective-permute-start(f32[2,160,128]{2,1,0:T(8,128)S(1)} %get-tuple-element.76.refs_9_), channel_id=1, source_target_pairs={{0,2},{1,3},{2,0},{3,1},{4,6},{5,7},{6,4},{7,5},{8,10},{9,11},{10,... | collective-permute-start | bytes 491528 | tf_op jit(solution)/shard_map/ppermute | solution.py:282
  19.7 1.8 %coils.5 = (f32[2,160,128]{2,1,0:T(8,128)S(1)}, f32[2,160,128]{2,1,0:T(8,128)S(1)}, f32[2,2,160,128]{3,2,1,0:T(8,128)S(1)}, f32[8,2,160,128]{3,2,1,0:T(8,128)S(1)}, f32[8,128]{1,0:T(8,128)S(1)}) custom-call(f32[2,8,2,160,128]{4,3,2,1,0:T(8,128)S(1)} %get-tuple-element.61.refs_0_, ...), custom_call_target="tpu_custom_call", output_to_operand_aliasing={{4}: (12, {}), {3}: (11, {})} | custom-call | flops 100000000 | bytes 100 | tf_op jit(solution)/shard_map/coils/pallas_call | solution.py:84
  21.5 1.6 %collective-permute-start.9 = (f32[2,160,128]{2,1,0:T(8,128)S(1)}, f32[2,160,128]{2,1,0:T(8,128)S(1)}, u32[]{:S(2)}, u32[]{:S(2)}) collective-permute-start(f32[2,160,128]{2,1,0:T(8,128)S(1)} %get-tuple-element.92), channel_id=1, source_target_pairs={{0,2},{1,3},{2,0},{3,1},{4,6},{5,7},{6,4},{7,5},{8,10},{9,11},{10,... | collective-permute-start | bytes 491528 | tf_op jit(solution)/shard_map/ppermute | solution.py:282
  23.1 1.5 %collective-permute-start.8 = (f32[4,160,128]{2,1,0:T(8,128)S(1)}, f32[4,160,128]{2,1,0:T(8,128)S(1)}, u32[]{:S(2)}, u32[]{:S(2)}) collective-permute-start(f32[4,160,128]{2,1,0:T(8,128)S(1)} %get-tuple-element.89.refs_1_), channel_id=1, source_target_pairs={{0,16},{16,0},{1,17},{17,1},{2,18},{18,2},{3,19},{19,3},{4,20},{20... | collective-permute-start | bytes 983048 | tf_op jit(solution)/shard_map/ppermute | solution.py:277
  24.6 1.7 %collective-permute-done.5.refs_10_ = f32[2,160,128]{2,1,0:T(8,128)S(1)} collective-permute-done((f32[2,160,128]{2,1,0:T(8,128)S(1)}, f32[2,160,128]{2,1,0:T(8,128)S(1)}, u32[]{:S(2)}, u32[]{:S(2)}) %collective-permute-start.5) | collective-permute-done | bytes 163872 | tf_op jit(solution)/shard_map/ppermute | solution.py:282
  26.2 1.8 %coils.6 = (f32[2,160,128]{2,1,0:T(8,128)S(1)}, f32[2,160,128]{2,1,0:T(8,128)S(1)}, f32[2,2,160,128]{3,2,1,0:T(8,128)S(1)}, f32[8,2,160,128]{3,2,1,0:T(8,128)S(1)}, f32[8,128]{1,0:T(8,128)S(1)}) custom-call(f32[2,8,2,160,128]{4,3,2,1,0:T(8,128)S(1)} %get-tuple-element.61.refs_0_, ...), custom_call_target="tpu_custom_call", output_to_operand_aliasing={{4}: (12, {}), {3}: (11, {})} | custom-call | flops 100000000 | bytes 100 | tf_op jit(solution)/shard_map/coils/pallas_call | solution.py:84
  28.1 0.1 collective-permute-start.11
  28.1 1.8 %coils.7 = (f32[2,160,128]{2,1,0:T(8,128)S(1)}, f32[2,160,128]{2,1,0:T(8,128)S(1)}, f32[2,2,160,128]{3,2,1,0:T(8,128)S(1)}, f32[8,2,160,128]{3,2,1,0:T(8,128)S(1)}, f32[8,128]{1,0:T(8,128)S(1)}) custom-call(f32[2,8,2,160,128]{4,3,2,1,0:T(8,128)S(1)} %get-tuple-element.61.refs_0_, ...), custom_call_target="tpu_custom_call", output_to_operand_aliasing={{4}: (11, {}), {3}: (10, {})} | custom-call | flops 100000000 | bytes 100 | tf_op jit(solution)/shard_map/coils/pallas_call | solution.py:84
  30.0 2.1 %collective-permute-start.10 = (f32[2,160,128]{2,1,0:T(8,128)S(1)}, f32[2,160,128]{2,1,0:T(8,128)S(1)}, u32[]{:S(2)}, u32[]{:S(2)}) collective-permute-start(f32[2,160,128]{2,1,0:T(8,128)S(1)} %get-tuple-element.95), channel_id=1, source_target_pairs={{0,2},{1,3},{2,0},{3,1},{4,6},{5,7},{6,4},{7,5},{8,10},{9,11},{10,... | collective-permute-start | bytes 491528 | tf_op jit(solution)/shard_map/ppermute | solution.py:282
  32.1 1.3 %collective-permute-start.12 = (f32[2,160,128]{2,1,0:T(8,128)S(1)}, f32[2,160,128]{2,1,0:T(8,128)S(1)}, u32[]{:S(2)}, u32[]{:S(2)}) collective-permute-start(f32[2,160,128]{2,1,0:T(8,128)S(1)} %get-tuple-element.104), channel_id=1, source_target_pairs={{0,8},{1,9},{2,10},{3,11},{4,12},{5,13},{6,14},{7,15},{8,0},{9,1},... | collective-permute-start | bytes 491528 | tf_op jit(solution)/shard_map/ppermute | solution.py:282
  33.3 1.3 %collective-permute-done.11.refs_1_ = f32[2,160,128]{2,1,0:T(8,128)S(1)} collective-permute-done((f32[2,160,128]{2,1,0:T(8,128)S(1)}, f32[2,160,128]{2,1,0:T(8,128)S(1)}, u32[]{:S(2)}, u32[]{:S(2)}) %collective-permute-start.11) | collective-permute-done | bytes 163872 | tf_op jit(solution)/shard_map/ppermute | solution.py:282
  34.7 2.8 %collective-permute-start.13 = (f32[2,160,128]{2,1,0:T(8,128)S(1)}, f32[2,160,128]{2,1,0:T(8,128)S(1)}, u32[]{:S(2)}, u32[]{:S(2)}) collective-permute-start(f32[2,160,128]{2,1,0:T(8,128)S(1)} %get-tuple-element.107), channel_id=1, source_target_pairs={{0,12},{1,13},{2,14},{3,15},{4,8},{5,9},{6,10},{7,11},{8,4},{9,5},... | collective-permute-start | bytes 491528 | tf_op jit(solution)/shard_map/ppermute | solution.py:282
  37.5 1.5 %collective-permute-start.15 = (f32[2,160,128]{2,1,0:T(8,128)S(1)}, f32[2,160,128]{2,1,0:T(8,128)S(1)}, u32[]{:S(2)}, u32[]{:S(2)}) collective-permute-start(f32[2,160,128]{2,1,0:T(8,128)S(1)} %get-tuple-element.111), channel_id=1, source_target_pairs={{0,2},{1,3},{2,0},{3,1},{4,6},{5,7},{6,4},{7,5},{8,10},{9,11},{10,... | collective-permute-start | bytes 491528 | tf_op jit(solution)/shard_map/ppermute | solution.py:282
  39.0 0.1 collective-permute-start.14
  39.1 0.1 collective-permute-start.7
  39.2 0.8 %temporal.1 = (f32[2,160,128]{2,1,0:T(8,128)}, f32[2,160,128]{2,1,0:T(8,128)S(1)}, f32[8,128]{1,0:T(8,128)S(1)}) custom-call(f32[2,160,128]{2,1,0:T(8,128)S(1)} %get-tuple-element.88.refs_0_, f32[4,160,128]{2,1,0:T(8,128)S(1)} %get-tuple-element.89.refs_1_, f32[4,160,128]{2,1,0:T(8,128)S(1)} %collective-permute-done.8.refs_2_, ...), custom_call_target="tpu_custom_call", output_to_operand_aliasing={{2}: (3, {})} | custom-call | flops 50000 | bytes 100 | tf_op jit(solution)/shard_map/temporal/pallas_call | solution.py:84
  39.9 1.1 %store.2 = (f32[2,1,1,16,160,128]{5,4,3,2,1,0:T(8,128)}, f32[8,128]{1,0:T(8,128)S(1)}) custom-call(f32[2,2,160,128]{3,2,1,0:T(8,128)S(1)} %get-tuple-element.84.refs_0_, f32[2,2,160,128]{3,2,1,0:T(8,128)S(1)} %get-tuple-element.85.refs_1_, f32[2,2,160,128]{3,2,1,0:T(8,128)S(1)} %get-tuple-element.86.refs_2_, ...), custom_call_target="tpu_custom_call", output_to_operand_aliasing={{1}: (4, {})} | custom-call | flops 1000 | bytes 100 | tf_op jit(solution)/shard_map/store/pallas_call | solution.py:329
  41.0 3.1 %collective-permute-done.12.refs_1_ = f32[2,160,128]{2,1,0:T(8,128)S(1)} collective-permute-done((f32[2,160,128]{2,1,0:T(8,128)S(1)}, f32[2,160,128]{2,1,0:T(8,128)S(1)}, u32[]{:S(2)}, u32[]{:S(2)}) %collective-permute-start.12) | collective-permute-done | bytes 163872 | tf_op jit(solution)/shard_map/ppermute | solution.py:282
  44.2 1.2 %collective-permute-done.14.refs_1_ = f32[2,160,128]{2,1,0:T(8,128)S(1)} collective-permute-done((f32[2,160,128]{2,1,0:T(8,128)S(1)}, f32[2,160,128]{2,1,0:T(8,128)S(1)}, u32[]{:S(2)}, u32[]{:S(2)}) %collective-permute-start.14) | collective-permute-done | bytes 163872 | tf_op jit(solution)/shard_map/ppermute | solution.py:282
  45.4 1.2 %store.3 = (f32[2,1,1,16,160,128]{5,4,3,2,1,0:T(8,128)}, f32[8,128]{1,0:T(8,128)S(1)}, f32[2,160,128]{2,1,0:T(8,128)}) custom-call(f32[8,2,160,128]{3,2,1,0:T(8,128)S(1)} %collective-permute-done.7.refs_0_, f32[2,1,1,16,160,128]{5,4,3,2,1,0:T(8,128)} %get-tuple-element.102.refs_1_, ...), custom_call_target="tpu_custom_call", output_to_operand_aliasing={{0}: (1, {}), {1}: (2, {})} | custom-call | flops 1000 | bytes 100 | tf_op jit(solution)/shard_map/store/pallas_call | solution.py:329
  (16 shorter events, 0.2 us)
Async XLA Ops:
  0.6 12.0 %collective-permute-start.2 = (f32[2,160,128]{2,1,0:T(8,128)}, f32[2,160,128]{2,1,0:T(8,128)S(1)}, u32[]{:S(2)}, u32[]{:S(2)}) collective-permute-start(f32[2,160,128]{2,1,0:T(8,128)} %bitcast.7), channel_id=1, source_target_pairs={{0,8},{1,9},{2,10},{3,11},{4,12},{5,13},{6,14},{7,15},{8,0},{9,1},... | collective-permute-start | bytes 491528 | tf_op jit(solution)/shard_map/ppermute | solution.py:282
  4.7 10.2 %collective-permute-start.1 = (f32[2,160,128]{2,1,0:T(8,128)}, f32[2,160,128]{2,1,0:T(8,128)S(1)}, u32[]{:S(2)}, u32[]{:S(2)}) collective-permute-start(f32[2,160,128]{2,1,0:T(8,128)} %bitcast.8), channel_id=1, source_target_pairs={{0,2},{1,3},{2,0},{3,1},{4,6},{5,7},{6,4},{7,5},{8,10},{9,11},{10,... | collective-permute-start | bytes 491528 | tf_op jit(solution)/shard_map/ppermute | solution.py:282
  10.7 5.0 %collective-permute-start = (f32[2,8,2,160,128]{4,3,2,1,0:T(8,128)S(1)}, f32[2,8,2,160,128]{4,3,2,1,0:T(8,128)S(1)}, u32[]{:S(2)}, u32[]{:S(2)}) collective-permute-start(f32[2,8,2,160,128]{4,3,2,1,0:T(8,128)S(1)} %get-tuple-element.62), channel_id=1, source_target_pairs={{0,1},{1,0},{2,3},{3,2},{4,5},{5,4},{6,7},{7,6},{8,9},{9,8},{10,11... | collective-permute-start | bytes 7864328 | tf_op jit(solution)/shard_map/ppermute | solution.py:282
  12.7 6.5 %collective-permute-start.4 = (f32[2,160,128]{2,1,0:T(8,128)S(1)}, f32[2,160,128]{2,1,0:T(8,128)S(1)}, u32[]{:S(2)}, u32[]{:S(2)}) collective-permute-start(f32[2,160,128]{2,1,0:T(8,128)S(1)} %get-tuple-element.75.refs_9_), channel_id=1, source_target_pairs={{0,4},{1,5},{2,6},{3,7},{4,0},{5,1},{6,2},{7,3},{8,12},{9,13},{10,... | collective-permute-start | bytes 491528 | tf_op jit(solution)/shard_map/ppermute | solution.py:282
  13.5 6.2 %collective-permute-start.6 = (f32[2,160,128]{2,1,0:T(8,128)S(1)}, f32[2,160,128]{2,1,0:T(8,128)S(1)}, u32[]{:S(2)}, u32[]{:S(2)}) collective-permute-start(f32[2,160,128]{2,1,0:T(8,128)S(1)} %get-tuple-element.75.refs_9_), channel_id=1, source_target_pairs={{0,2},{1,3},{2,0},{3,1},{4,6},{5,7},{6,4},{7,5},{8,10},{9,11},{10,... | collective-permute-start | bytes 491528 | tf_op jit(solution)/shard_map/ppermute | solution.py:282
  17.5 10.6 %collective-permute-start.3 = (f32[2,2,160,128]{3,2,1,0:T(8,128)S(1)}, f32[2,2,160,128]{3,2,1,0:T(8,128)S(1)}, u32[]{:S(2)}, u32[]{:S(2)}) collective-permute-start(f32[2,2,160,128]{3,2,1,0:T(8,128)S(1)} %get-tuple-element.73), channel_id=1, source_target_pairs={{0,4},{1,5},{2,6},{3,7},{4,0},{5,1},{6,2},{7,3},{8,12},{9,13},{10,... | collective-permute-start | bytes 983048 | tf_op jit(solution)/shard_map/ppermute | solution.py:282
  19.1 7.1 %collective-permute-start.5 = (f32[2,160,128]{2,1,0:T(8,128)S(1)}, f32[2,160,128]{2,1,0:T(8,128)S(1)}, u32[]{:S(2)}, u32[]{:S(2)}) collective-permute-start(f32[2,160,128]{2,1,0:T(8,128)S(1)} %get-tuple-element.76.refs_9_), channel_id=1, source_target_pairs={{0,2},{1,3},{2,0},{3,1},{4,6},{5,7},{6,4},{7,5},{8,10},{9,11},{10,... | collective-permute-start | bytes 491528 | tf_op jit(solution)/shard_map/ppermute | solution.py:282
  21.5 8.5 %collective-permute-start.9 = (f32[2,160,128]{2,1,0:T(8,128)S(1)}, f32[2,160,128]{2,1,0:T(8,128)S(1)}, u32[]{:S(2)}, u32[]{:S(2)}) collective-permute-start(f32[2,160,128]{2,1,0:T(8,128)S(1)} %get-tuple-element.92), channel_id=1, source_target_pairs={{0,2},{1,3},{2,0},{3,1},{4,6},{5,7},{6,4},{7,5},{8,10},{9,11},{10,... | collective-permute-start | bytes 491528 | tf_op jit(solution)/shard_map/ppermute | solution.py:282
  23.1 16.0 %collective-permute-start.8 = (f32[4,160,128]{2,1,0:T(8,128)S(1)}, f32[4,160,128]{2,1,0:T(8,128)S(1)}, u32[]{:S(2)}, u32[]{:S(2)}) collective-permute-start(f32[4,160,128]{2,1,0:T(8,128)S(1)} %get-tuple-element.89.refs_1_), channel_id=1, source_target_pairs={{0,16},{16,0},{1,17},{17,1},{2,18},{18,2},{3,19},{19,3},{4,20},{20... | collective-permute-start | bytes 983048 | tf_op jit(solution)/shard_map/ppermute | solution.py:277
  28.1 6.6 %collective-permute-start.11 = (f32[2,160,128]{2,1,0:T(8,128)S(1)}, f32[2,160,128]{2,1,0:T(8,128)S(1)}, u32[]{:S(2)}, u32[]{:S(2)}) collective-permute-start(f32[2,160,128]{2,1,0:T(8,128)S(1)} %get-tuple-element.97), channel_id=1, source_target_pairs={{0,2},{1,3},{2,0},{3,1},{4,6},{5,7},{6,4},{7,5},{8,10},{9,11},{10,... | collective-permute-start | bytes 491528 | tf_op jit(solution)/shard_map/ppermute | solution.py:282
  30.0 9.0 %collective-permute-start.10 = (f32[2,160,128]{2,1,0:T(8,128)S(1)}, f32[2,160,128]{2,1,0:T(8,128)S(1)}, u32[]{:S(2)}, u32[]{:S(2)}) collective-permute-start(f32[2,160,128]{2,1,0:T(8,128)S(1)} %get-tuple-element.95), channel_id=1, source_target_pairs={{0,2},{1,3},{2,0},{3,1},{4,6},{5,7},{6,4},{7,5},{8,10},{9,11},{10,... | collective-permute-start | bytes 491528 | tf_op jit(solution)/shard_map/ppermute | solution.py:282
  32.1 12.1 %collective-permute-start.12 = (f32[2,160,128]{2,1,0:T(8,128)S(1)}, f32[2,160,128]{2,1,0:T(8,128)S(1)}, u32[]{:S(2)}, u32[]{:S(2)}) collective-permute-start(f32[2,160,128]{2,1,0:T(8,128)S(1)} %get-tuple-element.104), channel_id=1, source_target_pairs={{0,8},{1,9},{2,10},{3,11},{4,12},{5,13},{6,14},{7,15},{8,0},{9,1},... | collective-permute-start | bytes 491528 | tf_op jit(solution)/shard_map/ppermute | solution.py:282
  34.7 9.5 %collective-permute-start.13 = (f32[2,160,128]{2,1,0:T(8,128)S(1)}, f32[2,160,128]{2,1,0:T(8,128)S(1)}, u32[]{:S(2)}, u32[]{:S(2)}) collective-permute-start(f32[2,160,128]{2,1,0:T(8,128)S(1)} %get-tuple-element.107), channel_id=1, source_target_pairs={{0,12},{1,13},{2,14},{3,15},{4,8},{5,9},{6,10},{7,11},{8,4},{9,5},... | collective-permute-start | bytes 491528 | tf_op jit(solution)/shard_map/ppermute | solution.py:282
  37.5 6.8 %collective-permute-start.15 = (f32[2,160,128]{2,1,0:T(8,128)S(1)}, f32[2,160,128]{2,1,0:T(8,128)S(1)}, u32[]{:S(2)}, u32[]{:S(2)}) collective-permute-start(f32[2,160,128]{2,1,0:T(8,128)S(1)} %get-tuple-element.111), channel_id=1, source_target_pairs={{0,2},{1,3},{2,0},{3,1},{4,6},{5,7},{6,4},{7,5},{8,10},{9,11},{10,... | collective-permute-start | bytes 491528 | tf_op jit(solution)/shard_map/ppermute | solution.py:282
  39.0 6.4 %collective-permute-start.14 = (f32[2,160,128]{2,1,0:T(8,128)S(1)}, f32[2,160,128]{2,1,0:T(8,128)S(1)}, u32[]{:S(2)}, u32[]{:S(2)}) collective-permute-start(f32[2,160,128]{2,1,0:T(8,128)S(1)} %get-tuple-element.110), channel_id=1, source_target_pairs={{0,4},{1,5},{2,6},{3,7},{4,0},{5,1},{6,2},{7,3},{8,12},{9,13},{10,... | collective-permute-start | bytes 491528 | tf_op jit(solution)/shard_map/ppermute | solution.py:282
  39.1 6.3 %collective-permute-start.7 = (f32[8,2,160,128]{3,2,1,0:T(8,128)S(1)}, f32[8,2,160,128]{3,2,1,0:T(8,128)S(1)}, u32[]{:S(2)}, u32[]{:S(2)}) collective-permute-start(f32[8,2,160,128]{3,2,1,0:T(8,128)S(1)} %get-tuple-element.83), channel_id=1, source_target_pairs={{0,1},{1,0},{2,3},{3,2},{4,5},{5,4},{6,7},{7,6},{8,9},{9,8},{10,11... | collective-permute-start | bytes 3932168 | tf_op jit(solution)/shard_map/ppermute | solution.py:282
